TPU v7x, 128 devices: a whole 4x4x4 slice. The times are simulated.
128 devices in a mesh: gx: 8 (over z, core), gy: 16 (over x, y).
Axes of the slice: x: 4, y: 4, z: 4, core: 2. Of those that a mesh axis runs over, the one named last changes fastest.
Arguments:
- right_side: float32 [64, 64, 2048], P(None, 'gx', 'gy'), may hold values from -4 to 10
- terrain: int32 [64, 64, 2048], P(None, 'gx', 'gy'), may hold values from 0 to 1, as said below
Outputs:
- pressure: float32 [64, 64, 2048], P(None, 'gx', 'gy')
Inputs may be any that keep to these rules, and one draw needn't show every extreme that they name: 1 marks a terrain cell; in every vertical column the terrain cells are the lowest ones, from none up to 32 of them.
All inputs are finite; a program needn't handle non-finite values.
Results may differ from a plain program's by a relative error of at most 0.0001.
Values sent between devices are 32-bit elements; how exact they have to be, the bound alone decides.
No kernel may reach another device: no remote copies, remote signals or barrier semaphores. Data moves between devices by JAX's collectives and lax.ppermute only.
A program may use at most 128 MiB of HBM per device.

v0:
```python
import jax
import jax.numpy as jnp
from jax import lax
from jax.sharding import PartitionSpec as P

SWEEPS = 4
LEVELS = 3
COARSE_SWEEPS = 8
CYCLES = 2


RELAX_WEIGHT = 0.8
TERRAIN_PENALTY = 0.05


def extended(block, sides, width):
    for axis, dim in sides:
        count = lax.axis_size(axis)
        forward = [(i, i + 1) for i in range(count - 1)]
        backward = [(target, source) for source, target in forward]
        low = lax.ppermute(
            lax.slice_in_dim(block, block.shape[dim] - width, None, axis=dim), axis, forward
        )
        high = lax.ppermute(lax.slice_in_dim(block, 0, width, axis=dim), axis, backward)
        block = jnp.concatenate([low, block, high], axis=dim)
    return block


def neighbors(padded):
    centre = padded[:, 1:-1, 1:-1]
    vertical = jnp.pad(centre, ((1, 1), (0, 0), (0, 0)))
    neighbor_sum = vertical[2:] + vertical[:-2]
    neighbor_sum = neighbor_sum + padded[:, 2:, 1:-1] + padded[:, :-2, 1:-1]
    neighbor_sum = neighbor_sum + padded[:, 1:-1, 2:] + padded[:, 1:-1, :-2]
    return (neighbor_sum, centre)


def relax_once(padded, source, shift_now):
    neighbor_sum, centre = neighbors(padded)
    diagonal = 6.0 + shift_now
    return centre + RELAX_WEIGHT * (source - diagonal * centre + neighbor_sum) / diagonal


def defect(padded, source, shift_now):
    neighbor_sum, centre = neighbors(padded)
    return source - (6.0 + shift_now) * centre + neighbor_sum


def first_sweep(source, shift_now):
    return RELAX_WEIGHT * source / (6.0 + shift_now)


def restrict(values):
    layers_here, rows_here, cols_here = values.shape
    blocks = values.reshape(layers_here // 2, 2, rows_here // 2, 2, cols_here // 2, 2)
    return 0.5 * blocks.sum(axis=(1, 3, 5))


def prolong(values):
    layers_here, rows_here, cols_here = values.shape
    spread = jnp.broadcast_to(
        values[:, None, :, None, :, None], (layers_here, 2, rows_here, 2, cols_here, 2)
    )
    return spread.reshape(2 * layers_here, 2 * rows_here, 2 * cols_here)


def fine_halo(values):
    return extended(values, (("gx", 1), ("gy", 2)), 1)


def level_halo(values):
    return extended(values, (("gx", 1), ("gy", 2)), 1)


def coarse_halo(values):
    return extended(values, (("gx", 1), ("gy", 2)), 1)


def per_device(right_side, terrain):
    shift_fine = TERRAIN_PENALTY * terrain.astype(jnp.float32)
    tile_levels = LEVELS
    pressure = jnp.zeros_like(right_side)
    for cycle_index in range(CYCLES):
        source, shift_now = (right_side, shift_fine)
        stored = []
        for level_index in range(tile_levels):
            if level_index == 0:
                if cycle_index == 0:
                    iterate = first_sweep(source, shift_now)
                    repeats = SWEEPS - 1
                else:
                    iterate = pressure
                    repeats = SWEEPS
                for repeat in range(repeats):
                    iterate = relax_once(fine_halo(iterate), source, shift_now)
                residual = defect(fine_halo(iterate), source, shift_now)
            else:
                iterate = first_sweep(source, shift_now)
                for repeat in range(SWEEPS - 1):
                    iterate = relax_once(level_halo(iterate), source, shift_now)
                residual = defect(level_halo(iterate), source, shift_now)
            stored.append((iterate, source, shift_now))
            source = restrict(residual)
            shift_now = restrict(shift_now)
        coarse_source, coarse_shift = (source, shift_now)
        correction = first_sweep(coarse_source, coarse_shift)
        correction = lax.fori_loop(
            0,
            COARSE_SWEEPS - 1,
            lambda counter, current: relax_once(coarse_halo(current), coarse_source, coarse_shift),
            correction,
        )
        for level_index in reversed(range(tile_levels)):
            iterate, source, shift_now = stored[level_index]
            iterate = iterate + prolong(correction)
            if level_index == 0:
                for repeat in range(SWEEPS):
                    iterate = relax_once(fine_halo(iterate), source, shift_now)
            else:
                for repeat in range(SWEEPS):
                    iterate = relax_once(level_halo(iterate), source, shift_now)
            correction = iterate
        pressure = correction
    return pressure


def solution(mesh):
    in_specs = (P(None, "gx", "gy"), P(None, "gx", "gy"))
    out_specs = P(None, "gx", "gy")
    return jax.shard_map(
        per_device, mesh=mesh, in_specs=in_specs, out_specs=out_specs, check_vma=False
    )
```

profile of v0, /device:TPU:6, one launch (start us, length us, event | category | flops | bytes accessed | tf_op | source)
XLA Modules:
  0.0 1360.5 jit_solution(10335685964789540396)
XLA Ops:
  14.6 10.1 collective-permute-done.11
  42.0 8.9 collective-permute-done.15
  69.1 7.8 collective-permute-done.19
  96.2 18.1 %reshape.143 = f32[32,2,4,2,64,2]{5,4,3,2,1,0:T(8,128)} reshape(f32[64,8,128]{2,1,0:T(8,128)S(1)} %get-tuple-element.219) | data formatting | bytes 524288 | tf_op jit(solution)/shard_map/reshape | solution.py:55
  114.3 7.0 reduce_sum.115
  121.8 18.1 %reshape.142 = f32[32,2,4,2,64,2]{5,4,3,2,1,0:T(8,128)} reshape(f32[64,8,128]{2,1,0:T(8,128)S(1)} %fusion.108) | data formatting | bytes 524288 | tf_op jit(solution)/shard_map/reshape | solution.py:55
  139.9 7.0 reduce_sum.114
  292.0 117.5 %while.24 = (s32[]{:T(128)}, f32[8,1,16]{2,1,0:T(1,128)S(1)}, f32[8,1,16]{2,1,0:T(1,128)S(1)}, f32[8,1,16]{2,1,0:T(1,128)S(1)}, s32[]{:T(128)}) while((s32[]{:T(128)}, f32[8,1,16]{2,1,0:T(1,128)S(1)}, f32[8,1,16]{2,1,0:T(1,128)S(1)}, f32[8,1,16]{2,1,0:T(1,128)S(1)}, s32[]{:T(128)}) %tuple.171), condition=%wide.region_9.10_spmd, body=%wide.region_8.9_spmd.sunk | while | flops 3074 | bytes 12829 | solution.py:107
  559.2 12.6 reshape.146
  587.6 7.8 collective-permute-done.91
  613.6 7.8 collective-permute-done.95
  639.7 7.7 collective-permute-done.99
  665.7 7.7 collective-permute-done.103
  691.7 7.6 collective-permute-done.107
  717.8 7.6 collective-permute-done.111
  743.8 7.5 collective-permute-done.115
  769.8 7.5 collective-permute-done.119
  805.4 18.1 %reshape.147 = f32[32,2,4,2,64,2]{5,4,3,2,1,0:T(8,128)} reshape(f32[64,8,128]{2,1,0:T(8,128)S(1)} %fusion.39) | data formatting | bytes 524288 | tf_op jit(solution)/shard_map/reshape | solution.py:55
  975.9 117.5 %while.25 = (s32[]{:T(128)}, f32[8,1,16]{2,1,0:T(1,128)S(1)}, f32[8,1,16]{2,1,0:T(1,128)S(1)}, f32[8,1,16]{2,1,0:T(1,128)S(1)}, s32[]{:T(128)}) while((s32[]{:T(128)}, f32[8,1,16]{2,1,0:T(1,128)S(1)}, f32[8,1,16]{2,1,0:T(1,128)S(1)}, f32[8,1,16]{2,1,0:T(1,128)S(1)}, s32[]{:T(128)}) %tuple.170), condition=%wide.region_15.16_spmd, body=%wide.region_14.15_spmd.sunk | while | flops 3074 | bytes 12829 | solution.py:107
  1243.1 12.6 reshape.150
  1271.6 7.8 collective-permute-done.191
  1297.6 7.8 collective-permute-done.195
  1323.7 7.7 collective-permute-done.199
  1349.7 7.7 collective-permute-done.203
  (787 shorter events, 1143.3 us)
Async XLA Ops:
  6.6 18.1 %collective-permute-start.11 = (f32[64,10,1]{2,1,0:T(8,128)S(1)}, f32[64,10,1]{2,1,0:T(8,128)S(1)}, u32[]{:S(2)}, u32[]{:S(2)}) collective-permute-start(f32[64,10,1]{2,1,0:T(8,128)S(1)} %get-tuple-element.192), channel_id=1, source_target_pairs={{0,1},{1,2},{2,3},{3,4},{4,5},{5,6},{6,7},{7,8},{8,9},{9,10},{10,1... | collective-permute-start | bytes 7688 | tf_op jit(solution)/shard_map/ppermute | solution.py:21
  10.1 16.4 %collective-permute-start.10 = (f32[64,10,1]{2,1,0:T(8,128)S(1)}, f32[64,10,1]{2,1,0:T(8,128)S(1)}, u32[]{:S(2)}, u32[]{:S(2)}) collective-permute-start(f32[64,10,1]{2,1,0:T(8,128)S(1)} %get-tuple-element.191), channel_id=1, source_target_pairs={{1,0},{2,1},{3,2},{4,3},{5,4},{6,5},{7,6},{8,7},{9,8},{10,9},{11,1... | collective-permute-start | bytes 7688 | tf_op jit(solution)/shard_map/ppermute | solution.py:24
  33.6 17.4 %collective-permute-start.15 = (f32[64,10,1]{2,1,0:T(8,128)S(1)}, f32[64,10,1]{2,1,0:T(8,128)S(1)}, u32[]{:S(2)}, u32[]{:S(2)}) collective-permute-start(f32[64,10,1]{2,1,0:T(8,128)S(1)} %get-tuple-element.190), channel_id=1, source_target_pairs={{0,1},{1,2},{2,3},{3,4},{4,5},{5,6},{6,7},{7,8},{8,9},{9,10},{10,1... | collective-permute-start | bytes 7688 | tf_op jit(solution)/shard_map/ppermute | solution.py:21
  37.0 15.7 %collective-permute-start.14 = (f32[64,10,1]{2,1,0:T(8,128)S(1)}, f32[64,10,1]{2,1,0:T(8,128)S(1)}, u32[]{:S(2)}, u32[]{:S(2)}) collective-permute-start(f32[64,10,1]{2,1,0:T(8,128)S(1)} %get-tuple-element.189), channel_id=1, source_target_pairs={{1,0},{2,1},{3,2},{4,3},{5,4},{6,5},{7,6},{8,7},{9,8},{10,9},{11,1... | collective-permute-start | bytes 7688 | tf_op jit(solution)/shard_map/ppermute | solution.py:24
  60.9 16.0 %collective-permute-start.19 = (f32[64,10,1]{2,1,0:T(8,128)S(1)}, f32[64,10,1]{2,1,0:T(8,128)S(1)}, u32[]{:S(2)}, u32[]{:S(2)}) collective-permute-start(f32[64,10,1]{2,1,0:T(8,128)S(1)} %get-tuple-element.188), channel_id=1, source_target_pairs={{0,1},{1,2},{2,3},{3,4},{4,5},{5,6},{6,7},{7,8},{8,9},{9,10},{10,1... | collective-permute-start | bytes 7688 | tf_op jit(solution)/shard_map/ppermute | solution.py:21
  88.0 33.3 %collective-permute-start.23 = (f32[64,10,1]{2,1,0:T(8,128)S(1)}, f32[64,10,1]{2,1,0:T(8,128)S(1)}, u32[]{:S(2)}, u32[]{:S(2)}) collective-permute-start(f32[64,10,1]{2,1,0:T(8,128)S(1)} %get-tuple-element.186), channel_id=1, source_target_pairs={{0,1},{1,2},{2,3},{3,4},{4,5},{5,6},{6,7},{7,8},{8,9},{9,10},{10,1... | collective-permute-start | bytes 7688 | tf_op jit(solution)/shard_map/ppermute | solution.py:21
  90.0 31.4 %collective-permute-start.22 = (f32[64,10,1]{2,1,0:T(8,128)S(1)}, f32[64,10,1]{2,1,0:T(8,128)S(1)}, u32[]{:S(2)}, u32[]{:S(2)}) collective-permute-start(f32[64,10,1]{2,1,0:T(8,128)S(1)} %get-tuple-element.185), channel_id=1, source_target_pairs={{1,0},{2,1},{3,2},{4,3},{5,4},{6,5},{7,6},{8,7},{9,8},{10,9},{11,1... | collective-permute-start | bytes 7688 | tf_op jit(solution)/shard_map/ppermute | solution.py:24
  579.5 16.0 %collective-permute-start.91 = (f32[64,10,1]{2,1,0:T(8,128)S(1)}, f32[64,10,1]{2,1,0:T(8,128)S(1)}, u32[]{:S(2)}, u32[]{:S(2)}) collective-permute-start(f32[64,10,1]{2,1,0:T(8,128)S(1)} %get-tuple-element.184), channel_id=1, source_target_pairs={{0,1},{1,2},{2,3},{3,4},{4,5},{5,6},{6,7},{7,8},{8,9},{9,10},{10,1... | collective-permute-start | bytes 7688 | tf_op jit(solution)/shard_map/ppermute | solution.py:21
  581.4 15.8 %collective-permute-start.90 = (f32[64,10,1]{2,1,0:T(8,128)S(1)}, f32[64,10,1]{2,1,0:T(8,128)S(1)}, u32[]{:S(2)}, u32[]{:S(2)}) collective-permute-start(f32[64,10,1]{2,1,0:T(8,128)S(1)} %get-tuple-element.183), channel_id=1, source_target_pairs={{1,0},{2,1},{3,2},{4,3},{5,4},{6,5},{7,6},{8,7},{9,8},{10,9},{11,1... | collective-permute-start | bytes 7688 | tf_op jit(solution)/shard_map/ppermute | solution.py:24
  605.5 15.9 %collective-permute-start.95 = (f32[64,10,1]{2,1,0:T(8,128)S(1)}, f32[64,10,1]{2,1,0:T(8,128)S(1)}, u32[]{:S(2)}, u32[]{:S(2)}) collective-permute-start(f32[64,10,1]{2,1,0:T(8,128)S(1)} %get-tuple-element.182), channel_id=1, source_target_pairs={{0,1},{1,2},{2,3},{3,4},{4,5},{5,6},{6,7},{7,8},{8,9},{9,10},{10,1... | collective-permute-start | bytes 7688 | tf_op jit(solution)/shard_map/ppermute | solution.py:21
  607.4 15.7 %collective-permute-start.94 = (f32[64,10,1]{2,1,0:T(8,128)S(1)}, f32[64,10,1]{2,1,0:T(8,128)S(1)}, u32[]{:S(2)}, u32[]{:S(2)}) collective-permute-start(f32[64,10,1]{2,1,0:T(8,128)S(1)} %get-tuple-element.181), channel_id=1, source_target_pairs={{1,0},{2,1},{3,2},{4,3},{5,4},{6,5},{7,6},{8,7},{9,8},{10,9},{11,1... | collective-permute-start | bytes 7688 | tf_op jit(solution)/shard_map/ppermute | solution.py:24
  631.5 15.9 %collective-permute-start.99 = (f32[64,10,1]{2,1,0:T(8,128)S(1)}, f32[64,10,1]{2,1,0:T(8,128)S(1)}, u32[]{:S(2)}, u32[]{:S(2)}) collective-permute-start(f32[64,10,1]{2,1,0:T(8,128)S(1)} %get-tuple-element.180), channel_id=1, source_target_pairs={{0,1},{1,2},{2,3},{3,4},{4,5},{5,6},{6,7},{7,8},{8,9},{9,10},{10,1... | collective-permute-start | bytes 7688 | tf_op jit(solution)/shard_map/ppermute | solution.py:21
  633.4 15.7 %collective-permute-start.98 = (f32[64,10,1]{2,1,0:T(8,128)S(1)}, f32[64,10,1]{2,1,0:T(8,128)S(1)}, u32[]{:S(2)}, u32[]{:S(2)}) collective-permute-start(f32[64,10,1]{2,1,0:T(8,128)S(1)} %get-tuple-element.179), channel_id=1, source_target_pairs={{1,0},{2,1},{3,2},{4,3},{5,4},{6,5},{7,6},{8,7},{9,8},{10,9},{11,1... | collective-permute-start | bytes 7688 | tf_op jit(solution)/shard_map/ppermute | solution.py:24
  657.6 15.8 %collective-permute-start.103 = (f32[64,10,1]{2,1,0:T(8,128)S(1)}, f32[64,10,1]{2,1,0:T(8,128)S(1)}, u32[]{:S(2)}, u32[]{:S(2)}) collective-permute-start(f32[64,10,1]{2,1,0:T(8,128)S(1)} %get-tuple-element.178), channel_id=1, source_target_pairs={{0,1},{1,2},{2,3},{3,4},{4,5},{5,6},{6,7},{7,8},{8,9},{9,10},{10,1... | collective-permute-start | bytes 7688 | tf_op jit(solution)/shard_map/ppermute | solution.py:21
  683.6 15.8 %collective-permute-start.107 = (f32[64,10,1]{2,1,0:T(8,128)S(1)}, f32[64,10,1]{2,1,0:T(8,128)S(1)}, u32[]{:S(2)}, u32[]{:S(2)}) collective-permute-start(f32[64,10,1]{2,1,0:T(8,128)S(1)} %get-tuple-element.176), channel_id=1, source_target_pairs={{0,1},{1,2},{2,3},{3,4},{4,5},{5,6},{6,7},{7,8},{8,9},{9,10},{10,1... | collective-permute-start | bytes 7688 | tf_op jit(solution)/shard_map/ppermute | solution.py:21
  709.6 15.7 %collective-permute-start.111 = (f32[64,10,1]{2,1,0:T(8,128)S(1)}, f32[64,10,1]{2,1,0:T(8,128)S(1)}, u32[]{:S(2)}, u32[]{:S(2)}) collective-permute-start(f32[64,10,1]{2,1,0:T(8,128)S(1)} %get-tuple-element.174), channel_id=1, source_target_pairs={{0,1},{1,2},{2,3},{3,4},{4,5},{5,6},{6,7},{7,8},{8,9},{9,10},{10,1... | collective-permute-start | bytes 7688 | tf_op jit(solution)/shard_map/ppermute | solution.py:21
  735.7 15.7 %collective-permute-start.115 = (f32[64,10,1]{2,1,0:T(8,128)S(1)}, f32[64,10,1]{2,1,0:T(8,128)S(1)}, u32[]{:S(2)}, u32[]{:S(2)}) collective-permute-start(f32[64,10,1]{2,1,0:T(8,128)S(1)} %get-tuple-element.172), channel_id=1, source_target_pairs={{0,1},{1,2},{2,3},{3,4},{4,5},{5,6},{6,7},{7,8},{8,9},{9,10},{10,1... | collective-permute-start | bytes 7688 | tf_op jit(solution)/shard_map/ppermute | solution.py:21
  1263.4 16.0 %collective-permute-start.191 = (f32[64,10,1]{2,1,0:T(8,128)S(1)}, f32[64,10,1]{2,1,0:T(8,128)S(1)}, u32[]{:S(2)}, u32[]{:S(2)}) collective-permute-start(f32[64,10,1]{2,1,0:T(8,128)S(1)} %get-tuple-element.166), channel_id=1, source_target_pairs={{0,1},{1,2},{2,3},{3,4},{4,5},{5,6},{6,7},{7,8},{8,9},{9,10},{10,1... | collective-permute-start | bytes 7688 | tf_op jit(solution)/shard_map/ppermute | solution.py:21
  1265.4 15.8 %collective-permute-start.190 = (f32[64,10,1]{2,1,0:T(8,128)S(1)}, f32[64,10,1]{2,1,0:T(8,128)S(1)}, u32[]{:S(2)}, u32[]{:S(2)}) collective-permute-start(f32[64,10,1]{2,1,0:T(8,128)S(1)} %get-tuple-element.165), channel_id=1, source_target_pairs={{1,0},{2,1},{3,2},{4,3},{5,4},{6,5},{7,6},{8,7},{9,8},{10,9},{11,1... | collective-permute-start | bytes 7688 | tf_op jit(solution)/shard_map/ppermute | solution.py:24
  1289.5 15.9 %collective-permute-start.195 = (f32[64,10,1]{2,1,0:T(8,128)S(1)}, f32[64,10,1]{2,1,0:T(8,128)S(1)}, u32[]{:S(2)}, u32[]{:S(2)}) collective-permute-start(f32[64,10,1]{2,1,0:T(8,128)S(1)} %get-tuple-element.164), channel_id=1, source_target_pairs={{0,1},{1,2},{2,3},{3,4},{4,5},{5,6},{6,7},{7,8},{8,9},{9,10},{10,1... | collective-permute-start | bytes 7688 | tf_op jit(solution)/shard_map/ppermute | solution.py:21
  1291.4 15.7 %collective-permute-start.194 = (f32[64,10,1]{2,1,0:T(8,128)S(1)}, f32[64,10,1]{2,1,0:T(8,128)S(1)}, u32[]{:S(2)}, u32[]{:S(2)}) collective-permute-start(f32[64,10,1]{2,1,0:T(8,128)S(1)} %get-tuple-element.163), channel_id=1, source_target_pairs={{1,0},{2,1},{3,2},{4,3},{5,4},{6,5},{7,6},{8,7},{9,8},{10,9},{11,1... | collective-permute-start | bytes 7688 | tf_op jit(solution)/shard_map/ppermute | solution.py:24
  1315.5 15.9 %collective-permute-start.199 = (f32[64,10,1]{2,1,0:T(8,128)S(1)}, f32[64,10,1]{2,1,0:T(8,128)S(1)}, u32[]{:S(2)}, u32[]{:S(2)}) collective-permute-start(f32[64,10,1]{2,1,0:T(8,128)S(1)} %get-tuple-element.162), channel_id=1, source_target_pairs={{0,1},{1,2},{2,3},{3,4},{4,5},{5,6},{6,7},{7,8},{8,9},{9,10},{10,1... | collective-permute-start | bytes 7688 | tf_op jit(solution)/shard_map/ppermute | solution.py:21
  1317.5 15.7 %collective-permute-start.198 = (f32[64,10,1]{2,1,0:T(8,128)S(1)}, f32[64,10,1]{2,1,0:T(8,128)S(1)}, u32[]{:S(2)}, u32[]{:S(2)}) collective-permute-start(f32[64,10,1]{2,1,0:T(8,128)S(1)} %get-tuple-element.161), channel_id=1, source_target_pairs={{1,0},{2,1},{3,2},{4,3},{5,4},{6,5},{7,6},{8,7},{9,8},{10,9},{11,1... | collective-permute-start | bytes 7688 | tf_op jit(solution)/shard_map/ppermute | solution.py:24
  1341.6 15.8 %collective-permute-start.203 = (f32[64,10,1]{2,1,0:T(8,128)S(1)}, f32[64,10,1]{2,1,0:T(8,128)S(1)}, u32[]{:S(2)}, u32[]{:S(2)}) collective-permute-start(f32[64,10,1]{2,1,0:T(8,128)S(1)} %get-tuple-element.160), channel_id=1, source_target_pairs={{0,1},{1,2},{2,3},{3,4},{4,5},{5,6},{6,7},{7,8},{8,9},{9,10},{10,1... | collective-permute-start | bytes 7688 | tf_op jit(solution)/shard_map/ppermute | solution.py:21
  (230 other events, 1735.1 us)
where the time goes:
time: 1380 us; the launch traced here: 1360 us
  starting transfers between devices  910 us (66%)
  waiting for transfers between devices  287 us (21%)
  local copies, waits for them, and re-layouts  112 us (8%)
  other arithmetic  46.2 us (3%)
    ppermute x126, starting transfers between devices, extended(): lax.ppermute(lax.slice_in_dim(block, 0, width, axis=dim), axis, backward)  464 us
    ppermute x126, starting transfers between devices, extended(): lax.ppermute(lax.slice_in_dim(block, block.shape[dim] - width, None, axis...  446 us
    ppermute x126, waiting for transfers between devices, extended(): lax.ppermute(lax.slice_in_dim(block, block.shape[dim] - width, None, axis...  192 us
    ppermute x126, waiting for transfers between devices, extended(): lax.ppermute(lax.slice_in_dim(block, 0, width, axis=dim), axis, backward)  95.5 us
    reshape x5, local copies, waits for them, and re-layouts, restrict(): values.reshape(layers_here // 2, 2, rows_here // 2, 2, cols_here // 2, 2)  58.6 us
    reshape x4, local copies, waits for them, and re-layouts, prolong(): return spread.reshape(2 * layers_here, 2 * rows_here, 2 * cols_here)  28.5 us
  transfers between devices with their start and end apart: 252, of which 156 were waited for; matrix products, arithmetic and copies ran while one was open for 2% of the time, Pallas kernels for 0%

commit v1 on v0

v1 whole, which is shorter than its diff:
```python
import jax
import jax.numpy as jnp
from jax import lax
from jax.experimental import pallas as pl
from jax.experimental.pallas import tpu as pltpu
from jax.sharding import PartitionSpec as P

SWEEPS = 4
COARSE_SWEEPS = 8
RELAX_WEIGHT = 0.8
TERRAIN_PENALTY = 0.05

F32 = jnp.float32
LANES = 128
LAYERS = 64
TILE_ROWS = 8
PAD = 8
WINDOW = 16
VMEM_LIMIT = 56 * 1024 * 1024


D_AIR = 6.0
D_TERRAIN = 6.0 + TERRAIN_PENALTY


def lanes_iota(shape):
    return lax.broadcasted_iota(jnp.int32, shape, len(shape) - 1)


def edge_mask(level, has_left, has_right):
    lane = lanes_iota((1, LANES))
    zero = jnp.zeros((1, LANES), F32)
    left = zero + has_left.astype(F32)
    right = zero + has_right.astype(F32)
    if level == 0:
        return jnp.where(lane < 64, right, left)
    if level == 1:
        return jnp.where(lane < 64, 1.0, jnp.where(lane < 96, right, left))
    if level == 2:
        return jnp.where(
            lane < 32, 1.0, jnp.where(lane < 64, right, jnp.where(lane < 96, 0.0, left))
        )
    return jnp.where(
        lane < 16, 1.0, jnp.where(lane < 32, right, jnp.where(lane < 112, 0.0, left))
    )


def dot(values, matrix):
    return lax.dot_general(
        values, matrix, (((1,), (0,)), ((), ())),
        precision=lax.Precision.HIGHEST, preferred_element_type=F32,
    )


def matrix_of(rule):
    row = lax.broadcasted_iota(jnp.int32, (LANES, LANES), 0)
    col = lax.broadcasted_iota(jnp.int32, (LANES, LANES), 1)
    return rule(row, col)


def half(flag):
    return jnp.where(flag, 0.5, 0.0).astype(F32)


def one(flag):
    return jnp.where(flag, 1.0, 0.0).astype(F32)


def side_sum(parts):
    ahead = [pltpu.roll(x, LANES - 1, axis=x.ndim - 1) for x in parts]
    behind = [pltpu.roll(x, 1, axis=x.ndim - 1) for x in parts]
    if len(parts) == 1:
        return [ahead[0] + behind[0]]
    lane = lanes_iota(parts[0].shape)
    first, last = lane == 0, lane == LANES - 1
    return [
        jnp.where(last, ahead[1 - h], ahead[h]) + jnp.where(first, behind[1 - h], behind[h])
        for h in range(2)
    ]


def at(ref, h, halves, row, layers):
    if halves == 2:
        return ref[h, row, layers, :]
    return ref[row, layers, :]


def put(ref, h, halves, row, layers, value):
    if halves == 2:
        ref[h, row, layers, :] = value
    else:
        ref[row, layers, :] = value


def stencil_pass(src, halves, first_row, rows, base, depth, shift, emit, group, unrolled):
    def layers(offset):
        return pl.ds(shift + (base + offset), depth)

    aligned = pl.ds(PAD + base, depth)

    def rows_at(row):
        return [at(src, h, halves, row, aligned) for h in range(halves)]

    def step(row, before, centre):
        after = rows_at(row + 2)
        sides = side_sum(centre)
        for h in range(halves):
            total = before[h] + after[h]
            total = total + at(src, h, halves, row + 1, layers(-1))
            total = total + at(src, h, halves, row + 1, layers(1))
            emit(row, h, centre[h], total + sides[h])
        return centre, after

    before, centre = rows_at(first_row), rows_at(first_row + 1)
    if unrolled:
        for i in range(rows):
            before, centre = step(first_row + i, before, centre)
        return

    def body(i, carry):
        before, centre = carry
        for k in range(group):
            before, centre = step(first_row + i * group + k, before, centre)
        return before, centre

    lax.fori_loop(0, rows // group, body, (before, centre))


class Fine:
    def __init__(self, source, height, edge, shift):
        self.source, self.height, self.shift = source, height, shift
        self.edge = [jnp.ones((1, LANES), F32), edge]
        self.layer = lax.broadcasted_iota(jnp.int32, (32, LANES), 0).astype(F32)

    def terrain(self, row, h):
        height = self.height[h, row]
        return self.layer < jnp.concatenate([height] * 4, axis=0)

    def weight(self, row, h, chunk):
        air = (RELAX_WEIGHT / D_AIR) * self.edge[h]
        if chunk == 1:
            return air
        ground = (RELAX_WEIGHT / D_TERRAIN) * self.edge[h]
        return jnp.where(self.terrain(row, h), ground, air)

    def first(self, dst, rows):
        def body(row, carry):
            for h in range(2):
                for chunk in range(2):
                    value = self.weight(row, h, chunk) * self.source[h, row, pl.ds(32 * chunk, 32), :]
                    dst[h, row + 1, pl.ds(PAD + 32 * chunk, 32), :] = value
            return carry

        lax.fori_loop(0, rows, body, 0)

    def relax(self, src, dst, first_row, rows):
        for chunk in range(2):
            def emit(row, h, centre, total, chunk=chunk):
                total = total + self.source[h, row, pl.ds(32 * chunk, 32), :]
                value = (1.0 - RELAX_WEIGHT) * centre + self.weight(row, h, chunk) * total
                dst[h, row + 1, pl.ds(PAD + 32 * chunk, 32), :] = value

            stencil_pass(src, 2, first_row, rows, 32 * chunk, 32, self.shift, emit, 2, False)

    def restricted_defect(self, src, spare, rows, out):
        for chunk in range(2):
            held = {}

            def emit(row, h, centre, total, chunk=chunk):
                total = total + self.source[h, row, pl.ds(32 * chunk, 32), :]
                diagonal = D_AIR
                if chunk == 0:
                    diagonal = jnp.where(self.terrain(row, h), D_TERRAIN, D_AIR)
                value = total - diagonal * centre
                if h not in held:
                    held[h] = value
                else:
                    target = lax.div(row, 2) + 1
                    spare[h, target, pl.ds(PAD + 32 * chunk, 32), :] = held.pop(h) + value

            stencil_pass(src, 2, 0, rows, 32 * chunk, 32, self.shift, emit, 2, False)
        pair_layers_and_lanes(spare, rows // 2, out)

    def coarse_shift(self, rows, spare, out):
        base = 2.0 * lax.broadcasted_iota(jnp.int32, (32, LANES), 0).astype(F32)

        def body(row, carry):
            for h in range(2):
                count = jnp.zeros((32, LANES), F32)
                for k in range(2):
                    height = jnp.concatenate([self.height[h, 2 * row + k]] * 4, axis=0)
                    count = count + jnp.clip(height - base, 0.0, 2.0)
                spare[h, row + 1, pl.ds(PAD, 32), :] = TERRAIN_PENALTY * count
            return carry

        lax.fori_loop(0, rows // 2, body, 0)
        lanes_to_level_1(
            lambda h, row: spare[h, row + 1, pl.ds(PAD, 32), :], rows // 2, out
        )


def lanes_to_level_1(part, rows, out):
    into = [
        matrix_of(lambda a, b: half(b == lax.div(a, 2))),
        matrix_of(lambda a, b: half(b == lax.div(a, 2) + 64)),
    ]
    group = 8

    def body(i, carry):
        total = 0.0
        for h in range(2):
            stacked = jnp.concatenate([part(h, i * group + k) for k in range(group)], axis=0)
            total = total + dot(stacked, into[h])
        for k in range(group):
            out[i * group + k] = total[32 * k:32 * (k + 1)]
        return carry

    lax.fori_loop(0, rows // group, body, 0)


def pair_layers_and_lanes(spare, rows, out):
    def part(h, row):
        return (
            spare[h, row + 1, pl.ds(PAD, 32, stride=2), :]
            + spare[h, row + 1, pl.ds(PAD + 1, 32, stride=2), :]
        )

    lanes_to_level_1(part, rows, out)


class Coarse:
    def __init__(self, source, weight, shift_now, rows, layers, shift, unrolled):
        self.source, self.weight, self.shift_now = source, weight, shift_now
        self.rows, self.layers, self.shift = rows, layers, shift
        self.unrolled = unrolled

    def set_weight(self, edge):
        for row in range(self.rows):
            self.weight[row] = edge * (RELAX_WEIGHT / (6.0 + self.shift_now[row]))

    def first(self, dst):
        for row in range(self.rows):
            dst[row + 1, pl.ds(PAD, self.layers), :] = self.weight[row] * self.source[row]

    def relax(self, src, dst):
        def emit(row, h, centre, total):
            value = (1.0 - RELAX_WEIGHT) * centre + self.weight[row] * (total + self.source[row])
            dst[row + 1, pl.ds(PAD, self.layers), :] = value

        stencil_pass(src, 1, 0, self.rows, 0, self.layers, self.shift, emit, 4, self.unrolled)

    def defect_pairs(self, src, spare):
        held = []

        def emit(row, h, centre, total):
            value = self.source[row] + total - (6.0 + self.shift_now[row]) * centre
            if not held:
                held.append(value)
            else:
                spare[lax.div(row, 2) + 1 if not isinstance(row, int) else row // 2 + 1,
                      pl.ds(PAD, self.layers), :] = held.pop() + value

        stencil_pass(src, 1, 0, self.rows, 0, self.layers, self.shift, emit, 4, self.unrolled)

    def pairs_of(self, spare, row):
        count = self.layers // 2
        return (
            spare[row + 1, pl.ds(PAD, count, stride=2), :]
            + spare[row + 1, pl.ds(PAD + 1, count, stride=2), :]
        )

    def shift_pairs(self, spare):
        for row in range(self.rows // 2):
            spare[row + 1, pl.ds(PAD, self.layers), :] = (
                self.shift_now[2 * row] + self.shift_now[2 * row + 1]
            )


def pack_level_2(level, spare, out, offset):
    each = level.rows // 8
    for_out = 0.0
    for g in range(4):
        into = matrix_of(lambda a, b: half((a < 64) & (b == lax.div(a, 2) + 32 * g)))
        stacked = jnp.concatenate(
            [level.pairs_of(spare, g * each + k) for k in range(each)], axis=0
        )
        for_out = for_out + dot(stacked, into)
    for k in range(each):
        out[offset + k] = for_out[16 * k:16 * (k + 1)]


def unpack_level_2(own, right, left, offset, each, out):
    lane = lanes_iota((16, LANES))
    for g in range(4):
        for k in range(each):
            parts = []
            for ref, place in ((own, 0), (right, 32), (left, 96)):
                value = ref[offset + k]
                amount = (place - 32 * g) % LANES
                parts.append(pltpu.roll(value, amount, axis=1) if amount else value)
            out[g * each + k] = jnp.where(
                lane < 32, parts[0],
                jnp.where(lane < 64, parts[1], jnp.where(lane < 96, 0.0, parts[2])),
            )


def coarsest(source, diagonal, edge, rows):
    weight = edge * (RELAX_WEIGHT / diagonal)
    layer = lax.broadcasted_iota(jnp.int32, (8, LANES), 0)
    weights = [weight[r] for r in range(rows)]
    sources = [source[r] for r in range(rows)]
    values = tuple(w * b for w, b in zip(weights, sources))

    def body(i, values):
        zero = jnp.zeros((8, LANES), F32)
        new = []
        for r in range(rows):
            v = values[r]
            total = (values[r - 1] if r > 0 else zero) + (values[r + 1] if r < rows - 1 else zero)
            total = total + jnp.where(layer == 0, 0.0, pltpu.roll(v, 1, axis=0))
            total = total + jnp.where(layer == 7, 0.0, pltpu.roll(v, 7, axis=0))
            total = total + side_sum([v])[0]
            new.append((1.0 - RELAX_WEIGHT) * v + weights[r] * (total + sources[r]))
        return tuple(new)

    return lax.fori_loop(0, COARSE_SWEEPS - 1, body, values)


def zero_rim(ref, rows, layers, halves):
    for h in range(halves):
        def body(row, carry):
            zero = jnp.zeros((PAD, LANES), F32)
            put(ref, h, halves, row, pl.ds(0, PAD), zero)
            put(ref, h, halves, row, pl.ds(PAD + layers, PAD), zero)
            return carry

        lax.fori_loop(0, rows + 2, body, 0)
        zero = jnp.zeros((layers, LANES), F32)
        put(ref, h, halves, 0, pl.ds(PAD, layers), zero)
        put(ref, h, halves, rows + 1, pl.ds(PAD, layers), zero)


def add_prolonged(target, source_rows, layers, dup):
    for row, value in source_rows:
        dup[row % 2, pl.ds(0, layers, stride=2), :] = value
        dup[row % 2, pl.ds(1, layers, stride=2), :] = value
        both = dup[row % 2, pl.ds(0, 2 * layers), :]
        for k in range(2):
            place = (2 * row + k + 1, pl.ds(PAD, 2 * layers), slice(None))
            target[place] = target[place] + both


def level_1_down(level, va, vb, spare):
    level.first(va)
    level.relax(va, vb)
    level.relax(vb, va)
    level.relax(va, vb)
    level.defect_pairs(vb, spare)


def coarse_part(own, right, left, own_s, right_s, left_s, s_ref, rows2, refs):
    va, vb, b2, sh2, w2, dup2 = refs
    shift, has_left, has_right = s_ref[0], s_ref[2], s_ref[3]
    each = rows2 // 4
    unpack_level_2(own, right, left, 0, each, b2)
    unpack_level_2(own_s, right_s, left_s, each, each, sh2)
    level = Coarse(b2, w2, sh2, rows2, 16, shift, True)
    level.set_weight(edge_mask(2, has_left, has_right))
    level.first(va)
    level.relax(va, vb)
    level.relax(vb, va)
    level.relax(va, vb)

    into = matrix_of(
        lambda a, b: half(b == jnp.where(a < 64, lax.div(a, 2), 64 + lax.div(a, 2)))
    )
    rows3 = rows2 // 2

    def to_level_3(spare):
        stacked = jnp.concatenate([level.pairs_of(spare, r) for r in range(rows3)], axis=0)
        return dot(stacked, into).reshape(rows3, 8, LANES)

    level.shift_pairs(va)
    shift_3 = to_level_3(va)
    level.defect_pairs(vb, va)
    source_3 = to_level_3(va)
    values = coarsest(source_3, 6.0 + shift_3, edge_mask(3, has_left, has_right), rows3)
    out_of = matrix_of(
        lambda a, b: one(a == jnp.where(b < 64, lax.div(b, 2), 64 + lax.div(b, 2)))
    )
    spread = dot(jnp.concatenate(values, axis=0), out_of)
    add_prolonged(vb, [(r, spread[8 * r:8 * (r + 1)]) for r in range(rows3)], 8, dup2)
    level.relax(vb, va)
    level.relax(va, vb)
    level.relax(vb, va)
    level.relax(va, vb)
    return vb


def level_1_up(level, e2, rows2, va, vb, dup):
    out_of = matrix_of(
        lambda a, b: one(a == jnp.where(b < 96, lax.div(b, 2), 64 + lax.div(b, 2)))
    )
    stacked = jnp.concatenate([e2[r + 1, pl.ds(PAD, 16), :] for r in range(rows2)], axis=0)
    spread = dot(stacked, out_of)
    add_prolonged(va, [(r, spread[16 * r:16 * (r + 1)]) for r in range(rows2)], 16, dup)
    level.relax(va, vb)
    level.relax(vb, va)
    level.relax(va, vb)
    level.relax(vb, va)


def add_to_fine(e1, target, first_pair, pairs, dup):
    out_of = [
        matrix_of(lambda a, b: one(a == lax.div(b, 2))),
        matrix_of(lambda a, b: one(a == lax.div(b, 2) + 64)),
    ]
    group = 4

    def body(i, carry):
        start = first_pair + i * group
        stacked = jnp.concatenate(
            [e1[start + k + 1, pl.ds(PAD, 32), :] for k in range(group)], axis=0
        )
        for h in range(2):
            spread = dot(stacked, out_of[h])
            for k in range(group):
                part = spread[32 * k:32 * (k + 1)]
                dup[h * group + k, pl.ds(0, 32, stride=2), :] = part
                dup[h * group + k, pl.ds(1, 32, stride=2), :] = part
        for h in range(2):
            for k in range(group):
                both = dup[h * group + k]
                for m in range(2):
                    row = 2 * (start + k) + m + 1
                    place = (h, row, pl.ds(PAD, 64), slice(None))
                    target[place] = target[place] + both
        return carry

    lax.fori_loop(0, pairs // group, body, 0)


def interior(ref, rows):
    return ref.at[:, pl.ds(1, rows), pl.ds(PAD, LAYERS), :]


def load_source(gathered, source, height, sems):
    copies = []
    for h in range(2):
        copies.append(pltpu.make_async_copy(
            gathered.at[:, h, pl.ds(0, LAYERS), :], source.at[h], sems.at[h]))
        copies.append(pltpu.make_async_copy(
            gathered.at[:, h, pl.ds(LAYERS, 8), :], height.at[h], sems.at[2 + h]))
    for copy in copies:
        copy.start()
    return copies


def pack_kernel(right_side, terrain, own, to_left, to_right):
    lane = lanes_iota((32, LANES))
    heights = terrain[pl.ds(0, TILE_ROWS), :]
    for z in range(1, 32):
        heights = heights + terrain[pl.ds(TILE_ROWS * z, TILE_ROWS), :]
    heights = heights.astype(F32)
    for r in range(TILE_ROWS):
        low = right_side[pl.ds(r, 32, stride=TILE_ROWS), :]
        high = right_side[pl.ds(32 * TILE_ROWS + r, 32, stride=TILE_ROWS), :]
        own[r, pl.ds(0, 32), :] = low
        own[r, pl.ds(32, 32), :] = high
        height = jnp.broadcast_to(heights[r:r + 1], (8, LANES))
        own[r, pl.ds(64, 8), :] = height
        to_left[r, pl.ds(0, 32), :] = jnp.where(lane < 64, low, pltpu.roll(high, 64, axis=1))
        to_right[r, pl.ds(0, 32), :] = jnp.where(lane < 64, pltpu.roll(low, 64, axis=1), high)
        to_left[r, pl.ds(32, 8), :] = height
        to_right[r, pl.ds(32, 8), :] = height


def merge_kernel(own, from_right, from_left, out):
    lane = lanes_iota((32, LANES))
    for r in range(TILE_ROWS):
        out[r, 0] = own[r]
        right, left = from_right[r, pl.ds(0, 32), :], from_left[r, pl.ds(0, 32), :]
        out[r, 1, pl.ds(0, 32), :] = jnp.where(lane < 64, right, pltpu.roll(left, 64, axis=1))
        out[r, 1, pl.ds(32, 32), :] = jnp.where(lane < 64, pltpu.roll(right, 64, axis=1), left)
        out[r, 1, pl.ds(64, 8), :] = jnp.where(
            lane[0:8] < 64, from_right[r, pl.ds(32, 8), :], from_left[r, pl.ds(32, 8), :]
        )


def down_kernel(rows, s_ref, gathered, u0, u1, b1, sh1, packed,
                source, height, va0, vb0, va1, vb1, w1, sems):
    copies = load_source(gathered, source, height, sems)
    shift, has_left, has_right = s_ref[0], s_ref[2], s_ref[3]
    for ref in (va0, vb0):
        zero_rim(ref, rows, LAYERS, 2)
    for ref in (va1, vb1):
        zero_rim(ref, rows // 2, 32, 1)
    for copy in copies:
        copy.wait()
    fine = Fine(source, height, edge_mask(0, has_left, has_right), shift)
    fine.coarse_shift(rows, va0, sh1)
    fine.first(va0, rows)
    fine.relax(va0, vb0, 0, rows)
    fine.relax(vb0, va0, 0, rows)
    fine.relax(va0, vb0, 0, rows)
    save = pltpu.make_async_copy(interior(vb0, rows), u0, sems.at[0])
    save.start()
    fine.restricted_defect(vb0, va0, rows, b1)
    level = Coarse(b1, w1, sh1, rows // 2, 32, shift, False)
    level.set_weight(edge_mask(1, has_left, has_right))
    level_1_down(level, va1, vb1, va1)
    pack_level_2(level, va1, packed, 0)
    level.shift_pairs(va1)
    pack_level_2(level, va1, packed, rows // 16)
    for row in range(rows // 2):
        u1[row] = vb1[row + 1, pl.ds(PAD, 32), :]
    save.wait()


def middle_kernel(rows, s_ref, gathered, u0, u1, b1, sh1, own, right, left,
                  u0_out, u1_out, b1_out, packed,
                  source, height, va0, vb0, va1, vb1, w1, va2, vb2, b2, sh2, w2,
                  dup0, dup1, dup2, sems):
    shift, has_left, has_right = s_ref[0], s_ref[2], s_ref[3]
    copies = load_source(gathered, source, height, sems)
    fetch = pltpu.make_async_copy(u0, interior(va0, rows), sems.at[4])
    fetch.start()
    for ref in (va2, vb2):
        zero_rim(ref, rows // 4, 16, 1)
    for ref in (va1, vb1):
        zero_rim(ref, rows // 2, 32, 1)
    e2 = coarse_part(own, right, left, own, right, left, s_ref, rows // 4,
                     (va2, vb2, b2, sh2, w2, dup2))
    level = Coarse(b1, w1, sh1, rows // 2, 32, shift, False)
    level.set_weight(edge_mask(1, has_left, has_right))
    for row in range(rows // 2):
        va1[row + 1, pl.ds(PAD, 32), :] = u1[row]
    level_1_up(level, e2, rows // 4, va1, vb1, dup1)
    fetch.wait()
    for copy in copies:
        copy.wait()
    for ref in (va0, vb0):
        zero_rim(ref, rows, LAYERS, 2)
    fine = Fine(source, height, edge_mask(0, has_left, has_right), shift)
    add_to_fine(va1, va0, 0, rows // 2, dup0)
    for _ in range(SWEEPS):
        fine.relax(va0, vb0, 0, rows)
        fine.relax(vb0, va0, 0, rows)
    save = pltpu.make_async_copy(interior(va0, rows), u0_out, sems.at[0])
    save.start()
    fine.restricted_defect(va0, vb0, rows, b1_out)
    level = Coarse(b1_out, w1, sh1, rows // 2, 32, shift, False)
    level_1_down(level, va1, vb1, va1)
    pack_level_2(level, va1, packed, 0)
    for row in range(rows // 2):
        u1_out[row] = vb1[row + 1, pl.ds(PAD, 32), :]
    save.wait()


def last_kernel(rows, s_ref, gathered, u0, u1, b1, sh1, own, right, left, own_s, right_s, left_s,
                out, source, height, va0, vb0, va1, vb1, w1, va2, vb2, b2, sh2, w2,
                dup0, dup1, dup2, sems):
    shift, has_left, has_right = s_ref[0], s_ref[2], s_ref[3]
    start, mine = s_ref[1], s_ref[4]
    window = pl.ds(start, WINDOW)
    copies = []
    for h in range(2):
        copies.append(pltpu.make_async_copy(
            gathered.at[window, h, pl.ds(0, LAYERS), :], source.at[h], sems.at[h]))
        copies.append(pltpu.make_async_copy(
            gathered.at[window, h, pl.ds(LAYERS, 8), :], height.at[h], sems.at[2 + h]))
    copies.append(pltpu.make_async_copy(
        u0.at[:, window], interior(va0, WINDOW), sems.at[4]))
    for copy in copies:
        copy.start()
    for ref in (va2, vb2):
        zero_rim(ref, rows // 4, 16, 1)
    for ref in (va1, vb1):
        zero_rim(ref, rows // 2, 32, 1)
    e2 = coarse_part(own, right, left, own_s, right_s, left_s, s_ref, rows // 4,
                     (va2, vb2, b2, sh2, w2, dup2))
    level = Coarse(b1, w1, sh1, rows // 2, 32, shift, False)
    level.set_weight(edge_mask(1, has_left, has_right))
    for row in range(rows // 2):
        va1[row + 1, pl.ds(PAD, 32), :] = u1[row]
    level_1_up(level, e2, rows // 4, va1, vb1, dup1)
    for copy in copies:
        copy.wait()
    for ref in (va0, vb0):
        zero_rim(ref, WINDOW, LAYERS, 2)
    fine = Fine(source, height, edge_mask(0, has_left, has_right), shift)

    class Shifted:
        def __getitem__(self, index):
            row, layers, lanes = index
            return va1[row + lax.div(start, 2), layers, lanes]

    add_to_fine(Shifted(), va0, 0, WINDOW // 2, dup0)
    for _ in range(SWEEPS // 2):
        fine.relax(va0, vb0, 0, WINDOW)
        fine.relax(vb0, va0, 0, WINDOW)
    for r in range(TILE_ROWS):
        out[pl.ds(r, LAYERS, stride=TILE_ROWS), :] = va0[0, mine - start + r + 1, pl.ds(PAD, LAYERS), :]


def spec(space=pltpu.VMEM):
    return pl.BlockSpec(memory_space=space)


def params():
    return pltpu.CompilerParams(vmem_limit_bytes=VMEM_LIMIT)


def shape(*dims):
    return jax.ShapeDtypeStruct(dims, F32)


def vmem(*dims):
    return pltpu.VMEM(dims, F32)


def level_0_scratch(rows):
    return [
        vmem(2, rows, LAYERS, LANES),
        vmem(2, rows, 8, LANES),
        vmem(2, rows + 2, LAYERS + 2 * PAD, LANES),
        vmem(2, rows + 2, LAYERS + 2 * PAD, LANES),
    ]


def level_1_scratch(rows):
    return [
        vmem(rows // 2 + 2, 32 + 2 * PAD, LANES),
        vmem(rows // 2 + 2, 32 + 2 * PAD, LANES),
        vmem(rows // 2, 32, LANES),
    ]


def level_2_scratch(rows):
    return [
        vmem(rows // 4 + 2, 16 + 2 * PAD, LANES),
        vmem(rows // 4 + 2, 16 + 2 * PAD, LANES),
        vmem(rows // 4, 16, LANES),
        vmem(rows // 4, 16, LANES),
        vmem(rows // 4, 16, LANES),
        vmem(8, 64, LANES),
        vmem(2, 32, LANES),
        vmem(2, 16, LANES),
    ]


def per_device(right_side, terrain):
    gx, gy = lax.axis_size("gx"), lax.axis_size("gy")
    rows = TILE_ROWS * gx
    i, j = lax.axis_index("gx"), lax.axis_index("gy")
    mine = TILE_ROWS * i
    start = jnp.clip(mine - 4, 0, rows - WINDOW)
    scalars = jnp.stack([
        jnp.int32(PAD), start, (j > 0).astype(jnp.int32), (j < gy - 1).astype(jnp.int32), mine
    ])
    rightward = [(k, k + 1) for k in range(gy - 1)]
    leftward = [(k + 1, k) for k in range(gy - 1)]

    def exchange(to_left, to_right):
        from_right = lax.ppermute(to_left, "gy", leftward)
        from_left = lax.ppermute(to_right, "gy", rightward)
        return from_right, from_left

    flat = LAYERS * TILE_ROWS
    own, to_left, to_right = pl.pallas_call(
        pack_kernel,
        out_shape=(shape(TILE_ROWS, 72, LANES), shape(TILE_ROWS, 40, LANES),
                   shape(TILE_ROWS, 40, LANES)),
        in_specs=[spec()] * 2, out_specs=(spec(),) * 3, name="pack",
    )(right_side.reshape(flat, LANES), terrain.reshape(flat, LANES))
    from_right, from_left = exchange(to_left, to_right)
    merged = pl.pallas_call(
        merge_kernel, out_shape=shape(TILE_ROWS, 2, 72, LANES),
        in_specs=[spec()] * 3, out_specs=spec(), name="merge",
    )(own, from_right, from_left)
    gathered = lax.all_gather(merged, "gx", axis=0, tiled=True)

    smem, hbm = spec(pltpu.SMEM), spec(pl.ANY)
    each = rows // 16
    level_1 = shape(rows // 2, 32, LANES)
    u0, u1, b1, sh1, packed = pl.pallas_call(
        lambda *refs: down_kernel(rows, *refs),
        out_shape=(shape(2, rows, LAYERS, LANES), level_1, level_1, level_1,
                   shape(2 * each, 16, LANES)),
        in_specs=[smem, hbm], out_specs=(hbm,) + (spec(),) * 4,
        scratch_shapes=level_0_scratch(rows) + level_1_scratch(rows)
        + [pltpu.SemaphoreType.DMA((5,))],
        compiler_params=params(), name="down",
    )(scalars, gathered)

    right, left = exchange(packed, packed)
    u0, u1, b1, packed_2 = pl.pallas_call(
        lambda *refs: middle_kernel(rows, *refs),
        out_shape=(shape(2, rows, LAYERS, LANES), level_1, level_1, shape(each, 16, LANES)),
        in_specs=[smem, hbm, hbm] + [spec()] * 6, out_specs=(hbm,) + (spec(),) * 3,
        scratch_shapes=level_0_scratch(rows) + level_1_scratch(rows) + level_2_scratch(rows)
        + [pltpu.SemaphoreType.DMA((5,))],
        compiler_params=params(), name="middle",
    )(scalars, gathered, u0, u1, b1, sh1, packed, right, left)

    right_2, left_2 = exchange(packed_2, packed_2)
    out = pl.pallas_call(
        lambda *refs: last_kernel(rows, *refs),
        out_shape=shape(flat, LANES),
        in_specs=[smem, hbm, hbm] + [spec()] * 9, out_specs=spec(),
        scratch_shapes=level_0_scratch(WINDOW) + level_1_scratch(rows) + level_2_scratch(rows)
        + [pltpu.SemaphoreType.DMA((5,))],
        compiler_params=params(), name="last",
    )(scalars, gathered, u0, u1, b1, sh1, packed_2, right_2, left_2, packed, right, left)
    return out.reshape(LAYERS, TILE_ROWS, LANES)


def solution(mesh):
    in_specs = (P(None, "gx", "gy"), P(None, "gx", "gy"))
    out_specs = P(None, "gx", "gy")
    return jax.shard_map(
        per_device, mesh=mesh, in_specs=in_specs, out_specs=out_specs, check_vma=False
    )
```

time: 1380 us -> 227 us (0.16); the launches traced: 1360 us -> 225 us
  starting transfers between devices: 910 us -> 23.2 us
  waiting for transfers between devices: 287 us -> 45.5 us
  Pallas kernels: 0 us -> 140 us
  local copies, waits for them, and re-layouts: 112 us -> 2.49 us
  other arithmetic: 46.2 us -> 0 us
    ppermute x252 -> x6, starting transfers between devices: 910 us -> 23.2 us  [the longest x3 14.9 us: exchange(): from_right = lax.ppermute(to_left, 'gy', leftward)]
    ppermute x252 -> x6, waiting for transfers between devices: 287 us -> 12 us  [the longest x3 6.79 us: exchange(): from_left = lax.ppermute(to_right, 'gy', rightward)]
    pallas_call x0 -> x5, Pallas kernels: none -> 140 us  [the longest x1 80 us: per_device(): pl.pallas_call(lambda *refs: middle_kernel(rows, *refs), out_shape=(shape...]
    reshape x9 -> x0, local copies, waits for them, and re-layouts: 87.1 us -> none  [the longest x5 58.6 us: restrict(): values.reshape(layers_here // 2, 2, rows_here // 2, 2, cols_here // 2, 2)]
    all_gather x0 -> x1, waiting for transfers between devices: none -> 33.5 us  [per_device(): gathered = lax.all_gather(merged, 'gx', axis=0, tiled=True)]
    reduce_sum x11 -> x0, other arithmetic: 22.1 us -> none  [restrict(): return 0.5 * blocks.sum(axis=(1, 3, 5))]
    add x66 -> x0, other arithmetic: 19.6 us -> none  [the longest x56 18 us: relax_once(): centre + RELAX_WEIGHT * (source - diagonal * centre + neighbor_sum) / dia...]
    broadcast_in_dim x8 -> x0, local copies, waits for them, and re-layouts: 13.8 us -> none  [prolong(): jnp.broadcast_to(values[:, None, :, None, :, None], (layers_here, 2, rows...]
  transfers between devices with their start and end apart: 252 -> 7, of which waited for: 156 -> 7; matrix products, arithmetic and copies ran while one was open for 2% -> 0% of each run, Pallas kernels for 0% -> 0%
where the time goes in v1:
time: 227 us; the launch traced here: 225 us
  Pallas kernels  140 us (62%)
  waiting for transfers between devices  45.5 us (20%)
  starting transfers between devices  23.2 us (10%)
  between operations  13.5 us (6%)
  local copies, waits for them, and re-layouts  2.49 us (1%)
    pallas_call x1, Pallas kernels, per_device(): pl.pallas_call(lambda *refs: middle_kernel(rows, *refs), out_shape=(shape...  80 us
    pallas_call x1, Pallas kernels, per_device(): pl.pallas_call(lambda *refs: down_kernel(rows, *refs), out_shape=(shape(2...  39.7 us
    all_gather x1, waiting for transfers between devices, per_device(): gathered = lax.all_gather(merged, 'gx', axis=0, tiled=True)  33.5 us
    pallas_call x1, Pallas kernels, per_device(): pl.pallas_call(lambda *refs: last_kernel(rows, *refs), out_shape=shape(fl...  16.6 us
    ppermute x3, starting transfers between devices, exchange(): from_right = lax.ppermute(to_left, 'gy', leftward)  14.9 us
    ppermute x3, starting transfers between devices, exchange(): from_left = lax.ppermute(to_right, 'gy', rightward)  8.31 us
    ppermute x3, waiting for transfers between devices, exchange(): from_left = lax.ppermute(to_right, 'gy', rightward)  6.79 us
    ppermute x3, waiting for transfers between devices, exchange(): from_right = lax.ppermute(to_left, 'gy', leftward)  5.24 us
  transfers between devices with their start and end apart: 7, of which 7 were waited for; matrix products, arithmetic and copies ran while one was open for 0% of the time, Pallas kernels for 0%

profile of v1, /device:TPU:6, one launch (start us, length us, event | category | flops | bytes accessed | tf_op | source)
XLA Modules:
  0.0 225.0 jit_solution(6048933527621544109)
XLA Ops:
  6.5 1.9 pack.1
  8.5 5.2 %collective-permute-start = (f32[8,40,128]{2,1,0:T(8,128)}, f32[8,40,128]{2,1,0:T(8,128)S(1)}, u32[]{:S(2)}, u32[]{:S(2)}) collective-permute-start(f32[8,40,128]{2,1,0:T(8,128)} %get-tuple-element.18), channel_id=1, source_target_pairs={{1,0},{2,1},{3,2},{4,3},{5,4},{6,5},{7,6},{8,7},{9,8},{10,9},{11,1... | collective-permute-start | bytes 491528 | tf_op jit(solution)/shard_map/ppermute | solution.py:665
  13.6 1.9 collective-permute-start.1
  15.6 1.8 collective-permute-done.from_right
  17.4 6.1 %collective-permute-done.1.from_left = f32[8,40,128]{2,1,0:T(8,128)S(1)} collective-permute-done((f32[8,40,128]{2,1,0:T(8,128)}, f32[8,40,128]{2,1,0:T(8,128)S(1)}, u32[]{:S(2)}, u32[]{:S(2)}) %collective-permute-start.1) | collective-permute-done | bytes 163872 | tf_op jit(solution)/shard_map/ppermute | solution.py:666
  23.5 0.7 copy-done.3
  24.2 2.0 merge.1
  26.2 0.0 all-gather.2.cloned.1.call-update
  26.2 0.6 stack.27.refs_0_
  26.9 33.5 %all-gather.2.cloned.1.call-done.refs_1_ = f32[64,2,72,128]{3,2,1,0:T(8,128)} async-done(((f32[8,2,72,128]{3,2,1,0:T(8,128)}), f32[64,2,72,128]{3,2,1,0:T(8,128)}) %all-gather.2.cloned.1.call-update) | async-done | bytes 4718608 | tf_op jit(solution)/shard_map/all_gather | solution.py:681
  60.3 39.7 %down.1 = (f32[2,64,64,128]{3,2,1,0:T(8,128)}, f32[32,32,128]{2,1,0:T(8,128)}, f32[32,32,128]{2,1,0:T(8,128)}, f32[32,32,128]{2,1,0:T(8,128)}, f32[8,16,128]{2,1,0:T(8,128)}) custom-call(s32[5]{0:T(128)} %stack.27.refs_0_, f32[64,2,72,128]{3,2,1,0:T(8,128)} %all-gather.2.cloned.1.call-done.refs_1_), custom_call_target="tpu_custom_call" | custom-call | tf_op jit(solution)/shard_map/down/pallas_call | solution.py:686
  100.1 3.4 %collective-permute-start.3 = (f32[8,16,128]{2,1,0:T(8,128)}, f32[8,16,128]{2,1,0:T(8,128)S(1)}, u32[]{:S(2)}, u32[]{:S(2)}) collective-permute-start(f32[8,16,128]{2,1,0:T(8,128)} %get-tuple-element.24.refs_6_.refs_9_), channel_id=1, source_target_pairs={{0,1},{1,2},{2,3},{3,4},{4,5},{5,6},{6,7},{7,8},{8,9},{9,10},{10,1... | collective-permute-start | bytes 196616 | tf_op jit(solution)/shard_map/ppermute | solution.py:666
  103.5 4.6 %collective-permute-start.2 = (f32[8,16,128]{2,1,0:T(8,128)}, f32[8,16,128]{2,1,0:T(8,128)S(1)}, u32[]{:S(2)}, u32[]{:S(2)}) collective-permute-start(f32[8,16,128]{2,1,0:T(8,128)} %get-tuple-element.24.refs_6_.refs_9_), channel_id=1, source_target_pairs={{1,0},{2,1},{3,2},{4,3},{5,4},{6,5},{7,6},{8,7},{9,8},{10,9},{11,1... | collective-permute-start | bytes 196616 | tf_op jit(solution)/shard_map/ppermute | solution.py:665
  108.0 0.5 collective-permute-done.3.refs_8_.refs_11_
  108.5 1.7 collective-permute-done.2.refs_7_.refs_10_
  110.2 0.0 copy-done
  110.2 0.6 copy-done.1
  110.8 80.0 %middle.1 = (f32[2,64,64,128]{3,2,1,0:T(8,128)}, f32[32,32,128]{2,1,0:T(8,128)}, f32[32,32,128]{2,1,0:T(8,128)}, f32[4,16,128]{2,1,0:T(8,128)}) custom-call(s32[5]{0:T(128)} %stack.27.refs_0_, f32[64,2,72,128]{3,2,1,0:T(8,128)} %all-gather.2.cloned.1.call-done.refs_1_, f32[2,64,64,128]{3,2,1,0:T(8,128)} %get-tuple-element.20.refs_2_, ...), custom_call_target="tpu_custom_call" | custom-call | tf_op jit(solution)/shard_map/middle/pallas_call | solution.py:697
  190.8 3.0 %collective-permute-start.5 = (f32[4,16,128]{2,1,0:T(8,128)}, f32[4,16,128]{2,1,0:T(8,128)S(1)}, u32[]{:S(2)}, u32[]{:S(2)}) collective-permute-start(f32[4,16,128]{2,1,0:T(8,128)} %get-tuple-element.28.refs_6_), channel_id=1, source_target_pairs={{0,1},{1,2},{2,3},{3,4},{4,5},{5,6},{6,7},{7,8},{8,9},{9,10},{10,1... | collective-permute-start | bytes 98312 | tf_op jit(solution)/shard_map/ppermute | solution.py:666
  193.8 5.2 %collective-permute-start.4 = (f32[4,16,128]{2,1,0:T(8,128)}, f32[4,16,128]{2,1,0:T(8,128)S(1)}, u32[]{:S(2)}, u32[]{:S(2)}) collective-permute-start(f32[4,16,128]{2,1,0:T(8,128)} %get-tuple-element.28.refs_6_), channel_id=1, source_target_pairs={{1,0},{2,1},{3,2},{4,3},{5,4},{6,5},{7,6},{8,7},{9,8},{10,9},{11,1... | collective-permute-start | bytes 98312 | tf_op jit(solution)/shard_map/ppermute | solution.py:665
  199.0 0.2 collective-permute-done.5.refs_8_
  199.2 1.7 collective-permute-done.4.refs_7_
  200.9 0.6 copy-done.5
  201.5 16.6 %last.1 = f32[512,128]{1,0:T(8,128)} custom-call(s32[5]{0:T(128)} %stack.27.refs_0_, f32[64,2,72,128]{3,2,1,0:T(8,128)} %all-gather.2.cloned.1.call-done.refs_1_, f32[2,64,64,128]{3,2,1,0:T(8,128)} %get-tuple-element.25.refs_2_, f32[32,32,128]{2,1,0:T(8,128)} %get-tuple-element.26.refs_3_, f32[32,32,128]{2,1,0:T(8,128)} %get-tuple-element.27.refs_4_, ...), custom_call_target="tpu_custom_call" | custom-call | tf_op jit(solution)/shard_map/last/pallas_call | solution.py:707
  (9 shorter events, 0.0 us)
Async XLA Ops:
  6.5 53.8 %all-gather.2.cloned.1.call-start = ((), (), s32[]{:S(2)}) async-start(), calls=%async_computation | async-start | bytes 5308416 | tf_op jit(solution)/shard_map/all_gather | solution.py:681
  8.5 8.9 %collective-permute-start = (f32[8,40,128]{2,1,0:T(8,128)}, f32[8,40,128]{2,1,0:T(8,128)S(1)}, u32[]{:S(2)}, u32[]{:S(2)}) collective-permute-start(f32[8,40,128]{2,1,0:T(8,128)} %get-tuple-element.18), channel_id=1, source_target_pairs={{1,0},{2,1},{3,2},{4,3},{5,4},{6,5},{7,6},{8,7},{9,8},{10,9},{11,1... | collective-permute-start | bytes 491528 | tf_op jit(solution)/shard_map/ppermute | solution.py:665
  13.6 9.9 %collective-permute-start.1 = (f32[8,40,128]{2,1,0:T(8,128)}, f32[8,40,128]{2,1,0:T(8,128)S(1)}, u32[]{:S(2)}, u32[]{:S(2)}) collective-permute-start(f32[8,40,128]{2,1,0:T(8,128)} %get-tuple-element.19), channel_id=1, source_target_pairs={{0,1},{1,2},{2,3},{3,4},{4,5},{5,6},{6,7},{7,8},{8,9},{9,10},{10,1... | collective-permute-start | bytes 491528 | tf_op jit(solution)/shard_map/ppermute | solution.py:666
  17.4 6.1 %copy-start.2 = (f32[8,40,128]{2,1,0:T(8,128)}, f32[8,40,128]{2,1,0:T(8,128)S(1)}, u32[]{:S(2)}) copy-start(f32[8,40,128]{2,1,0:T(8,128)S(1)} %collective-permute-done.from_right) | copy-start | bytes 491524
  23.5 0.7 copy-start.3
  100.1 8.5 %collective-permute-start.3 = (f32[8,16,128]{2,1,0:T(8,128)}, f32[8,16,128]{2,1,0:T(8,128)S(1)}, u32[]{:S(2)}, u32[]{:S(2)}) collective-permute-start(f32[8,16,128]{2,1,0:T(8,128)} %get-tuple-element.24.refs_6_.refs_9_), channel_id=1, source_target_pairs={{0,1},{1,2},{2,3},{3,4},{4,5},{5,6},{6,7},{7,8},{8,9},{9,10},{10,1... | collective-permute-start | bytes 196616 | tf_op jit(solution)/shard_map/ppermute | solution.py:666
  103.5 6.8 %collective-permute-start.2 = (f32[8,16,128]{2,1,0:T(8,128)}, f32[8,16,128]{2,1,0:T(8,128)S(1)}, u32[]{:S(2)}, u32[]{:S(2)}) collective-permute-start(f32[8,16,128]{2,1,0:T(8,128)} %get-tuple-element.24.refs_6_.refs_9_), channel_id=1, source_target_pairs={{1,0},{2,1},{3,2},{4,3},{5,4},{6,5},{7,6},{8,7},{9,8},{10,9},{11,1... | collective-permute-start | bytes 196616 | tf_op jit(solution)/shard_map/ppermute | solution.py:665
  108.5 1.7 copy-start
  110.2 0.6 copy-start.1
  190.8 8.4 %collective-permute-start.5 = (f32[4,16,128]{2,1,0:T(8,128)}, f32[4,16,128]{2,1,0:T(8,128)S(1)}, u32[]{:S(2)}, u32[]{:S(2)}) collective-permute-start(f32[4,16,128]{2,1,0:T(8,128)} %get-tuple-element.28.refs_6_), channel_id=1, source_target_pairs={{0,1},{1,2},{2,3},{3,4},{4,5},{5,6},{6,7},{7,8},{8,9},{9,10},{10,1... | collective-permute-start | bytes 98312 | tf_op jit(solution)/shard_map/ppermute | solution.py:666
  193.8 7.1 %collective-permute-start.4 = (f32[4,16,128]{2,1,0:T(8,128)}, f32[4,16,128]{2,1,0:T(8,128)S(1)}, u32[]{:S(2)}, u32[]{:S(2)}) collective-permute-start(f32[4,16,128]{2,1,0:T(8,128)} %get-tuple-element.28.refs_6_), channel_id=1, source_target_pairs={{1,0},{2,1},{3,2},{4,3},{5,4},{6,5},{7,6},{8,7},{9,8},{10,9},{11,1... | collective-permute-start | bytes 98312 | tf_op jit(solution)/shard_map/ppermute | solution.py:665
  199.2 1.7 copy-start.4
  200.9 0.6 copy-start.5
Sparse Core Ops, SparseCore 0:
  26.3 33.9 all-gather.1

commit v2 on v0

v2 whole, which is shorter than its diff:
```python
import jax
import jax.numpy as jnp
from jax import lax
from jax.experimental import pallas as pl
from jax.experimental.pallas import tpu as pltpu
from jax.sharding import PartitionSpec as P

SWEEPS = 4
COARSE_SWEEPS = 8
RELAX_WEIGHT = 0.8
TERRAIN_PENALTY = 0.05

F32 = jnp.float32
LANES = 128
SUB = 8
LAYERS = 64
TILE_ROWS = 8
WINDOW = 16
VMEM_LIMIT = 56 * 1024 * 1024

D_AIR = 6.0
D_TERRAIN = 6.0 + TERRAIN_PENALTY


def lanes_iota(shape):
    return lax.broadcasted_iota(jnp.int32, shape, len(shape) - 1)


def edge_mask(level, has_left, has_right):
    lane = lanes_iota((1, LANES))
    zero = jnp.zeros((1, LANES), F32)
    left = zero + has_left.astype(F32)
    right = zero + has_right.astype(F32)
    if level < 2:
        return jnp.where(lane < 64, 1.0, jnp.where(lane < 96, right, left))
    if level == 2:
        return jnp.where(
            lane < 32, 1.0, jnp.where(lane < 64, right, jnp.where(lane < 96, 0.0, left))
        )
    return jnp.where(
        lane < 16, 1.0, jnp.where(lane < 32, right, jnp.where(lane < 112, 0.0, left))
    )


def dot(values, matrix):
    return lax.dot_general(
        values, matrix, (((1,), (0,)), ((), ())),
        precision=lax.Precision.HIGHEST, preferred_element_type=F32,
    )


def matrix_of(rule, value=1.0):
    row = lax.broadcasted_iota(jnp.int32, (LANES, LANES), 0)
    col = lax.broadcasted_iota(jnp.int32, (LANES, LANES), 1)
    return jnp.where(rule(row, col), value, 0.0).astype(F32)


def layer_sum(v):
    count = v.shape[0]
    sub = lax.broadcasted_iota(jnp.int32, (1, SUB, LANES), 1)
    below = jnp.where(sub == 0, 0.0, pltpu.roll(v[count - 1:], 1, axis=1))
    above = jnp.where(sub == SUB - 1, 0.0, pltpu.roll(v[:1], SUB - 1, axis=1))
    if count == 1:
        return below + above
    return jnp.concatenate([below, v[:-1]], axis=0) + jnp.concatenate([v[1:], above], axis=0)


def column_sum(parts):
    if len(parts) == 1:
        v = parts[0]
        return [pltpu.roll(v, 1, axis=2) + pltpu.roll(v, LANES - 1, axis=2)]
    even, odd = parts
    return [odd + pltpu.roll(odd, 1, axis=2), even + pltpu.roll(even, LANES - 1, axis=2)]


def stencil_group(load, first, count, emit):
    held = [load(first + k - 1) for k in range(count + 2)]
    stores = []
    for k in range(count):
        centre = held[k + 1]
        sides = column_sum(centre)
        pairs = []
        for h, v in enumerate(centre):
            total = held[k][h] + held[k + 2][h]
            pairs.append((v, total + layer_sum(v) + sides[h]))
        stores.append(emit(first + k, pairs))
    for store in stores:
        store()


def over_rows(start, rows, group, body):
    if isinstance(rows, int) and rows <= group:
        body(start, rows)
        return

    def step(i, carry):
        body(start + i * group, group)
        return carry

    lax.fori_loop(0, rows // group, step, 0)


class Fine:
    def __init__(self, source, weight, height):
        self.source, self.weight, self.height = source, weight, height

    @staticmethod
    def loader(src):
        return lambda row: [src[h, row + 1] for h in range(2)]

    def ground(self, row, h):
        layer = (
            8 * lax.broadcasted_iota(jnp.int32, (8, SUB, LANES), 1)
            + lax.broadcasted_iota(jnp.int32, (8, SUB, LANES), 0)
        ).astype(F32)
        return layer < self.height[h, row][None]

    def relax(self, src, dst, start, rows, group):
        def emit(row, pairs):
            new = [
                (1.0 - RELAX_WEIGHT) * v + self.weight[h, row] * (total + self.source[h, row])
                for h, (v, total) in enumerate(pairs)
            ]

            def store():
                for h in range(2):
                    dst[h, row + 1] = new[h]

            return store

        over_rows(start, rows, group,
                  lambda first, count: stencil_group(self.loader(src), first, count, emit))

    def restricted_defect(self, src, rows, out):
        load = self.loader(src)

        def body(first, count):
            sums = []

            def emit(row, pairs):
                total = 0.0
                for h, (v, near) in enumerate(pairs):
                    diagonal = jnp.where(self.ground(row, h), D_TERRAIN, D_AIR)
                    total = total + (self.source[h, row] + near - diagonal * v)
                sums.append(total)
                return lambda: None

            stencil_group(load, first, count, emit)
            for k in range(count // 2):
                both = sums[2 * k] + sums[2 * k + 1]
                for z in range(4):
                    out[lax.div(first, 2) + k, z] = 0.5 * (both[2 * z] + both[2 * z + 1])

        over_rows(0, rows, 8, body)

    def coarse_shift(self, rows, out):
        base = (
            8 * lax.broadcasted_iota(jnp.int32, (4, SUB, LANES), 1)
            + 2 * lax.broadcasted_iota(jnp.int32, (4, SUB, LANES), 0)
        ).astype(F32)

        def body(first, count):
            for k in range(count):
                total = 0.0
                for h in range(2):
                    for m in range(2):
                        height = self.height[h, 2 * (first + k) + m][None]
                        total = total + jnp.clip(height - base, 0.0, 2.0)
                out[first + k] = (0.5 * TERRAIN_PENALTY) * total

        over_rows(0, rows // 2, 4, body)


class Coarse:
    def __init__(self, source, weight, shift_now, rows, group):
        self.source, self.weight, self.shift_now = source, weight, shift_now
        self.rows, self.group = rows, group

    def set_weight(self, edge):
        def body(first, count):
            for k in range(count):
                self.weight[first + k] = edge * (RELAX_WEIGHT / (6.0 + self.shift_now[first + k]))

        over_rows(0, self.rows, self.group, body)

    def first(self, dst):
        def body(first, count):
            for k in range(count):
                dst[first + k + 1] = self.weight[first + k] * self.source[first + k]

        over_rows(0, self.rows, self.group, body)

    def relax(self, src, dst):
        def emit(row, pairs):
            v, total = pairs[0]
            new = (1.0 - RELAX_WEIGHT) * v + self.weight[row] * (total + self.source[row])

            def store():
                dst[row + 1] = new

            return store

        load = lambda row: [src[row + 1]]
        over_rows(0, self.rows, self.group,
                  lambda first, count: stencil_group(load, first, count, emit))

    def defect_pairs(self, src):
        sums = []

        def emit(row, pairs):
            v, total = pairs[0]
            sums.append(self.source[row] + total - (6.0 + self.shift_now[row]) * v)
            return lambda: None

        stencil_group(lambda row: [src[row + 1]], 0, self.rows, emit)
        return pair_up(sums)

    def shift_pairs(self):
        return pair_up([self.shift_now[row] for row in range(self.rows)])


def pair_up(rows):
    out = []
    for k in range(len(rows) // 2):
        both = rows[2 * k] + rows[2 * k + 1]
        out.append(jnp.stack([both[2 * z] + both[2 * z + 1] for z in range(both.shape[0] // 2)]))
    return out


def pack_level_2(pairs, out, offset):
    into = matrix_of(lambda a, b: (a < 64) & (b == lax.div(a, 2)), 0.5)
    count = len(pairs) // 4
    flat = jnp.stack(pairs).reshape(len(pairs) * 2 * SUB, LANES)
    lanes = dot(flat, into).reshape(4, count, 2, SUB, LANES)
    total = lanes[0]
    for g in range(1, 4):
        total = total + pltpu.roll(lanes[g], 32 * g, axis=3)
    out[pl.ds(offset, count)] = total


def unpack_level_2(own, right, left, offset, each, out):
    lane = lanes_iota((each, 2, SUB, LANES))
    for g in range(4):
        parts = []
        for ref, place in ((own, 0), (right, 32), (left, 96)):
            value = ref[pl.ds(offset, each)]
            amount = (place - 32 * g) % LANES
            parts.append(pltpu.roll(value, amount, axis=3) if amount else value)
        out[pl.ds(g * each, each)] = jnp.where(
            lane < 32, parts[0],
            jnp.where(lane < 64, parts[1], jnp.where(lane < 96, 0.0, parts[2])),
        )


def coarsest(source, diagonal, edge, rows):
    weight = edge * (RELAX_WEIGHT / diagonal)
    zero = jnp.zeros((1, SUB, LANES), F32)

    def body(i, v):
        total = jnp.concatenate([zero, v[:-1]], axis=0) + jnp.concatenate([v[1:], zero], axis=0)
        sub = lax.broadcasted_iota(jnp.int32, (rows, SUB, LANES), 1)
        total = total + jnp.where(sub == 0, 0.0, pltpu.roll(v, 1, axis=1))
        total = total + jnp.where(sub == SUB - 1, 0.0, pltpu.roll(v, SUB - 1, axis=1))
        total = total + column_sum([v])[0]
        return (1.0 - RELAX_WEIGHT) * v + weight * (total + source)

    v = weight * source
    for i in range(COARSE_SWEEPS - 1):
        v = body(i, v)
    return v


def zero_rim(ref, rows, halves):
    if halves == 2:
        zero = jnp.zeros((2,) + ref.shape[2:], F32)
        ref[:, 0] = zero
        ref[:, rows + 1] = zero
    else:
        zero = jnp.zeros(ref.shape[1:], F32)
        ref[0] = zero
        ref[rows + 1] = zero


def level_1_down(level, va, vb, packed):
    level.first(va)
    level.relax(va, vb)
    level.relax(vb, va)
    level.relax(va, vb)
    pack_level_2(level.defect_pairs(vb), packed, 0)


def coarse_part(own, right, left, own_s, right_s, left_s, has_left, has_right, rows2, refs):
    va, vb, b2, sh2, w2 = refs
    each = rows2 // 4
    unpack_level_2(own, right, left, 0, each, b2)
    unpack_level_2(own_s, right_s, left_s, each, each, sh2)
    for ref in (va, vb):
        zero_rim(ref, rows2, 1)
    level = Coarse(b2, w2, sh2, rows2, rows2)
    level.set_weight(edge_mask(2, has_left, has_right))
    level.first(va)
    level.relax(va, vb)
    level.relax(vb, va)
    level.relax(va, vb)

    into = matrix_of(
        lambda a, b: b == jnp.where(a < 64, lax.div(a, 2), 64 + lax.div(a, 2)), 0.5
    )
    rows3 = rows2 // 2

    def to_level_3(pairs):
        flat = jnp.stack(pairs).reshape(rows3 * SUB, LANES)
        return dot(flat, into).reshape(rows3, SUB, LANES)

    shift_3 = to_level_3(level.shift_pairs())
    source_3 = to_level_3(level.defect_pairs(vb))
    e3 = coarsest(source_3, 6.0 + shift_3, edge_mask(3, has_left, has_right), rows3)
    out_of = matrix_of(
        lambda a, b: a == jnp.where(b < 64, lax.div(b, 2), 64 + lax.div(b, 2))
    )
    spread = dot(e3.reshape(rows3 * SUB, LANES), out_of).reshape(rows3, SUB, LANES)
    for row in range(rows2):
        vb[row + 1] = vb[row + 1] + spread[row // 2][None]
    for _ in range(SWEEPS // 2):
        level.relax(vb, va)
        level.relax(va, vb)
    return vb


def level_1_up(level, e2, rows2, u1, va, vb):
    out_of = matrix_of(
        lambda a, b: a == jnp.where(b < 96, lax.div(b, 2), 64 + lax.div(b, 2))
    )
    flat = e2[pl.ds(1, rows2)].reshape(rows2 * 2 * SUB, LANES)
    spread = dot(flat, out_of).reshape(rows2, 2, SUB, LANES)
    for row in range(2 * rows2):
        e = spread[row // 2]
        for z in range(4):
            va[row + 1, z] = u1[row, z] + e[z // 2]
    for _ in range(SWEEPS // 2):
        level.relax(va, vb)
        level.relax(vb, va)


def add_to_fine(e1, target, first_pair, pairs):
    def body(first, count):
        for k in range(count):
            e = e1[first_pair + first + k + 1]
            twice = jnp.stack([e[z // 2] for z in range(8)])
            for h in range(2):
                for m in range(2):
                    row = 2 * (first + k) + m + 1
                    target[h, row] = target[h, row] + twice

    over_rows(0, pairs, 4, body)


def interior(ref, rows):
    return ref.at[:, pl.ds(1, rows)]


def first_columns(shape):
    return lax.rem(lax.div(lanes_iota(shape), 32), 2) == 0


def pack_kernel(right_side, terrain, own, to_left, to_right):
    apart = matrix_of(lambda a, b: b == lax.div(a, 2) + 64 * lax.rem(a, 2))
    heights = terrain[pl.ds(0, TILE_ROWS), :]
    for z in range(1, 32):
        heights = heights + terrain[pl.ds(TILE_ROWS * z, TILE_ROWS), :]
    heights = dot(heights.astype(F32), apart)
    own[64] = heights
    heights = pltpu.roll(heights, 64, axis=1)
    to_left[32] = heights
    to_right[32] = heights
    first = first_columns((4, SUB, LANES))
    for r in range(TILE_ROWS):
        layers = [
            right_side[pl.ds(zz * TILE_ROWS + r, SUB, stride=8 * TILE_ROWS), :] for zz in range(8)
        ]
        value = dot(jnp.concatenate(layers, axis=0), apart).reshape(8, SUB, LANES)
        own[pl.ds(8 * r, 8)] = value
        value = pltpu.roll(value, 64, axis=2)
        low, high = value[:4], value[4:]
        to_left[pl.ds(4 * r, 4)] = jnp.where(first, low, pltpu.roll(high, 32, axis=2))
        to_right[pl.ds(4 * r, 4)] = jnp.where(first, pltpu.roll(high, 96, axis=2), low)


def merge_kernel(own, from_right, from_left, out):
    first = first_columns((4, SUB, LANES))
    for r in range(TILE_ROWS):
        part, place = r // 4, 8 * (r % 4)
        out[part, pl.ds(place, 8)] = own[pl.ds(8 * r, 8)]
        right, left = from_right[pl.ds(4 * r, 4)], from_left[pl.ds(4 * r, 4)]
        out[part, pl.ds(32 + place, 4)] = jnp.where(first, right, left)
        out[part, pl.ds(32 + place + 4, 4)] = jnp.where(
            first, pltpu.roll(right, 96, axis=2), pltpu.roll(left, 32, axis=2)
        )
    out[0, 64] = own[64]
    out[1, 64] = jnp.where(first[0], from_right[32], from_left[32])


def down_kernel(rows, s_ref, *refs):
    tiles, refs = refs[:10], refs[10:]
    (u0, source_out, weight_out, height_out, u1, b1, sh1, packed,
     source, weight, height, own, beside, heights, va0, vb0, va1, vb1, w1, sems) = refs
    has_left, has_right = s_ref[2], s_ref[3]
    chips = rows // (2 * TILE_ROWS)
    me = lax.div(s_ref[4], TILE_ROWS)
    z, core = lax.div(me, 2), lax.rem(me, 2)

    def device(step, other):
        return 2 * lax.rem(z + step + chips, chips) + (1 - core if other else core)

    pieces = []
    for other, (w, a, b, c0, c1) in ((False, tiles[:5]), (True, tiles[5:])):
        for ref, step in ((w, 0), (a, -1), (b, 1)):
            for part in range(2):
                pieces.append((ref.at[part], device(step, other), part))
        pieces.append((c0, device(2, other), 0))
        pieces.append((c1, device(2, other), 1))
    copies = []
    for n, (ref, dev, part) in enumerate(pieces):
        row = TILE_ROWS * dev + 4 * part
        copies += [
            pltpu.make_async_copy(ref.at[pl.ds(0, 32)], own.at[pl.ds(8 * row, 32)], sems.at[3 * n]),
            pltpu.make_async_copy(
                ref.at[pl.ds(32, 32)], beside.at[pl.ds(8 * row, 32)], sems.at[3 * n + 1]),
            pltpu.make_async_copy(ref.at[64], heights.at[part, dev], sems.at[3 * n + 2]),
        ]
    for copy in copies:
        copy.start()
    for ref in (va0, vb0):
        zero_rim(ref, rows, 2)
    for ref in (va1, vb1):
        zero_rim(ref, rows // 2, 1)
    for copy in copies:
        copy.wait()

    edge = edge_mask(0, has_left, has_right)
    fine = Fine(source, weight, height)
    lane = lanes_iota((8, SUB, LANES))
    low = lane < 64

    def halves(own_value, beside_value, low):
        even = jnp.where(low, own_value, beside_value)
        odd = jnp.where(low, beside_value, own_value)
        return even, pltpu.roll(odd, 64, axis=odd.ndim - 1)

    def assemble(dev, carry):
        tall = halves(heights[0, dev], heights[1, dev], low[0])
        for r in range(TILE_ROWS):
            row = TILE_ROWS * dev + r
            place = pl.ds(8 * row, 8)
            both = halves(own[place], beside[place], low)
            for h in range(2):
                source[h, row] = both[h]
                height[h, row] = jnp.broadcast_to(tall[h][r:r + 1], (SUB, LANES))
                now = edge * jnp.where(
                    fine.ground(row, h), RELAX_WEIGHT / D_TERRAIN, RELAX_WEIGHT / D_AIR
                )
                weight[h, row] = now
                va0[h, row + 1] = now * both[h]
        return carry

    lax.fori_loop(0, rows // TILE_ROWS, assemble, 0)
    saves = [
        pltpu.make_async_copy(source, source_out, sems.at[1]),
        pltpu.make_async_copy(weight, weight_out, sems.at[2]),
        pltpu.make_async_copy(height, height_out, sems.at[3]),
    ]
    for save in saves:
        save.start()
    fine.coarse_shift(rows, sh1)
    fine.relax(va0, vb0, 0, rows, 8)
    fine.relax(vb0, va0, 0, rows, 8)
    fine.relax(va0, vb0, 0, rows, 8)
    saves.append(pltpu.make_async_copy(interior(vb0, rows), u0, sems.at[0]))
    saves[-1].start()
    fine.restricted_defect(vb0, rows, b1)
    level = Coarse(b1, w1, sh1, rows // 2, 16)
    level.set_weight(edge_mask(1, has_left, has_right))
    level_1_down(level, va1, vb1, packed)
    pack_level_2(level.shift_pairs(), packed, rows // 16)
    u1[...] = vb1[pl.ds(1, rows // 2)]
    for save in saves:
        save.wait()


def middle_kernel(rows, s_ref, source_in, weight_in, height_in, u0, u1, b1, sh1, own, right, left,
                  u0_out, u1_out, b1_out, packed,
                  source, weight, height, va0, vb0, va1, vb1, w1, va2, vb2, b2, sh2, w2, sems):
    has_left, has_right = s_ref[2], s_ref[3]
    copies = [
        pltpu.make_async_copy(u0, interior(va0, rows), sems.at[0]),
        pltpu.make_async_copy(source_in, source, sems.at[1]),
        pltpu.make_async_copy(weight_in, weight, sems.at[2]),
        pltpu.make_async_copy(height_in, height, sems.at[3]),
    ]
    for copy in copies:
        copy.start()
    for ref in (va1, vb1):
        zero_rim(ref, rows // 2, 1)
    e2 = coarse_part(own, right, left, own, right, left, has_left, has_right, rows // 4,
                     (va2, vb2, b2, sh2, w2))
    level = Coarse(b1, w1, sh1, rows // 2, 16)
    level.set_weight(edge_mask(1, has_left, has_right))
    level_1_up(level, e2, rows // 4, u1, va1, vb1)
    for ref in (va0, vb0):
        zero_rim(ref, rows, 2)
    for copy in copies:
        copy.wait()
    fine = Fine(source, weight, height)
    add_to_fine(va1, va0, 0, rows // 2)
    for _ in range(SWEEPS):
        fine.relax(va0, vb0, 0, rows, 8)
        fine.relax(vb0, va0, 0, rows, 8)
    save = pltpu.make_async_copy(interior(va0, rows), u0_out, sems.at[0])
    save.start()
    fine.restricted_defect(va0, rows, b1_out)
    level = Coarse(b1_out, w1, sh1, rows // 2, 16)
    level_1_down(level, va1, vb1, packed)
    u1_out[...] = vb1[pl.ds(1, rows // 2)]
    save.wait()


def last_kernel(rows, s_ref, source_in, weight_in, u0, u1, b1, sh1,
                own, right, left, own_s, right_s, left_s,
                out, source, weight, va0, vb0, va1, vb1, w1, va2, vb2, b2, sh2, w2, sems):
    start, has_left, has_right, mine = s_ref[1], s_ref[2], s_ref[3], s_ref[4]
    window = pl.ds(start, WINDOW)
    copies = [
        pltpu.make_async_copy(u0.at[:, window], interior(va0, WINDOW), sems.at[0]),
        pltpu.make_async_copy(source_in.at[:, window], source, sems.at[1]),
        pltpu.make_async_copy(weight_in.at[:, window], weight, sems.at[2]),
    ]
    for copy in copies:
        copy.start()
    for ref in (va1, vb1):
        zero_rim(ref, rows // 2, 1)
    e2 = coarse_part(own, right, left, own_s, right_s, left_s, has_left, has_right, rows // 4,
                     (va2, vb2, b2, sh2, w2))
    level = Coarse(b1, w1, sh1, rows // 2, 16)
    level.set_weight(edge_mask(1, has_left, has_right))
    level_1_up(level, e2, rows // 4, u1, va1, vb1)
    for ref in (va0, vb0):
        zero_rim(ref, WINDOW, 2)
    for copy in copies:
        copy.wait()
    fine = Fine(source, weight, None)
    add_to_fine(va1, va0, lax.div(start, 2), WINDOW // 2)
    src, dst = va0, vb0
    for k in range(SWEEPS):
        reach = SWEEPS - 1 - k
        count = TILE_ROWS + 2 * reach
        first = jnp.clip(mine - start - reach, 0, WINDOW - count)
        fine.relax(src, dst, first, count, count)
        src, dst = dst, src
    together = [
        matrix_of(lambda a, b, h=h: (a < 64) & (b == 2 * a + h)) for h in range(2)
    ]
    for r in range(TILE_ROWS):
        row = mine - start + r + 1
        value = 0.0
        for h in range(2):
            value = value + dot(src[h, row].reshape(8 * SUB, LANES), together[h])
        for zz in range(8):
            out[pl.ds(zz * TILE_ROWS + r, SUB, stride=8 * TILE_ROWS), :] = (
                value[SUB * zz:SUB * (zz + 1)]
            )


def spec(space=pltpu.VMEM):
    return pl.BlockSpec(memory_space=space)


def params():
    return pltpu.CompilerParams(vmem_limit_bytes=VMEM_LIMIT)


def shape(*dims):
    return jax.ShapeDtypeStruct(dims + (SUB, LANES), F32)


def vmem(*dims):
    return pltpu.VMEM(dims + (SUB, LANES), F32)


def level_1_scratch(rows):
    return [vmem(rows // 2 + 2, 4), vmem(rows // 2 + 2, 4), vmem(rows // 2, 4)]


def level_2_scratch(rows):
    return [vmem(rows // 4 + 2, 2)] * 2 + [vmem(rows // 4, 2)] * 3


def per_device(right_side, terrain):
    gx, gy = lax.axis_size("gx"), lax.axis_size("gy")
    rows = TILE_ROWS * gx
    i, j = lax.axis_index("gx"), lax.axis_index("gy")
    mine = TILE_ROWS * i
    start = jnp.clip(mine - 4, 0, rows - WINDOW)
    scalars = jnp.stack([
        jnp.int32(0), start, (j > 0).astype(jnp.int32), (j < gy - 1).astype(jnp.int32), mine
    ])
    rightward = [(k, k + 1) for k in range(gy - 1)]
    leftward = [(k + 1, k) for k in range(gy - 1)]

    def exchange(to_left, to_right):
        from_right = lax.ppermute(to_left, "gy", leftward)
        from_left = lax.ppermute(to_right, "gy", rightward)
        return from_right, from_left

    flat = LAYERS * TILE_ROWS
    blocks = TILE_ROWS * 8
    own, to_left, to_right = pl.pallas_call(
        pack_kernel,
        out_shape=(shape(blocks + 1), shape(blocks // 2 + 1), shape(blocks // 2 + 1)),
        in_specs=[spec()] * 2, out_specs=(spec(),) * 3, name="pack",
    )(right_side.reshape(flat, LANES), terrain.reshape(flat, LANES))
    from_right, from_left = exchange(to_left, to_right)
    tile = pl.pallas_call(
        merge_kernel, out_shape=shape(2, blocks + 1),
        in_specs=[spec()] * 3, out_specs=spec(), name="merge",
    )(own, from_right, from_left)

    up = [(k, (k + 2) % gx) for k in range(gx)]
    down = [(k, (k - 2) % gx) for k in range(gx)]
    swap = [(k, k ^ 1) for k in range(gx)]
    below = lax.ppermute(tile, "gx", up)
    above = lax.ppermute(tile, "gx", down)
    tile_s = lax.ppermute(tile, "gx", swap)
    far_0 = lax.ppermute(below[0], "gx", up)
    far_1 = lax.ppermute(above[1], "gx", down)
    below_s = lax.ppermute(below, "gx", swap)
    above_s = lax.ppermute(above, "gx", swap)
    far_0_s = lax.ppermute(far_0, "gx", swap)
    far_1_s = lax.ppermute(far_1, "gx", swap)
    tiles = (tile, below, above, far_0, far_1, tile_s, below_s, above_s, far_0_s, far_1_s)

    smem, hbm = spec(pltpu.SMEM), spec(pl.ANY)
    each = rows // 16
    level_0, level_1 = shape(2, rows, 8), shape(rows // 2, 4)
    fine_rows = [vmem(2, rows + 2, 8)] * 2
    u0, source, weight, height, u1, b1, sh1, packed = pl.pallas_call(
        lambda *refs: down_kernel(rows, *refs),
        out_shape=(level_0, level_0, level_0, shape(2, rows), level_1, level_1, level_1,
                   shape(2 * each, 2)),
        in_specs=[smem] + [hbm] * 10, out_specs=(hbm,) * 4 + (spec(),) * 4,
        scratch_shapes=[vmem(2, rows, 8), vmem(2, rows, 8), vmem(2, rows),
                        vmem(rows * 8), vmem(rows * 8), vmem(2, gx)]
        + fine_rows + level_1_scratch(rows) + [pltpu.SemaphoreType.DMA((48,))],
        compiler_params=params(), name="down",
    )(scalars, *tiles)

    right, left = exchange(packed, packed)
    u0, u1, b1, packed_2 = pl.pallas_call(
        lambda *refs: middle_kernel(rows, *refs),
        out_shape=(level_0, level_1, level_1, shape(each, 2)),
        in_specs=[smem] + [hbm] * 4 + [spec()] * 6, out_specs=(hbm,) + (spec(),) * 3,
        scratch_shapes=[vmem(2, rows, 8), vmem(2, rows, 8), vmem(2, rows)]
        + fine_rows + level_1_scratch(rows) + level_2_scratch(rows)
        + [pltpu.SemaphoreType.DMA((4,))],
        compiler_params=params(), name="middle",
    )(scalars, source, weight, height, u0, u1, b1, sh1, packed, right, left)

    right_2, left_2 = exchange(packed_2, packed_2)
    out = pl.pallas_call(
        lambda *refs: last_kernel(rows, *refs),
        out_shape=jax.ShapeDtypeStruct((flat, LANES), F32),
        in_specs=[smem] + [hbm] * 3 + [spec()] * 9, out_specs=spec(),
        scratch_shapes=[vmem(2, WINDOW, 8), vmem(2, WINDOW, 8)]
        + [vmem(2, WINDOW + 2, 8)] * 2 + level_1_scratch(rows) + level_2_scratch(rows)
        + [pltpu.SemaphoreType.DMA((3,))],
        compiler_params=params(), name="last",
    )(scalars, source, weight, u0, u1, b1, sh1,
      packed_2, right_2, left_2, packed, right, left)
    return out.reshape(LAYERS, TILE_ROWS, LANES)


def solution(mesh):
    in_specs = (P(None, "gx", "gy"), P(None, "gx", "gy"))
    out_specs = P(None, "gx", "gy")
    return jax.shard_map(
        per_device, mesh=mesh, in_specs=in_specs, out_specs=out_specs, check_vma=False
    )
```

time: 1380 us -> 120 us (0.09); the launches traced: 1360 us -> 118 us
  starting transfers between devices: 910 us -> 31.8 us
  waiting for transfers between devices: 287 us -> 29.5 us
  local copies, waits for them, and re-layouts: 112 us -> 3.33 us
  Pallas kernels: 0 us -> 53.4 us
  other arithmetic: 46.2 us -> 0 us
    ppermute x252 -> x15, starting transfers between devices: 910 us -> 31.8 us  [the longest x3 17.7 us: exchange(): from_right = lax.ppermute(to_left, 'gy', leftward)]
    ppermute x252 -> x15, waiting for transfers between devices: 287 us -> 29.5 us  [the longest x1 10.2 us: per_device(): above = lax.ppermute(tile, 'gx', down)]
    reshape x9 -> x0, local copies, waits for them, and re-layouts: 87.1 us -> none  [the longest x5 58.6 us: restrict(): values.reshape(layers_here // 2, 2, rows_here // 2, 2, cols_here // 2, 2)]
    pallas_call x0 -> x5, Pallas kernels: none -> 53.4 us  [the longest x1 25.6 us: per_device(): pl.pallas_call(lambda *refs: middle_kernel(rows, *refs), out_shape=(level...]
    reduce_sum x11 -> x0, other arithmetic: 22.1 us -> none  [restrict(): return 0.5 * blocks.sum(axis=(1, 3, 5))]
    add x66 -> x0, other arithmetic: 19.6 us -> none  [the longest x56 18 us: relax_once(): centre + RELAX_WEIGHT * (source - diagonal * centre + neighbor_sum) / dia...]
    broadcast_in_dim x8 -> x0, local copies, waits for them, and re-layouts: 13.8 us -> none  [prolong(): jnp.broadcast_to(values[:, None, :, None, :, None], (layers_here, 2, rows...]
  transfers between devices with their start and end apart: 252 -> 15, of which waited for: 156 -> 10; matrix products, arithmetic and copies ran while one was open for 2% -> 1% of each run, Pallas kernels for 0% -> 0%
where the time goes in v2:
time: 120 us; the launch traced here: 118 us
  Pallas kernels  53.4 us (44%)
  starting transfers between devices  31.8 us (26%)
  waiting for transfers between devices  29.5 us (25%)
  local copies, waits for them, and re-layouts  3.33 us (3%)
    pallas_call x1, Pallas kernels, per_device(): pl.pallas_call(lambda *refs: middle_kernel(rows, *refs), out_shape=(level...  25.6 us
    ppermute x3, starting transfers between devices, exchange(): from_right = lax.ppermute(to_left, 'gy', leftward)  17.7 us
    pallas_call x1, Pallas kernels, per_device(): pl.pallas_call(lambda *refs: down_kernel(rows, *refs), out_shape=(level_0...  15.3 us
    ppermute x1, waiting for transfers between devices, per_device(): above = lax.ppermute(tile, 'gx', down)  10.2 us
    pallas_call x1, Pallas kernels, per_device(): pl.pallas_call(lambda *refs: last_kernel(rows, *refs), out_shape=jax.Shap...  7.97 us
    ppermute x3, waiting for transfers between devices, exchange(): from_left = lax.ppermute(to_right, 'gy', rightward)  6.77 us
    ppermute x3, starting transfers between devices, exchange(): from_left = lax.ppermute(to_right, 'gy', rightward)  5.76 us
    ppermute x3, waiting for transfers between devices, exchange(): from_right = lax.ppermute(to_left, 'gy', leftward)  4.46 us
  transfers between devices with their start and end apart: 15, of which 10 were waited for; matrix products, arithmetic and copies ran while one was open for 1% of the time, Pallas kernels for 0%

profile of v2, /device:TPU:6, one launch (start us, length us, event | category | flops | bytes accessed | tf_op | source)
XLA Modules:
  0.0 118.4 jit_solution(7595757910204063236)
XLA Ops:
  0.0 2.5 %pack.1 = (f32[65,8,128]{2,1,0:T(8,128)}, f32[33,8,128]{2,1,0:T(8,128)}, f32[33,8,128]{2,1,0:T(8,128)}) custom-call(f32[512,128]{1,0:T(8,128)} %bitcast.11, s32[512,128]{1,0:T(8,128)} %bitcast.12), custom_call_target="tpu_custom_call" | custom-call | tf_op jit(solution)/shard_map/pack/pallas_call | solution.py:616
  2.5 5.2 %collective-permute-start = (f32[33,8,128]{2,1,0:T(8,128)}, f32[33,8,128]{2,1,0:T(8,128)S(1)}, u32[]{:S(2)}, u32[]{:S(2)}) collective-permute-start(f32[33,8,128]{2,1,0:T(8,128)} %get-tuple-element.21), channel_id=1, source_target_pairs={{1,0},{2,1},{3,2},{4,3},{5,4},{6,5},{7,6},{8,7},{9,8},{10,9},{11,1... | collective-permute-start | bytes 405512 | tf_op jit(solution)/shard_map/ppermute | solution.py:610
  7.7 1.9 %collective-permute-start.1 = (f32[33,8,128]{2,1,0:T(8,128)}, f32[33,8,128]{2,1,0:T(8,128)S(1)}, u32[]{:S(2)}, u32[]{:S(2)}) collective-permute-start(f32[33,8,128]{2,1,0:T(8,128)} %get-tuple-element.22), channel_id=1, source_target_pairs={{0,1},{1,2},{2,3},{3,4},{4,5},{5,6},{6,7},{7,8},{8,9},{9,10},{10,1... | collective-permute-start | bytes 405512 | tf_op jit(solution)/shard_map/ppermute | solution.py:611
  9.6 1.2 %collective-permute-done.from_right = f32[33,8,128]{2,1,0:T(8,128)S(1)} collective-permute-done((f32[33,8,128]{2,1,0:T(8,128)}, f32[33,8,128]{2,1,0:T(8,128)S(1)}, u32[]{:S(2)}, u32[]{:S(2)}) %collective-permute-start) | collective-permute-done | bytes 135200 | tf_op jit(solution)/shard_map/ppermute | solution.py:610
  10.8 6.1 %collective-permute-done.1.from_left = f32[33,8,128]{2,1,0:T(8,128)S(1)} collective-permute-done((f32[33,8,128]{2,1,0:T(8,128)}, f32[33,8,128]{2,1,0:T(8,128)S(1)}, u32[]{:S(2)}, u32[]{:S(2)}) %collective-permute-start.1) | collective-permute-done | bytes 135200 | tf_op jit(solution)/shard_map/ppermute | solution.py:611
  16.9 0.7 copy-done.11
  17.6 2.0 %merge.1.refs_1_ = f32[2,65,8,128]{3,2,1,0:T(8,128)} custom-call(f32[65,8,128]{2,1,0:T(8,128)} %get-tuple-element.20.own, f32[33,8,128]{2,1,0:T(8,128)} %copy-done.10, f32[33,8,128]{2,1,0:T(8,128)} %copy-done.11), custom_call_target="tpu_custom_call" | custom-call | tf_op jit(solution)/shard_map/merge/pallas_call | solution.py:622
  19.6 4.0 %collective-permute-start.3 = (f32[2,65,8,128]{3,2,1,0:T(8,128)}, f32[2,65,8,128]{3,2,1,0:T(8,128)S(1)}, u32[]{:S(2)}, u32[]{:S(2)}) collective-permute-start(f32[2,65,8,128]{3,2,1,0:T(8,128)} %merge.1.refs_1_), channel_id=1, source_target_pairs={{0,96},{16,112},{32,0},{48,16},{64,32},{80,48},{96,64},{112,80},{1... | collective-permute-start | bytes 1597448 | tf_op jit(solution)/shard_map/ppermute | solution.py:631
  23.7 10.2 %collective-permute-done.3.refs_3_ = f32[2,65,8,128]{3,2,1,0:T(8,128)S(1)} collective-permute-done((f32[2,65,8,128]{3,2,1,0:T(8,128)}, f32[2,65,8,128]{3,2,1,0:T(8,128)S(1)}, u32[]{:S(2)}, u32[]{:S(2)}) %collective-permute-start.3) | collective-permute-done | bytes 532512 | tf_op jit(solution)/shard_map/ppermute | solution.py:631
  33.9 3.7 %collective-permute-start.5 = (f32[65,8,128]{2,1,0:T(8,128)S(1)}, f32[65,8,128]{2,1,0:T(8,128)S(1)}, u32[]{:S(2)}, u32[]{:S(2)}) collective-permute-start(f32[65,8,128]{2,1,0:T(8,128)S(1)} %slice_bitcast_fusion), channel_id=1, source_target_pairs={{0,96},{16,112},{32,0},{48,16},{64,32},{80,48},{96,64},{112,80},{1... | collective-permute-start | bytes 798728 | tf_op jit(solution)/shard_map/ppermute | solution.py:634
  38.3 3.2 %collective-permute-done.5.refs_5_ = f32[65,8,128]{2,1,0:T(8,128)S(1)} collective-permute-done((f32[65,8,128]{2,1,0:T(8,128)S(1)}, f32[65,8,128]{2,1,0:T(8,128)S(1)}, u32[]{:S(2)}, u32[]{:S(2)}) %collective-permute-start.5) | collective-permute-done | bytes 266272 | tf_op jit(solution)/shard_map/ppermute | solution.py:634
  41.5 3.8 %collective-permute-done.4.refs_4_ = f32[65,8,128]{2,1,0:T(8,128)S(1)} collective-permute-done((f32[65,8,128]{2,1,0:T(8,128)S(1)}, f32[65,8,128]{2,1,0:T(8,128)S(1)}, u32[]{:S(2)}, u32[]{:S(2)}) %collective-permute-start.4) | collective-permute-done | bytes 266272 | tf_op jit(solution)/shard_map/ppermute | solution.py:633
  45.9 1.0 collective-permute-done.9.refs_9_
  47.0 0.8 copy-done.4
  47.8 15.3 %down.1 = (f32[2,64,8,8,128]{4,3,2,1,0:T(8,128)}, f32[2,64,8,8,128]{4,3,2,1,0:T(8,128)}, f32[2,64,8,8,128]{4,3,2,1,0:T(8,128)}, f32[2,64,8,128]{3,2,1,0:T(8,128)...) custom-call(s32[5]{0:T(128)} %stack.27.refs_0_, ...), custom_call_target="tpu_custom_call" | custom-call | tf_op jit(solution)/shard_map/down/pallas_call | solution.py:645
  63.2 1.9 %collective-permute-start.12 = (f32[8,2,8,128]{3,2,1,0:T(8,128)}, f32[8,2,8,128]{3,2,1,0:T(8,128)S(1)}, u32[]{:S(2)}, u32[]{:S(2)}) collective-permute-start(f32[8,2,8,128]{3,2,1,0:T(8,128)} %get-tuple-element.30.refs_8_.refs_10_), channel_id=1, source_target_pairs={{0,1},{1,2},{2,3},{3,4},{4,5},{5,6},{6,7},{7,8},{8,9},{9,10},{10,1... | collective-permute-start | bytes 196616 | tf_op jit(solution)/shard_map/ppermute | solution.py:611
  65.1 6.2 %collective-permute-start.11 = (f32[8,2,8,128]{3,2,1,0:T(8,128)}, f32[8,2,8,128]{3,2,1,0:T(8,128)S(1)}, u32[]{:S(2)}, u32[]{:S(2)}) collective-permute-start(f32[8,2,8,128]{3,2,1,0:T(8,128)} %get-tuple-element.30.refs_8_.refs_10_), channel_id=1, source_target_pairs={{1,0},{2,1},{3,2},{4,3},{5,4},{6,5},{7,6},{8,7},{9,8},{10,9},{11,1... | collective-permute-start | bytes 196616 | tf_op jit(solution)/shard_map/ppermute | solution.py:610
  71.8 1.5 %collective-permute-done.11.refs_9_.refs_11_ = f32[8,2,8,128]{3,2,1,0:T(8,128)S(1)} collective-permute-done((f32[8,2,8,128]{3,2,1,0:T(8,128)}, f32[8,2,8,128]{3,2,1,0:T(8,128)S(1)}, u32[]{:S(2)}, u32[]{:S(2)}) %collective-permute-start.11) | collective-permute-done | bytes 65568 | tf_op jit(solution)/shard_map/ppermute | solution.py:610
  73.3 0.6 copy-done.9
  73.9 25.6 %middle.1 = (f32[2,64,8,8,128]{4,3,2,1,0:T(8,128)}, f32[32,4,8,128]{3,2,1,0:T(8,128)}, f32[32,4,8,128]{3,2,1,0:T(8,128)}, f32[4,2,8,128]{3,2,1,0:T(8,128)}) custom-call(s32[5]{0:T(128)} %stack.27.refs_0_, f32[2,64,8,8,128]{4,3,2,1,0:T(8,128)} %get-tuple-element.23.refs_1_, f32[2,64,8,8,128]{4,3,2,1,0:T(8,128)} %get-tuple-element.24.refs_2_, ...), custom_call_target="tpu_custom_call" | custom-call | tf_op jit(solution)/shard_map/middle/pallas_call | solution.py:657
  99.6 1.9 %collective-permute-start.14 = (f32[4,2,8,128]{3,2,1,0:T(8,128)}, f32[4,2,8,128]{3,2,1,0:T(8,128)S(1)}, u32[]{:S(2)}, u32[]{:S(2)}) collective-permute-start(f32[4,2,8,128]{3,2,1,0:T(8,128)} %get-tuple-element.34.refs_7_), channel_id=1, source_target_pairs={{0,1},{1,2},{2,3},{3,4},{4,5},{5,6},{6,7},{7,8},{8,9},{9,10},{10,1... | collective-permute-start | bytes 98312 | tf_op jit(solution)/shard_map/ppermute | solution.py:611
  101.5 6.3 %collective-permute-start.13 = (f32[4,2,8,128]{3,2,1,0:T(8,128)}, f32[4,2,8,128]{3,2,1,0:T(8,128)S(1)}, u32[]{:S(2)}, u32[]{:S(2)}) collective-permute-start(f32[4,2,8,128]{3,2,1,0:T(8,128)} %get-tuple-element.34.refs_7_), channel_id=1, source_target_pairs={{1,0},{2,1},{3,2},{4,3},{5,4},{6,5},{7,6},{8,7},{9,8},{10,9},{11,1... | collective-permute-start | bytes 98312 | tf_op jit(solution)/shard_map/ppermute | solution.py:610
  107.9 1.7 %collective-permute-done.13.refs_8_ = f32[4,2,8,128]{3,2,1,0:T(8,128)S(1)} collective-permute-done((f32[4,2,8,128]{3,2,1,0:T(8,128)}, f32[4,2,8,128]{3,2,1,0:T(8,128)S(1)}, u32[]{:S(2)}, u32[]{:S(2)}) %collective-permute-start.13) | collective-permute-done | bytes 32800 | tf_op jit(solution)/shard_map/ppermute | solution.py:610
  110.3 8.0 %last.1 = f32[512,128]{1,0:T(8,128)} custom-call(s32[5]{0:T(128)} %stack.27.refs_0_, f32[2,64,8,8,128]{4,3,2,1,0:T(8,128)} %get-tuple-element.23.refs_1_, f32[2,64,8,8,128]{4,3,2,1,0:T(8,128)} %get-tuple-element.24.refs_2_, f32[2,64,8,8,128]{4,3,2,1,0:T(8,128)} %get-tuple-element.31.refs_3_, f32[32,4,8,128]{3,2,1,0:T(8,128)} %get-tuple-element.32.refs_4_, ...), custom_call_target="tpu_custom_call" | custom-call | tf_op jit(solution)/shard_map/last/pallas_call | solution.py:668
  (42 shorter events, 2.6 us)
Async XLA Ops:
  2.5 8.3 %collective-permute-start = (f32[33,8,128]{2,1,0:T(8,128)}, f32[33,8,128]{2,1,0:T(8,128)S(1)}, u32[]{:S(2)}, u32[]{:S(2)}) collective-permute-start(f32[33,8,128]{2,1,0:T(8,128)} %get-tuple-element.21), channel_id=1, source_target_pairs={{1,0},{2,1},{3,2},{4,3},{5,4},{6,5},{7,6},{8,7},{9,8},{10,9},{11,1... | collective-permute-start | bytes 405512 | tf_op jit(solution)/shard_map/ppermute | solution.py:610
  7.7 9.3 %collective-permute-start.1 = (f32[33,8,128]{2,1,0:T(8,128)}, f32[33,8,128]{2,1,0:T(8,128)S(1)}, u32[]{:S(2)}, u32[]{:S(2)}) collective-permute-start(f32[33,8,128]{2,1,0:T(8,128)} %get-tuple-element.22), channel_id=1, source_target_pairs={{0,1},{1,2},{2,3},{3,4},{4,5},{5,6},{6,7},{7,8},{8,9},{9,10},{10,1... | collective-permute-start | bytes 405512 | tf_op jit(solution)/shard_map/ppermute | solution.py:611
  10.8 6.1 %copy-start.10 = (f32[33,8,128]{2,1,0:T(8,128)}, f32[33,8,128]{2,1,0:T(8,128)S(1)}, u32[]{:S(2)}) copy-start(f32[33,8,128]{2,1,0:T(8,128)S(1)} %collective-permute-done.from_right) | copy-start | bytes 405508
  19.6 14.2 %collective-permute-start.3 = (f32[2,65,8,128]{3,2,1,0:T(8,128)}, f32[2,65,8,128]{3,2,1,0:T(8,128)S(1)}, u32[]{:S(2)}, u32[]{:S(2)}) collective-permute-start(f32[2,65,8,128]{3,2,1,0:T(8,128)} %merge.1.refs_1_), channel_id=1, source_target_pairs={{0,96},{16,112},{32,0},{48,16},{64,32},{80,48},{96,64},{112,80},{1... | collective-permute-start | bytes 1597448 | tf_op jit(solution)/shard_map/ppermute | solution.py:631
  23.7 13.9 %collective-permute-start.2 = (f32[2,65,8,128]{3,2,1,0:T(8,128)}, f32[2,65,8,128]{3,2,1,0:T(8,128)S(1)}, u32[]{:S(2)}, u32[]{:S(2)}) collective-permute-start(f32[2,65,8,128]{3,2,1,0:T(8,128)} %merge.1.refs_1_), channel_id=1, source_target_pairs={{0,32},{16,48},{32,64},{48,80},{64,96},{80,112},{96,0},{112,16},{1... | collective-permute-start | bytes 1597448 | tf_op jit(solution)/shard_map/ppermute | solution.py:630
  23.7 22.2 %collective-permute-start.6 = (f32[2,65,8,128]{3,2,1,0:T(8,128)}, f32[2,65,8,128]{3,2,1,0:T(8,128)S(1)}, u32[]{:S(2)}, u32[]{:S(2)}) collective-permute-start(f32[2,65,8,128]{3,2,1,0:T(8,128)} %merge.1.refs_1_), channel_id=1, source_target_pairs={{0,16},{16,0},{32,48},{48,32},{64,80},{80,64},{96,112},{112,96},{1... | collective-permute-start | bytes 1597448 | tf_op jit(solution)/shard_map/ppermute | solution.py:632
  33.9 13.1 %copy-start = (f32[2,65,8,128]{3,2,1,0:T(8,128)}, f32[2,65,8,128]{3,2,1,0:T(8,128)S(1)}, u32[]{:S(2)}) copy-start(f32[2,65,8,128]{3,2,1,0:T(8,128)S(1)} %collective-permute-done.3.refs_3_) | copy-start | bytes 1597444
  33.9 7.6 %collective-permute-start.5 = (f32[65,8,128]{2,1,0:T(8,128)S(1)}, f32[65,8,128]{2,1,0:T(8,128)S(1)}, u32[]{:S(2)}, u32[]{:S(2)}) collective-permute-start(f32[65,8,128]{2,1,0:T(8,128)S(1)} %slice_bitcast_fusion), channel_id=1, source_target_pairs={{0,96},{16,112},{32,0},{48,16},{64,32},{80,48},{96,64},{112,80},{1... | collective-permute-start | bytes 798728 | tf_op jit(solution)/shard_map/ppermute | solution.py:634
  37.6 9.4 %copy-start.1 = (f32[2,65,8,128]{3,2,1,0:T(8,128)}, f32[2,65,8,128]{3,2,1,0:T(8,128)S(1)}, u32[]{:S(2)}) copy-start(f32[2,65,8,128]{3,2,1,0:T(8,128)S(1)} %collective-permute-done.2.refs_2_) | copy-start | bytes 1597444
  37.6 7.7 %collective-permute-start.4 = (f32[65,8,128]{2,1,0:T(8,128)S(1)}, f32[65,8,128]{2,1,0:T(8,128)S(1)}, u32[]{:S(2)}, u32[]{:S(2)}) collective-permute-start(f32[65,8,128]{2,1,0:T(8,128)S(1)} %slice_bitcast_fusion.1), channel_id=1, source_target_pairs={{0,32},{16,48},{32,64},{48,80},{64,96},{80,112},{96,0},{112,16},{1... | collective-permute-start | bytes 798728 | tf_op jit(solution)/shard_map/ppermute | solution.py:633
  37.7 8.2 %collective-permute-start.8 = (f32[2,65,8,128]{3,2,1,0:T(8,128)S(1)}, f32[2,65,8,128]{3,2,1,0:T(8,128)S(1)}, u32[]{:S(2)}, u32[]{:S(2)}) collective-permute-start(f32[2,65,8,128]{3,2,1,0:T(8,128)S(1)} %collective-permute-done.3.refs_3_), channel_id=1, source_target_pairs={{0,16},{16,0},{32,48},{48,32},{64,80},{80,64},{96,112},{112,96},{1... | collective-permute-start | bytes 1597448 | tf_op jit(solution)/shard_map/ppermute | solution.py:636
  37.8 9.2 %collective-permute-start.7 = (f32[2,65,8,128]{3,2,1,0:T(8,128)S(1)}, f32[2,65,8,128]{3,2,1,0:T(8,128)S(1)}, u32[]{:S(2)}, u32[]{:S(2)}) collective-permute-start(f32[2,65,8,128]{3,2,1,0:T(8,128)S(1)} %collective-permute-done.2.refs_2_), channel_id=1, source_target_pairs={{0,16},{16,0},{32,48},{48,32},{64,80},{80,64},{96,112},{112,96},{1... | collective-permute-start | bytes 1597448 | tf_op jit(solution)/shard_map/ppermute | solution.py:635
  41.5 5.5 %copy-start.5 = (f32[65,8,128]{2,1,0:T(8,128)}, f32[65,8,128]{2,1,0:T(8,128)S(1)}, u32[]{:S(2)}) copy-start(f32[65,8,128]{2,1,0:T(8,128)S(1)} %collective-permute-done.5.refs_5_) | copy-start | bytes 798724
  41.5 4.4 %collective-permute-start.10 = (f32[65,8,128]{2,1,0:T(8,128)S(1)}, f32[65,8,128]{2,1,0:T(8,128)S(1)}, u32[]{:S(2)}, u32[]{:S(2)}) collective-permute-start(f32[65,8,128]{2,1,0:T(8,128)S(1)} %collective-permute-done.5.refs_5_), channel_id=1, source_target_pairs={{0,16},{16,0},{32,48},{48,32},{64,80},{80,64},{96,112},{112,96},{1... | collective-permute-start | bytes 798728 | tf_op jit(solution)/shard_map/ppermute | solution.py:638
  45.3 1.7 %copy-start.6 = (f32[65,8,128]{2,1,0:T(8,128)}, f32[65,8,128]{2,1,0:T(8,128)S(1)}, u32[]{:S(2)}) copy-start(f32[65,8,128]{2,1,0:T(8,128)S(1)} %collective-permute-done.4.refs_4_) | copy-start | bytes 798724
  45.3 1.7 %collective-permute-start.9 = (f32[65,8,128]{2,1,0:T(8,128)S(1)}, f32[65,8,128]{2,1,0:T(8,128)}, u32[]{:S(2)}, u32[]{:S(2)}) collective-permute-start(f32[65,8,128]{2,1,0:T(8,128)S(1)} %collective-permute-done.4.refs_4_), channel_id=1, source_target_pairs={{0,16},{16,0},{32,48},{48,32},{64,80},{80,64},{96,112},{112,96},{1... | collective-permute-start | bytes 798728 | tf_op jit(solution)/shard_map/ppermute | solution.py:637
  45.9 1.1 copy-start.2
  45.9 1.1 copy-start.7
  63.2 8.6 %collective-permute-start.12 = (f32[8,2,8,128]{3,2,1,0:T(8,128)}, f32[8,2,8,128]{3,2,1,0:T(8,128)S(1)}, u32[]{:S(2)}, u32[]{:S(2)}) collective-permute-start(f32[8,2,8,128]{3,2,1,0:T(8,128)} %get-tuple-element.30.refs_8_.refs_10_), channel_id=1, source_target_pairs={{0,1},{1,2},{2,3},{3,4},{4,5},{5,6},{6,7},{7,8},{8,9},{9,10},{10,1... | collective-permute-start | bytes 196616 | tf_op jit(solution)/shard_map/ppermute | solution.py:611
  65.1 8.2 %collective-permute-start.11 = (f32[8,2,8,128]{3,2,1,0:T(8,128)}, f32[8,2,8,128]{3,2,1,0:T(8,128)S(1)}, u32[]{:S(2)}, u32[]{:S(2)}) collective-permute-start(f32[8,2,8,128]{3,2,1,0:T(8,128)} %get-tuple-element.30.refs_8_.refs_10_), channel_id=1, source_target_pairs={{1,0},{2,1},{3,2},{4,3},{5,4},{6,5},{7,6},{8,7},{9,8},{10,9},{11,1... | collective-permute-start | bytes 196616 | tf_op jit(solution)/shard_map/ppermute | solution.py:610
  71.8 1.5 %copy-start.8 = (f32[8,2,8,128]{3,2,1,0:T(8,128)}, f32[8,2,8,128]{3,2,1,0:T(8,128)S(1)}, u32[]{:S(2)}) copy-start(f32[8,2,8,128]{3,2,1,0:T(8,128)S(1)} %collective-permute-done.12.refs_10_.refs_12_) | copy-start | bytes 196612
  99.6 8.4 %collective-permute-start.14 = (f32[4,2,8,128]{3,2,1,0:T(8,128)}, f32[4,2,8,128]{3,2,1,0:T(8,128)S(1)}, u32[]{:S(2)}, u32[]{:S(2)}) collective-permute-start(f32[4,2,8,128]{3,2,1,0:T(8,128)} %get-tuple-element.34.refs_7_), channel_id=1, source_target_pairs={{0,1},{1,2},{2,3},{3,4},{4,5},{5,6},{6,7},{7,8},{8,9},{9,10},{10,1... | collective-permute-start | bytes 98312 | tf_op jit(solution)/shard_map/ppermute | solution.py:611
  101.5 8.2 %collective-permute-start.13 = (f32[4,2,8,128]{3,2,1,0:T(8,128)}, f32[4,2,8,128]{3,2,1,0:T(8,128)S(1)}, u32[]{:S(2)}, u32[]{:S(2)}) collective-permute-start(f32[4,2,8,128]{3,2,1,0:T(8,128)} %get-tuple-element.34.refs_7_), channel_id=1, source_target_pairs={{1,0},{2,1},{3,2},{4,3},{5,4},{6,5},{7,6},{8,7},{9,8},{10,9},{11,1... | collective-permute-start | bytes 98312 | tf_op jit(solution)/shard_map/ppermute | solution.py:610
  107.9 1.7 %copy-start.12 = (f32[4,2,8,128]{3,2,1,0:T(8,128)}, f32[4,2,8,128]{3,2,1,0:T(8,128)S(1)}, u32[]{:S(2)}) copy-start(f32[4,2,8,128]{3,2,1,0:T(8,128)S(1)} %collective-permute-done.14.refs_9_) | copy-start | bytes 98308
  (5 other events, 3.8 us)

commit v3 on v2

--- a/solution.py
+++ b/solution.py
@@ -74,18 +74,16 @@
 
 
 def stencil_group(load, first, count, emit):
-    held = [load(first + k - 1) for k in range(count + 2)]
-    stores = []
+    before, centre = load(first - 1), load(first)
     for k in range(count):
-        centre = held[k + 1]
+        after = load(first + k + 1)
         sides = column_sum(centre)
         pairs = []
         for h, v in enumerate(centre):
-            total = held[k][h] + held[k + 2][h]
+            total = before[h] + after[h]
             pairs.append((v, total + layer_sum(v) + sides[h]))
-        stores.append(emit(first + k, pairs))
-    for store in stores:
-        store()
+        emit(first + k, pairs)
+        before, centre = centre, after
 
 
 def over_rows(start, rows, group, body):
@@ -117,16 +115,9 @@
 
     def relax(self, src, dst, start, rows, group):
         def emit(row, pairs):
-            new = [
-                (1.0 - RELAX_WEIGHT) * v + self.weight[h, row] * (total + self.source[h, row])
-                for h, (v, total) in enumerate(pairs)
-            ]
-
-            def store():
-                for h in range(2):
-                    dst[h, row + 1] = new[h]
-
-            return store
+            for h, (v, total) in enumerate(pairs):
+                total = total + self.source[h, row]
+                dst[h, row + 1] = (1.0 - RELAX_WEIGHT) * v + self.weight[h, row] * total
 
         over_rows(start, rows, group,
                   lambda first, count: stencil_group(self.loader(src), first, count, emit))
@@ -143,7 +134,6 @@
                     diagonal = jnp.where(self.ground(row, h), D_TERRAIN, D_AIR)
                     total = total + (self.source[h, row] + near - diagonal * v)
                 sums.append(total)
-                return lambda: None
 
             stencil_group(load, first, count, emit)
             for k in range(count // 2):
@@ -193,12 +183,8 @@
     def relax(self, src, dst):
         def emit(row, pairs):
             v, total = pairs[0]
-            new = (1.0 - RELAX_WEIGHT) * v + self.weight[row] * (total + self.source[row])
-
-            def store():
-                dst[row + 1] = new
-
-            return store
+            total = total + self.source[row]
+            dst[row + 1] = (1.0 - RELAX_WEIGHT) * v + self.weight[row] * total
 
         load = lambda row: [src[row + 1]]
         over_rows(0, self.rows, self.group,
@@ -210,7 +196,6 @@
         def emit(row, pairs):
             v, total = pairs[0]
             sums.append(self.source[row] + total - (6.0 + self.shift_now[row]) * v)
-            return lambda: None
 
         stencil_group(lambda row: [src[row + 1]], 0, self.rows, emit)
         return pair_up(sums)
@@ -238,12 +223,14 @@
     out[pl.ds(offset, count)] = total
 
 
-def unpack_level_2(own, right, left, offset, each, out):
+def unpack_level_2(own, first, second, even, offset, each, out):
     lane = lanes_iota((each, 2, SUB, LANES))
+    held = [ref[pl.ds(offset, each)] for ref in (own, first, second)]
+    left = jnp.where(even, held[1], held[2])
+    right = jnp.where(even, held[2], held[1])
     for g in range(4):
         parts = []
-        for ref, place in ((own, 0), (right, 32), (left, 96)):
-            value = ref[pl.ds(offset, each)]
+        for value, place in ((held[0], 0), (right, 32), (left, 96)):
             amount = (place - 32 * g) % LANES
             parts.append(pltpu.roll(value, amount, axis=3) if amount else value)
         out[pl.ds(g * each, each)] = jnp.where(
@@ -289,11 +276,12 @@
     pack_level_2(level.defect_pairs(vb), packed, 0)
 
 
-def coarse_part(own, right, left, own_s, right_s, left_s, has_left, has_right, rows2, refs):
+def coarse_part(tiles, shift_tiles, s_ref, rows2, refs):
     va, vb, b2, sh2, w2 = refs
+    has_left, has_right, even = s_ref[2], s_ref[3], s_ref[5] == 1
     each = rows2 // 4
-    unpack_level_2(own, right, left, 0, each, b2)
-    unpack_level_2(own_s, right_s, left_s, each, each, sh2)
+    unpack_level_2(*tiles, even, 0, each, b2)
+    unpack_level_2(*shift_tiles, even, each, each, sh2)
     for ref in (va, vb):
         zero_rim(ref, rows2, 1)
     level = Coarse(b2, w2, sh2, rows2, rows2)
@@ -363,45 +351,35 @@
     return lax.rem(lax.div(lanes_iota(shape), 32), 2) == 0
 
 
-def pack_kernel(right_side, terrain, own, to_left, to_right):
+def pack_kernel(s_ref, right_side, terrain, own, first_out, second_out):
+    even = s_ref[5] == 1
     apart = matrix_of(lambda a, b: b == lax.div(a, 2) + 64 * lax.rem(a, 2))
     heights = terrain[pl.ds(0, TILE_ROWS), :]
     for z in range(1, 32):
         heights = heights + terrain[pl.ds(TILE_ROWS * z, TILE_ROWS), :]
     heights = dot(heights.astype(F32), apart)
-    own[64] = heights
+    own[0, 32] = heights
+    own[1, 32] = heights
     heights = pltpu.roll(heights, 64, axis=1)
-    to_left[32] = heights
-    to_right[32] = heights
+    first_out[32] = heights
+    second_out[32] = heights
     first = first_columns((4, SUB, LANES))
     for r in range(TILE_ROWS):
         layers = [
             right_side[pl.ds(zz * TILE_ROWS + r, SUB, stride=8 * TILE_ROWS), :] for zz in range(8)
         ]
         value = dot(jnp.concatenate(layers, axis=0), apart).reshape(8, SUB, LANES)
-        own[pl.ds(8 * r, 8)] = value
+        own[r // 4, pl.ds(8 * (r % 4), 8)] = value
         value = pltpu.roll(value, 64, axis=2)
         low, high = value[:4], value[4:]
-        to_left[pl.ds(4 * r, 4)] = jnp.where(first, low, pltpu.roll(high, 32, axis=2))
-        to_right[pl.ds(4 * r, 4)] = jnp.where(first, pltpu.roll(high, 96, axis=2), low)
-
-
-def merge_kernel(own, from_right, from_left, out):
-    first = first_columns((4, SUB, LANES))
-    for r in range(TILE_ROWS):
-        part, place = r // 4, 8 * (r % 4)
-        out[part, pl.ds(place, 8)] = own[pl.ds(8 * r, 8)]
-        right, left = from_right[pl.ds(4 * r, 4)], from_left[pl.ds(4 * r, 4)]
-        out[part, pl.ds(32 + place, 4)] = jnp.where(first, right, left)
-        out[part, pl.ds(32 + place + 4, 4)] = jnp.where(
-            first, pltpu.roll(right, 96, axis=2), pltpu.roll(left, 32, axis=2)
-        )
-    out[0, 64] = own[64]
-    out[1, 64] = jnp.where(first[0], from_right[32], from_left[32])
+        to_left = jnp.where(first, low, pltpu.roll(high, 32, axis=2))
+        to_right = jnp.where(first, pltpu.roll(high, 96, axis=2), low)
+        first_out[pl.ds(4 * r, 4)] = jnp.where(even, to_left, to_right)
+        second_out[pl.ds(4 * r, 4)] = jnp.where(even, to_right, to_left)
 
 
 def down_kernel(rows, s_ref, *refs):
-    tiles, refs = refs[:10], refs[10:]
+    tiles, refs = refs[:20], refs[20:]
     (u0, source_out, weight_out, height_out, u1, b1, sh1, packed,
      source, weight, height, own, beside, heights, va0, vb0, va1, vb1, w1, sems) = refs
     has_left, has_right = s_ref[2], s_ref[3]
@@ -412,22 +390,22 @@
     def device(step, other):
         return 2 * lax.rem(z + step + chips, chips) + (1 - core if other else core)
 
-    pieces = []
-    for other, (w, a, b, c0, c1) in ((False, tiles[:5]), (True, tiles[5:])):
-        for ref, step in ((w, 0), (a, -1), (b, 1)):
-            for part in range(2):
-                pieces.append((ref.at[part], device(step, other), part))
-        pieces.append((c0, device(2, other), 0))
-        pieces.append((c1, device(2, other), 1))
     copies = []
-    for n, (ref, dev, part) in enumerate(pieces):
-        row = TILE_ROWS * dev + 4 * part
-        copies += [
-            pltpu.make_async_copy(ref.at[pl.ds(0, 32)], own.at[pl.ds(8 * row, 32)], sems.at[3 * n]),
-            pltpu.make_async_copy(
-                ref.at[pl.ds(32, 32)], beside.at[pl.ds(8 * row, 32)], sems.at[3 * n + 1]),
-            pltpu.make_async_copy(ref.at[64], heights.at[part, dev], sems.at[3 * n + 2]),
-        ]
+
+    def start_copy(source_ref, target_ref):
+        copies.append(pltpu.make_async_copy(source_ref, target_ref, sems.at[len(copies)]))
+
+    for kind in range(2):
+        for other in range(2):
+            w, a, b, c0, c1 = tiles[10 * kind + 5 * other:10 * kind + 5 * other + 5]
+            pieces = [(ref.at[part], device(step, other), part)
+                      for ref, step in ((w, 0), (a, -1), (b, 1)) for part in range(2)]
+            pieces += [(c0, device(2, other), 0), (c1, device(2, other), 1)]
+            for ref, dev, part in pieces:
+                target = own.at[2 * dev + part] if kind == 0 else beside.at[part, dev]
+                start_copy(ref.at[pl.ds(0, 32)], target)
+                if part == 0:
+                    start_copy(ref.at[32], heights.at[kind, dev])
     for copy in copies:
         copy.start()
     for ref in (va0, vb0):
@@ -447,12 +425,16 @@
         odd = jnp.where(low, beside_value, own_value)
         return even, pltpu.roll(odd, 64, axis=odd.ndim - 1)
 
+    first = first_columns((4, SUB, LANES))
+
     def assemble(dev, carry):
         tall = halves(heights[0, dev], heights[1, dev], low[0])
         for r in range(TILE_ROWS):
             row = TILE_ROWS * dev + r
-            place = pl.ds(8 * row, 8)
-            both = halves(own[place], beside[place], low)
+            upper = beside[1, dev, pl.ds(4 * r, 4)]
+            upper = jnp.where(first, pltpu.roll(upper, 96, axis=2), pltpu.roll(upper, 32, axis=2))
+            side = jnp.concatenate([beside[0, dev, pl.ds(4 * r, 4)], upper], axis=0)
+            both = halves(own[2 * dev + r // 4, pl.ds(8 * (r % 4), 8)], side, low)
             for h in range(2):
                 source[h, row] = both[h]
                 height[h, row] = jnp.broadcast_to(tall[h][r:r + 1], (SUB, LANES))
@@ -472,9 +454,9 @@
     for save in saves:
         save.start()
     fine.coarse_shift(rows, sh1)
-    fine.relax(va0, vb0, 0, rows, 8)
-    fine.relax(vb0, va0, 0, rows, 8)
-    fine.relax(va0, vb0, 0, rows, 8)
+    fine.relax(va0, vb0, 0, rows, 16)
+    fine.relax(vb0, va0, 0, rows, 16)
+    fine.relax(va0, vb0, 0, rows, 16)
     saves.append(pltpu.make_async_copy(interior(vb0, rows), u0, sems.at[0]))
     saves[-1].start()
     fine.restricted_defect(vb0, rows, b1)
@@ -487,7 +469,7 @@
         save.wait()
 
 
-def middle_kernel(rows, s_ref, source_in, weight_in, height_in, u0, u1, b1, sh1, own, right, left,
+def middle_kernel(rows, s_ref, source_in, weight_in, height_in, u0, u1, b1, sh1, own, second, first,
                   u0_out, u1_out, b1_out, packed,
                   source, weight, height, va0, vb0, va1, vb1, w1, va2, vb2, b2, sh2, w2, sems):
     has_left, has_right = s_ref[2], s_ref[3]
@@ -501,7 +483,7 @@
         copy.start()
     for ref in (va1, vb1):
         zero_rim(ref, rows // 2, 1)
-    e2 = coarse_part(own, right, left, own, right, left, has_left, has_right, rows // 4,
+    e2 = coarse_part((own, first, second), (own, first, second), s_ref, rows // 4,
                      (va2, vb2, b2, sh2, w2))
     level = Coarse(b1, w1, sh1, rows // 2, 16)
     level.set_weight(edge_mask(1, has_left, has_right))
@@ -525,7 +507,7 @@
 
 
 def last_kernel(rows, s_ref, source_in, weight_in, u0, u1, b1, sh1,
-                own, right, left, own_s, right_s, left_s,
+                own, second, first, own_s, second_s, first_s,
                 out, source, weight, va0, vb0, va1, vb1, w1, va2, vb2, b2, sh2, w2, sems):
     start, has_left, has_right, mine = s_ref[1], s_ref[2], s_ref[3], s_ref[4]
     window = pl.ds(start, WINDOW)
@@ -538,7 +520,7 @@
         copy.start()
     for ref in (va1, vb1):
         zero_rim(ref, rows // 2, 1)
-    e2 = coarse_part(own, right, left, own_s, right_s, left_s, has_left, has_right, rows // 4,
+    e2 = coarse_part((own, first, second), (own_s, first_s, second_s), s_ref, rows // 4,
                      (va2, vb2, b2, sh2, w2))
     level = Coarse(b1, w1, sh1, rows // 2, 16)
     level.set_weight(edge_mask(1, has_left, has_right))
@@ -600,45 +582,49 @@
     i, j = lax.axis_index("gx"), lax.axis_index("gy")
     mine = TILE_ROWS * i
     start = jnp.clip(mine - 4, 0, rows - WINDOW)
+    even = 1 - lax.rem(j, 2)
     scalars = jnp.stack([
-        jnp.int32(0), start, (j > 0).astype(jnp.int32), (j < gy - 1).astype(jnp.int32), mine
+        jnp.int32(0), start, (j > 0).astype(jnp.int32), (j < gy - 1).astype(jnp.int32), mine, even
     ])
-    rightward = [(k, k + 1) for k in range(gy - 1)]
-    leftward = [(k + 1, k) for k in range(gy - 1)]
-
-    def exchange(to_left, to_right):
-        from_right = lax.ppermute(to_left, "gy", leftward)
-        from_left = lax.ppermute(to_right, "gy", rightward)
-        return from_right, from_left
-
+
+    def swaps(begin):
+        pairs = [(k, k + 1) for k in range(begin, gy - 1, 2)]
+        return pairs + [(b, a) for a, b in pairs]
+
+    def exchange(first_out, second_out):
+        first = lax.ppermute(first_out, "gy", swaps(1))
+        second = lax.ppermute(second_out, "gy", swaps(0))
+        return first, second
+
+    smem, hbm = spec(pltpu.SMEM), spec(pl.ANY)
     flat = LAYERS * TILE_ROWS
-    blocks = TILE_ROWS * 8
-    own, to_left, to_right = pl.pallas_call(
+    own, first_out, second_out = pl.pallas_call(
         pack_kernel,
-        out_shape=(shape(blocks + 1), shape(blocks // 2 + 1), shape(blocks // 2 + 1)),
-        in_specs=[spec()] * 2, out_specs=(spec(),) * 3, name="pack",
-    )(right_side.reshape(flat, LANES), terrain.reshape(flat, LANES))
-    from_right, from_left = exchange(to_left, to_right)
-    tile = pl.pallas_call(
-        merge_kernel, out_shape=shape(2, blocks + 1),
-        in_specs=[spec()] * 3, out_specs=spec(), name="merge",
-    )(own, from_right, from_left)
+        out_shape=(shape(2, 33), shape(33), shape(33)),
+        in_specs=[smem] + [spec()] * 2, out_specs=(spec(),) * 3, name="pack",
+    )(scalars, right_side.reshape(flat, LANES), terrain.reshape(flat, LANES))
+    first, second = exchange(first_out, second_out)
 
     up = [(k, (k + 2) % gx) for k in range(gx)]
     down = [(k, (k - 2) % gx) for k in range(gx)]
     swap = [(k, k ^ 1) for k in range(gx)]
-    below = lax.ppermute(tile, "gx", up)
-    above = lax.ppermute(tile, "gx", down)
-    tile_s = lax.ppermute(tile, "gx", swap)
-    far_0 = lax.ppermute(below[0], "gx", up)
-    far_1 = lax.ppermute(above[1], "gx", down)
-    below_s = lax.ppermute(below, "gx", swap)
-    above_s = lax.ppermute(above, "gx", swap)
-    far_0_s = lax.ppermute(far_0, "gx", swap)
-    far_1_s = lax.ppermute(far_1, "gx", swap)
-    tiles = (tile, below, above, far_0, far_1, tile_s, below_s, above_s, far_0_s, far_1_s)
-
-    smem, hbm = spec(pltpu.SMEM), spec(pl.ANY)
+
+    def gather_rows(tile):
+        below = lax.ppermute(tile, "gx", up)
+        above = lax.ppermute(tile, "gx", down)
+        tile_s = lax.ppermute(tile, "gx", swap)
+        far_0 = lax.ppermute(below[0], "gx", up)
+        far_1 = lax.ppermute(above[1], "gx", down)
+        below_s = lax.ppermute(below, "gx", swap)
+        above_s = lax.ppermute(above, "gx", swap)
+        far_0_s = lax.ppermute(far_0, "gx", swap)
+        far_1_s = lax.ppermute(far_1, "gx", swap)
+        return (tile, below, above, far_0, far_1, tile_s, below_s, above_s, far_0_s, far_1_s)
+
+    is_last = first_columns((1, 1, LANES)) != (even == 1)
+    halo = jnp.stack([jnp.where(is_last, first, second), jnp.where(is_last, second, first)])
+    tiles = gather_rows(own) + gather_rows(halo)
+
     each = rows // 16
     level_0, level_1 = shape(2, rows, 8), shape(rows // 2, 4)
     fine_rows = [vmem(2, rows + 2, 8)] * 2
@@ -646,14 +632,14 @@
         lambda *refs: down_kernel(rows, *refs),
         out_shape=(level_0, level_0, level_0, shape(2, rows), level_1, level_1, level_1,
                    shape(2 * each, 2)),
-        in_specs=[smem] + [hbm] * 10, out_specs=(hbm,) * 4 + (spec(),) * 4,
+        in_specs=[smem] + [hbm] * 20, out_specs=(hbm,) * 4 + (spec(),) * 4,
         scratch_shapes=[vmem(2, rows, 8), vmem(2, rows, 8), vmem(2, rows),
-                        vmem(rows * 8), vmem(rows * 8), vmem(2, gx)]
+                        vmem(2 * gx, 32), vmem(2, gx, 32), vmem(2, gx)]
         + fine_rows + level_1_scratch(rows) + [pltpu.SemaphoreType.DMA((48,))],
         compiler_params=params(), name="down",
     )(scalars, *tiles)
 
-    right, left = exchange(packed, packed)
+    first, second = exchange(packed, packed)
     u0, u1, b1, packed_2 = pl.pallas_call(
         lambda *refs: middle_kernel(rows, *refs),
         out_shape=(level_0, level_1, level_1, shape(each, 2)),
@@ -662,9 +648,9 @@
         + fine_rows + level_1_scratch(rows) + level_2_scratch(rows)
         + [pltpu.SemaphoreType.DMA((4,))],
         compiler_params=params(), name="middle",
-    )(scalars, source, weight, height, u0, u1, b1, sh1, packed, right, left)
-
-    right_2, left_2 = exchange(packed_2, packed_2)
+    )(scalars, source, weight, height, u0, u1, b1, sh1, packed, second, first)
+
+    first_2, second_2 = exchange(packed_2, packed_2)
     out = pl.pallas_call(
         lambda *refs: last_kernel(rows, *refs),
         out_shape=jax.ShapeDtypeStruct((flat, LANES), F32),
@@ -674,7 +660,7 @@
         + [pltpu.SemaphoreType.DMA((3,))],
         compiler_params=params(), name="last",
     )(scalars, source, weight, u0, u1, b1, sh1,
-      packed_2, right_2, left_2, packed, right, left)
+      packed_2, second_2, first_2, packed, second, first)
     return out.reshape(LAYERS, TILE_ROWS, LANES)
 
 

time: 120 us -> 110 us (0.917)
  starting transfers between devices: 31.8 us -> 26.4 us
  Pallas kernels: 53.4 us -> 51.8 us
  waiting for transfers between devices: 29.5 us -> 28.1 us
    ppermute x15 -> x24, starting transfers between devices: 31.8 us -> 26.4 us  [the longest x3 12.4 us: exchange(): first = lax.ppermute(first_out, 'gy', swaps(1))]
    pallas_call x2 -> x1, Pallas kernels: 4.52 us -> 2.5 us  [per_device(): pl.pallas_call(pack_kernel, out_shape=(shape(2, 33), shape(33), shape(33)...]
    ppermute x15 -> x24, waiting for transfers between devices: 29.5 us -> 28.1 us  [the longest x3 8.18 us: exchange(): first = lax.ppermute(first_out, 'gy', swaps(1))]
    unnamed x28 -> x46, local copies, waits for them, and re-layouts: 2.71 us -> 2 us
  transfers between devices with their start and end apart: 15 -> 24, of which waited for: 10 -> 13; matrix products, arithmetic and copies ran while one was open for 1% -> 0% of each run, Pallas kernels for 0% -> 0%
where the time goes in v3:
time: 110 us
  Pallas kernels  51.8 us (47%)
  waiting for transfers between devices  28.1 us (26%)
  starting transfers between devices  26.4 us (24%)
  local copies, waits for them, and re-layouts  2.64 us (2%)
    pallas_call x1, Pallas kernels, per_device(): pl.pallas_call(lambda *refs: middle_kernel(rows, *refs), out_shape=(level...  25.7 us
    pallas_call x1, Pallas kernels, per_device(): pl.pallas_call(lambda *refs: down_kernel(rows, *refs), out_shape=(level_0...  15.7 us
    ppermute x3, starting transfers between devices, exchange(): first = lax.ppermute(first_out, 'gy', swaps(1))  12.4 us
    ppermute x2, starting transfers between devices, gather_rows(): above = lax.ppermute(tile, 'gx', down)  8.21 us
    ppermute x3, waiting for transfers between devices, exchange(): first = lax.ppermute(first_out, 'gy', swaps(1))  8.18 us
    pallas_call x1, Pallas kernels, per_device(): pl.pallas_call(lambda *refs: last_kernel(rows, *refs), out_shape=jax.Shap...  7.97 us
    ppermute x2, waiting for transfers between devices, gather_rows(): below = lax.ppermute(tile, 'gx', up)  5.99 us
    ppermute x2, waiting for transfers between devices, gather_rows(): above = lax.ppermute(tile, 'gx', down)  3.79 us
  transfers between devices with their start and end apart: 24, of which 13 were waited for; matrix products, arithmetic and copies ran while one was open for 0% of the time, Pallas kernels for 0%

profile of v3, /device:TPU:6, one launch (start us, length us, event | category | flops | bytes accessed | tf_op | source)
XLA Modules:
  0.0 109.5 jit_solution(1488684091988639099)
XLA Ops:
  0.6 2.5 %pack.1 = (f32[2,33,8,128]{3,2,1,0:T(8,128)}, f32[33,8,128]{2,1,0:T(8,128)}, f32[33,8,128]{2,1,0:T(8,128)}) custom-call(s32[6]{0:T(128)} %stack.40.s_ref.refs_0_, f32[512,128]{1,0:T(8,128)} %bitcast.20, s32[512,128]{1,0:T(8,128)} %bitcast.21), custom_call_target="tpu_custom_call" | custom-call | tf_op jit(solution)/shard_map/pack/pallas_call | solution.py:601
  3.1 5.2 %collective-permute-start.9 = (f32[33,8,128]{2,1,0:T(8,128)}, f32[33,8,128]{2,1,0:T(8,128)S(1)}, u32[]{:S(2)}, u32[]{:S(2)}) collective-permute-start(f32[33,8,128]{2,1,0:T(8,128)} %get-tuple-element.21), channel_id=1, source_target_pairs={{1,2},{3,4},{5,6},{7,8},{9,10},{11,12},{13,14},{2,1},{4,3},{6,5},{... | collective-permute-start | bytes 405512 | tf_op jit(solution)/shard_map/ppermute | solution.py:595
  8.5 4.1 %collective-permute-start.1 = (f32[2,33,8,128]{3,2,1,0:T(8,128)}, f32[2,33,8,128]{3,2,1,0:T(8,128)S(1)}, u32[]{:S(2)}, u32[]{:S(2)}) collective-permute-start(f32[2,33,8,128]{3,2,1,0:T(8,128)} %get-tuple-element.20.refs_1_), channel_id=1, source_target_pairs={{0,96},{16,112},{32,0},{48,16},{64,32},{80,48},{96,64},{112,80},{1... | collective-permute-start | bytes 811016 | tf_op jit(solution)/shard_map/ppermute | solution.py:614
  12.6 1.0 collective-permute-done.10
  13.8 4.1 %collective-permute-start.12 = (f32[2,33,8,128]{3,2,1,0:T(8,128)S(1)}, f32[2,33,8,128]{3,2,1,0:T(8,128)S(1)}, u32[]{:S(2)}, u32[]{:S(2)}) collective-permute-start(f32[2,33,8,128]{3,2,1,0:T(8,128)S(1)} %pad_maximum_fusion.refs_11_), channel_id=1, source_target_pairs={{0,96},{16,112},{32,0},{48,16},{64,32},{80,48},{96,64},{112,80},{1... | collective-permute-start | bytes 811016 | tf_op jit(solution)/shard_map/ppermute | solution.py:614
  17.9 1.8 %collective-permute-done.1.refs_3_ = f32[2,33,8,128]{3,2,1,0:T(8,128)S(1)} collective-permute-done((f32[2,33,8,128]{3,2,1,0:T(8,128)}, f32[2,33,8,128]{3,2,1,0:T(8,128)S(1)}, u32[]{:S(2)}, u32[]{:S(2)}) %collective-permute-start.1) | collective-permute-done | bytes 270368 | tf_op jit(solution)/shard_map/ppermute | solution.py:614
  19.9 2.6 %collective-permute-done.refs_2_ = f32[2,33,8,128]{3,2,1,0:T(8,128)S(1)} collective-permute-done((f32[2,33,8,128]{3,2,1,0:T(8,128)}, f32[2,33,8,128]{3,2,1,0:T(8,128)S(1)}, u32[]{:S(2)}, u32[]{:S(2)}) %collective-permute-start) | collective-permute-done | bytes 270368 | tf_op jit(solution)/shard_map/ppermute | solution.py:613
  22.6 0.8 collective-permute-start.3
  23.4 2.0 %collective-permute-done.12.refs_13_ = f32[2,33,8,128]{3,2,1,0:T(8,128)S(1)} collective-permute-done((f32[2,33,8,128]{3,2,1,0:T(8,128)S(1)}, f32[2,33,8,128]{3,2,1,0:T(8,128)S(1)}, u32[]{:S(2)}, u32[]{:S(2)}) %collective-permute-start.12) | collective-permute-done | bytes 270368 | tf_op jit(solution)/shard_map/ppermute | solution.py:614
  25.7 3.4 %collective-permute-done.11.refs_12_ = f32[2,33,8,128]{3,2,1,0:T(8,128)S(1)} collective-permute-done((f32[2,33,8,128]{3,2,1,0:T(8,128)S(1)}, f32[2,33,8,128]{3,2,1,0:T(8,128)S(1)}, u32[]{:S(2)}, u32[]{:S(2)}) %collective-permute-start.11) | collective-permute-done | bytes 270368 | tf_op jit(solution)/shard_map/ppermute | solution.py:613
  29.2 1.8 %collective-permute-start.14 = (f32[33,8,128]{2,1,0:T(8,128)S(1)}, f32[33,8,128]{2,1,0:T(8,128)S(1)}, u32[]{:S(2)}, u32[]{:S(2)}) collective-permute-start(f32[33,8,128]{2,1,0:T(8,128)S(1)} %slice_bitcast_fusion), channel_id=1, source_target_pairs={{0,96},{16,112},{32,0},{48,16},{64,32},{80,48},{96,64},{112,80},{1... | collective-permute-start | bytes 405512 | tf_op jit(solution)/shard_map/ppermute | solution.py:617
  31.3 0.8 collective-permute-done.2.refs_4_
  32.1 3.2 %collective-permute-done.14.refs_15_ = f32[33,8,128]{2,1,0:T(8,128)S(1)} collective-permute-done((f32[33,8,128]{2,1,0:T(8,128)S(1)}, f32[33,8,128]{2,1,0:T(8,128)S(1)}, u32[]{:S(2)}, u32[]{:S(2)}) %collective-permute-start.14) | collective-permute-done | bytes 135200 | tf_op jit(solution)/shard_map/ppermute | solution.py:617
  35.2 2.7 %collective-permute-done.13.refs_14_ = f32[33,8,128]{2,1,0:T(8,128)S(1)} collective-permute-done((f32[33,8,128]{2,1,0:T(8,128)S(1)}, f32[33,8,128]{2,1,0:T(8,128)S(1)}, u32[]{:S(2)}, u32[]{:S(2)}) %collective-permute-start.13) | collective-permute-done | bytes 135200 | tf_op jit(solution)/shard_map/ppermute | solution.py:616
  38.5 1.1 %collective-permute-done.7.refs_9_ = f32[33,8,128]{2,1,0:T(8,128)S(1)} collective-permute-done((f32[33,8,128]{2,1,0:T(8,128)S(1)}, f32[33,8,128]{2,1,0:T(8,128)S(1)}, u32[]{:S(2)}, u32[]{:S(2)}) %collective-permute-start.7) | collective-permute-done | bytes 135200 | tf_op jit(solution)/shard_map/ppermute | solution.py:620
  39.9 1.2 %collective-permute-done.18.refs_19_ = f32[33,8,128]{2,1,0:T(8,128)S(1)} collective-permute-done((f32[33,8,128]{2,1,0:T(8,128)S(1)}, f32[33,8,128]{2,1,0:T(8,128)S(1)}, u32[]{:S(2)}, u32[]{:S(2)}) %collective-permute-start.18) | collective-permute-done | bytes 135200 | tf_op jit(solution)/shard_map/ppermute | solution.py:620
  41.8 15.7 %down.1 = (f32[2,64,8,8,128]{4,3,2,1,0:T(8,128)}, f32[2,64,8,8,128]{4,3,2,1,0:T(8,128)}, f32[2,64,8,8,128]{4,3,2,1,0:T(8,128)}, f32[2,64,8,128]{3,2,1,0:T(8,128)...) custom-call(s32[6]{0:T(128)} %stack.40.s_ref.refs_0_, ...), custom_call_target="tpu_custom_call" | custom-call | tf_op jit(solution)/shard_map/down/pallas_call | solution.py:631
  57.6 3.1 %collective-permute-start.21 = (f32[8,2,8,128]{3,2,1,0:T(8,128)}, f32[8,2,8,128]{3,2,1,0:T(8,128)S(1)}, u32[]{:S(2)}, u32[]{:S(2)}) collective-permute-start(f32[8,2,8,128]{3,2,1,0:T(8,128)} %get-tuple-element.30.refs_8_.refs_10_), channel_id=1, source_target_pairs={{1,2},{3,4},{5,6},{7,8},{9,10},{11,12},{13,14},{2,1},{4,3},{6,5},{... | collective-permute-start | bytes 196616 | tf_op jit(solution)/shard_map/ppermute | solution.py:595
  60.6 1.1 %collective-permute-start.20 = (f32[8,2,8,128]{3,2,1,0:T(8,128)}, f32[8,2,8,128]{3,2,1,0:T(8,128)S(1)}, u32[]{:S(2)}, u32[]{:S(2)}) collective-permute-start(f32[8,2,8,128]{3,2,1,0:T(8,128)} %get-tuple-element.30.refs_8_.refs_10_), channel_id=1, source_target_pairs={{0,1},{2,3},{4,5},{6,7},{8,9},{10,11},{12,13},{14,15},{1,0},{3,2},... | collective-permute-start | bytes 196616 | tf_op jit(solution)/shard_map/ppermute | solution.py:596
  61.7 4.3 %collective-permute-done.21.refs_10_.refs_12_ = f32[8,2,8,128]{3,2,1,0:T(8,128)S(1)} collective-permute-done((f32[8,2,8,128]{3,2,1,0:T(8,128)}, f32[8,2,8,128]{3,2,1,0:T(8,128)S(1)}, u32[]{:S(2)}, u32[]{:S(2)}) %collective-permute-start.21) | collective-permute-done | bytes 65568 | tf_op jit(solution)/shard_map/ppermute | solution.py:595
  66.7 25.7 %middle.1 = (f32[2,64,8,8,128]{4,3,2,1,0:T(8,128)}, f32[32,4,8,128]{3,2,1,0:T(8,128)}, f32[32,4,8,128]{3,2,1,0:T(8,128)}, f32[4,2,8,128]{3,2,1,0:T(8,128)}) custom-call(s32[6]{0:T(128)} %stack.40.s_ref.refs_0_, f32[2,64,8,8,128]{4,3,2,1,0:T(8,128)} %get-tuple-element.23.refs_1_, f32[2,64,8,8,128]{4,3,2,1,0:T(8,128)} %get-tuple-element.24.refs_2_, ...), custom_call_target="tpu_custom_call" | custom-call | tf_op jit(solution)/shard_map/middle/pallas_call | solution.py:643
  92.4 4.2 %collective-permute-start.23 = (f32[4,2,8,128]{3,2,1,0:T(8,128)}, f32[4,2,8,128]{3,2,1,0:T(8,128)S(1)}, u32[]{:S(2)}, u32[]{:S(2)}) collective-permute-start(f32[4,2,8,128]{3,2,1,0:T(8,128)} %get-tuple-element.34.refs_7_), channel_id=1, source_target_pairs={{1,2},{3,4},{5,6},{7,8},{9,10},{11,12},{13,14},{2,1},{4,3},{6,5},{... | collective-permute-start | bytes 98312 | tf_op jit(solution)/shard_map/ppermute | solution.py:595
  96.6 3.8 %collective-permute-done.23.refs_9_ = f32[4,2,8,128]{3,2,1,0:T(8,128)S(1)} collective-permute-done((f32[4,2,8,128]{3,2,1,0:T(8,128)}, f32[4,2,8,128]{3,2,1,0:T(8,128)S(1)}, u32[]{:S(2)}, u32[]{:S(2)}) %collective-permute-start.23) | collective-permute-done | bytes 32800 | tf_op jit(solution)/shard_map/ppermute | solution.py:595
  101.4 8.0 %last.1 = f32[512,128]{1,0:T(8,128)} custom-call(s32[6]{0:T(128)} %stack.40.s_ref.refs_0_, f32[2,64,8,8,128]{4,3,2,1,0:T(8,128)} %get-tuple-element.23.refs_1_, f32[2,64,8,8,128]{4,3,2,1,0:T(8,128)} %get-tuple-element.24.refs_2_, f32[2,64,8,8,128]{4,3,2,1,0:T(8,128)} %get-tuple-element.31.refs_3_, f32[32,4,8,128]{3,2,1,0:T(8,128)} %get-tuple-element.32.refs_4_, ...), custom_call_target="tpu_custom_call" | custom-call | tf_op jit(solution)/shard_map/last/pallas_call | solution.py:654
  (82 shorter events, 5.0 us)
Async XLA Ops:
  3.1 9.5 %collective-permute-start.9 = (f32[33,8,128]{2,1,0:T(8,128)}, f32[33,8,128]{2,1,0:T(8,128)S(1)}, u32[]{:S(2)}, u32[]{:S(2)}) collective-permute-start(f32[33,8,128]{2,1,0:T(8,128)} %get-tuple-element.21), channel_id=1, source_target_pairs={{1,2},{3,4},{5,6},{7,8},{9,10},{11,12},{13,14},{2,1},{4,3},{6,5},{... | collective-permute-start | bytes 405512 | tf_op jit(solution)/shard_map/ppermute | solution.py:595
  8.3 5.3 %collective-permute-start.10 = (f32[33,8,128]{2,1,0:T(8,128)}, f32[33,8,128]{2,1,0:T(8,128)S(1)}, u32[]{:S(2)}, u32[]{:S(2)}) collective-permute-start(f32[33,8,128]{2,1,0:T(8,128)} %get-tuple-element.22), channel_id=1, source_target_pairs={{0,1},{2,3},{4,5},{6,7},{8,9},{10,11},{12,13},{14,15},{1,0},{3,2},... | collective-permute-start | bytes 405512 | tf_op jit(solution)/shard_map/ppermute | solution.py:596
  8.4 20.8 %collective-permute-start.4 = (f32[2,33,8,128]{3,2,1,0:T(8,128)}, f32[2,33,8,128]{3,2,1,0:T(8,128)S(1)}, u32[]{:S(2)}, u32[]{:S(2)}) collective-permute-start(f32[2,33,8,128]{3,2,1,0:T(8,128)} %get-tuple-element.20.refs_1_), channel_id=1, source_target_pairs={{0,16},{16,0},{32,48},{48,32},{64,80},{80,64},{96,112},{112,96},{1... | collective-permute-start | bytes 811016 | tf_op jit(solution)/shard_map/ppermute | solution.py:615
  8.5 11.2 %collective-permute-start.1 = (f32[2,33,8,128]{3,2,1,0:T(8,128)}, f32[2,33,8,128]{3,2,1,0:T(8,128)S(1)}, u32[]{:S(2)}, u32[]{:S(2)}) collective-permute-start(f32[2,33,8,128]{3,2,1,0:T(8,128)} %get-tuple-element.20.refs_1_), channel_id=1, source_target_pairs={{0,96},{16,112},{32,0},{48,16},{64,32},{80,48},{96,64},{112,80},{1... | collective-permute-start | bytes 811016 | tf_op jit(solution)/shard_map/ppermute | solution.py:614
  12.6 10.0 %collective-permute-start = (f32[2,33,8,128]{3,2,1,0:T(8,128)}, f32[2,33,8,128]{3,2,1,0:T(8,128)S(1)}, u32[]{:S(2)}, u32[]{:S(2)}) collective-permute-start(f32[2,33,8,128]{3,2,1,0:T(8,128)} %get-tuple-element.20.refs_1_), channel_id=1, source_target_pairs={{0,32},{16,48},{32,64},{48,80},{64,96},{80,112},{96,0},{112,16},{1... | collective-permute-start | bytes 811016 | tf_op jit(solution)/shard_map/ppermute | solution.py:613
  13.7 17.3 %collective-permute-start.15 = (f32[2,33,8,128]{3,2,1,0:T(8,128)S(1)}, f32[2,33,8,128]{3,2,1,0:T(8,128)S(1)}, u32[]{:S(2)}, u32[]{:S(2)}) collective-permute-start(f32[2,33,8,128]{3,2,1,0:T(8,128)S(1)} %pad_maximum_fusion.refs_11_), channel_id=1, source_target_pairs={{0,16},{16,0},{32,48},{48,32},{64,80},{80,64},{96,112},{112,96},{1... | collective-permute-start | bytes 811016 | tf_op jit(solution)/shard_map/ppermute | solution.py:615
  13.8 11.6 %collective-permute-start.12 = (f32[2,33,8,128]{3,2,1,0:T(8,128)S(1)}, f32[2,33,8,128]{3,2,1,0:T(8,128)S(1)}, u32[]{:S(2)}, u32[]{:S(2)}) collective-permute-start(f32[2,33,8,128]{3,2,1,0:T(8,128)S(1)} %pad_maximum_fusion.refs_11_), channel_id=1, source_target_pairs={{0,96},{16,112},{32,0},{48,16},{64,32},{80,48},{96,64},{112,80},{1... | collective-permute-start | bytes 811016 | tf_op jit(solution)/shard_map/ppermute | solution.py:614
  19.7 9.4 %collective-permute-start.11 = (f32[2,33,8,128]{3,2,1,0:T(8,128)S(1)}, f32[2,33,8,128]{3,2,1,0:T(8,128)S(1)}, u32[]{:S(2)}, u32[]{:S(2)}) collective-permute-start(f32[2,33,8,128]{3,2,1,0:T(8,128)S(1)} %pad_maximum_fusion.refs_11_), channel_id=1, source_target_pairs={{0,32},{16,48},{32,64},{48,80},{64,96},{80,112},{96,0},{112,16},{1... | collective-permute-start | bytes 811016 | tf_op jit(solution)/shard_map/ppermute | solution.py:613
  22.6 8.7 %collective-permute-start.3 = (f32[33,8,128]{2,1,0:T(8,128)S(1)}, f32[33,8,128]{2,1,0:T(8,128)S(1)}, u32[]{:S(2)}, u32[]{:S(2)}) collective-permute-start(f32[33,8,128]{2,1,0:T(8,128)S(1)} %slice_bitcast_fusion.2), channel_id=1, source_target_pairs={{0,96},{16,112},{32,0},{48,16},{64,32},{80,48},{96,64},{112,80},{1... | collective-permute-start | bytes 405512 | tf_op jit(solution)/shard_map/ppermute | solution.py:617
  25.4 6.7 %collective-permute-start.2 = (f32[33,8,128]{2,1,0:T(8,128)S(1)}, f32[33,8,128]{2,1,0:T(8,128)S(1)}, u32[]{:S(2)}, u32[]{:S(2)}) collective-permute-start(f32[33,8,128]{2,1,0:T(8,128)S(1)} %slice_bitcast_fusion.3), channel_id=1, source_target_pairs={{0,32},{16,48},{32,64},{48,80},{64,96},{80,112},{96,0},{112,16},{1... | collective-permute-start | bytes 405512 | tf_op jit(solution)/shard_map/ppermute | solution.py:616
  29.1 9.3 %collective-permute-start.6 = (f32[2,33,8,128]{3,2,1,0:T(8,128)S(1)}, f32[2,33,8,128]{3,2,1,0:T(8,128)S(1)}, u32[]{:S(2)}, u32[]{:S(2)}) collective-permute-start(f32[2,33,8,128]{3,2,1,0:T(8,128)S(1)} %collective-permute-done.1.refs_3_), channel_id=1, source_target_pairs={{0,16},{16,0},{32,48},{48,32},{64,80},{80,64},{96,112},{112,96},{1... | collective-permute-start | bytes 811016 | tf_op jit(solution)/shard_map/ppermute | solution.py:619
  29.2 6.1 %collective-permute-start.14 = (f32[33,8,128]{2,1,0:T(8,128)S(1)}, f32[33,8,128]{2,1,0:T(8,128)S(1)}, u32[]{:S(2)}, u32[]{:S(2)}) collective-permute-start(f32[33,8,128]{2,1,0:T(8,128)S(1)} %slice_bitcast_fusion), channel_id=1, source_target_pairs={{0,96},{16,112},{32,0},{48,16},{64,32},{80,48},{96,64},{112,80},{1... | collective-permute-start | bytes 405512 | tf_op jit(solution)/shard_map/ppermute | solution.py:617
  31.0 6.9 %collective-permute-start.13 = (f32[33,8,128]{2,1,0:T(8,128)S(1)}, f32[33,8,128]{2,1,0:T(8,128)S(1)}, u32[]{:S(2)}, u32[]{:S(2)}) collective-permute-start(f32[33,8,128]{2,1,0:T(8,128)S(1)} %slice_bitcast_fusion.1), channel_id=1, source_target_pairs={{0,32},{16,48},{32,64},{48,80},{64,96},{80,112},{96,0},{112,16},{1... | collective-permute-start | bytes 405512 | tf_op jit(solution)/shard_map/ppermute | solution.py:616
  31.3 6.6 %collective-permute-start.8 = (f32[33,8,128]{2,1,0:T(8,128)S(1)}, f32[33,8,128]{2,1,0:T(8,128)S(1)}, u32[]{:S(2)}, u32[]{:S(2)}) collective-permute-start(f32[33,8,128]{2,1,0:T(8,128)S(1)} %collective-permute-done.3.refs_5_), channel_id=1, source_target_pairs={{0,16},{16,0},{32,48},{48,32},{64,80},{80,64},{96,112},{112,96},{1... | collective-permute-start | bytes 405512 | tf_op jit(solution)/shard_map/ppermute | solution.py:621
  32.1 7.7 %collective-permute-start.5 = (f32[2,33,8,128]{3,2,1,0:T(8,128)S(1)}, f32[2,33,8,128]{3,2,1,0:T(8,128)S(1)}, u32[]{:S(2)}, u32[]{:S(2)}) collective-permute-start(f32[2,33,8,128]{3,2,1,0:T(8,128)S(1)} %collective-permute-done.refs_2_), channel_id=1, source_target_pairs={{0,16},{16,0},{32,48},{48,32},{64,80},{80,64},{96,112},{112,96},{1... | collective-permute-start | bytes 811016 | tf_op jit(solution)/shard_map/ppermute | solution.py:618
  35.2 4.6 %collective-permute-start.17 = (f32[2,33,8,128]{3,2,1,0:T(8,128)S(1)}, f32[2,33,8,128]{3,2,1,0:T(8,128)S(1)}, u32[]{:S(2)}, u32[]{:S(2)}) collective-permute-start(f32[2,33,8,128]{3,2,1,0:T(8,128)S(1)} %collective-permute-done.12.refs_13_), channel_id=1, source_target_pairs={{0,16},{16,0},{32,48},{48,32},{64,80},{80,64},{96,112},{112,96},{1... | collective-permute-start | bytes 811016 | tf_op jit(solution)/shard_map/ppermute | solution.py:619
  37.9 1.9 %collective-permute-start.16 = (f32[2,33,8,128]{3,2,1,0:T(8,128)S(1)}, f32[2,33,8,128]{3,2,1,0:T(8,128)S(1)}, u32[]{:S(2)}, u32[]{:S(2)}) collective-permute-start(f32[2,33,8,128]{3,2,1,0:T(8,128)S(1)} %collective-permute-done.11.refs_12_), channel_id=1, source_target_pairs={{0,16},{16,0},{32,48},{48,32},{64,80},{80,64},{96,112},{112,96},{1... | collective-permute-start | bytes 811016 | tf_op jit(solution)/shard_map/ppermute | solution.py:618
  37.9 1.7 %collective-permute-start.7 = (f32[33,8,128]{2,1,0:T(8,128)S(1)}, f32[33,8,128]{2,1,0:T(8,128)S(1)}, u32[]{:S(2)}, u32[]{:S(2)}) collective-permute-start(f32[33,8,128]{2,1,0:T(8,128)S(1)} %collective-permute-done.2.refs_4_), channel_id=1, source_target_pairs={{0,16},{16,0},{32,48},{48,32},{64,80},{80,64},{96,112},{112,96},{1... | collective-permute-start | bytes 405512 | tf_op jit(solution)/shard_map/ppermute | solution.py:620
  38.4 1.4 %collective-permute-start.19 = (f32[33,8,128]{2,1,0:T(8,128)S(1)}, f32[33,8,128]{2,1,0:T(8,128)S(1)}, u32[]{:S(2)}, u32[]{:S(2)}) collective-permute-start(f32[33,8,128]{2,1,0:T(8,128)S(1)} %collective-permute-done.14.refs_15_), channel_id=1, source_target_pairs={{0,16},{16,0},{32,48},{48,32},{64,80},{80,64},{96,112},{112,96},{1... | collective-permute-start | bytes 405512 | tf_op jit(solution)/shard_map/ppermute | solution.py:621
  39.7 1.4 %collective-permute-start.18 = (f32[33,8,128]{2,1,0:T(8,128)S(1)}, f32[33,8,128]{2,1,0:T(8,128)S(1)}, u32[]{:S(2)}, u32[]{:S(2)}) collective-permute-start(f32[33,8,128]{2,1,0:T(8,128)S(1)} %collective-permute-done.13.refs_14_), channel_id=1, source_target_pairs={{0,16},{16,0},{32,48},{48,32},{64,80},{80,64},{96,112},{112,96},{1... | collective-permute-start | bytes 405512 | tf_op jit(solution)/shard_map/ppermute | solution.py:620
  57.6 8.5 %collective-permute-start.21 = (f32[8,2,8,128]{3,2,1,0:T(8,128)}, f32[8,2,8,128]{3,2,1,0:T(8,128)S(1)}, u32[]{:S(2)}, u32[]{:S(2)}) collective-permute-start(f32[8,2,8,128]{3,2,1,0:T(8,128)} %get-tuple-element.30.refs_8_.refs_10_), channel_id=1, source_target_pairs={{1,2},{3,4},{5,6},{7,8},{9,10},{11,12},{13,14},{2,1},{4,3},{6,5},{... | collective-permute-start | bytes 196616 | tf_op jit(solution)/shard_map/ppermute | solution.py:595
  60.6 5.4 %collective-permute-start.20 = (f32[8,2,8,128]{3,2,1,0:T(8,128)}, f32[8,2,8,128]{3,2,1,0:T(8,128)S(1)}, u32[]{:S(2)}, u32[]{:S(2)}) collective-permute-start(f32[8,2,8,128]{3,2,1,0:T(8,128)} %get-tuple-element.30.refs_8_.refs_10_), channel_id=1, source_target_pairs={{0,1},{2,3},{4,5},{6,7},{8,9},{10,11},{12,13},{14,15},{1,0},{3,2},... | collective-permute-start | bytes 196616 | tf_op jit(solution)/shard_map/ppermute | solution.py:596
  92.4 8.1 %collective-permute-start.23 = (f32[4,2,8,128]{3,2,1,0:T(8,128)}, f32[4,2,8,128]{3,2,1,0:T(8,128)S(1)}, u32[]{:S(2)}, u32[]{:S(2)}) collective-permute-start(f32[4,2,8,128]{3,2,1,0:T(8,128)} %get-tuple-element.34.refs_7_), channel_id=1, source_target_pairs={{1,2},{3,4},{5,6},{7,8},{9,10},{11,12},{13,14},{2,1},{4,3},{6,5},{... | collective-permute-start | bytes 98312 | tf_op jit(solution)/shard_map/ppermute | solution.py:595
  96.6 4.2 %collective-permute-start.22 = (f32[4,2,8,128]{3,2,1,0:T(8,128)}, f32[4,2,8,128]{3,2,1,0:T(8,128)S(1)}, u32[]{:S(2)}, u32[]{:S(2)}) collective-permute-start(f32[4,2,8,128]{3,2,1,0:T(8,128)} %get-tuple-element.34.refs_7_), channel_id=1, source_target_pairs={{0,1},{2,3},{4,5},{6,7},{8,9},{10,11},{12,13},{14,15},{1,0},{3,2},... | collective-permute-start | bytes 98312 | tf_op jit(solution)/shard_map/ppermute | solution.py:596
  (23 other events, 160.3 us)

commit v4 on v3

--- a/solution.py
+++ b/solution.py
@@ -113,14 +113,46 @@
         ).astype(F32)
         return layer < self.height[h, row][None]
 
-    def relax(self, src, dst, start, rows, group):
-        def emit(row, pairs):
-            for h, (v, total) in enumerate(pairs):
-                total = total + self.source[h, row]
-                dst[h, row + 1] = (1.0 - RELAX_WEIGHT) * v + self.weight[h, row] * total
-
-        over_rows(start, rows, group,
-                  lambda first, count: stencil_group(self.loader(src), first, count, emit))
+    def relax(self, src, dst, start, rows, group, together=1):
+        sub = lax.broadcasted_iota(jnp.int32, (1, SUB, LANES), 1)
+
+        def body(first, count):
+            for z in (0, 4):
+                chunk = pl.ds(z, 4)
+
+                def load(row):
+                    return [src[h, row + 1, chunk] for h in range(2)]
+
+                before, centre = load(first - 1), load(first)
+                pending = []
+                for k in range(count):
+                    row = first + k
+                    after = load(row + 1)
+                    sides = column_sum(centre)
+                    for h, v in enumerate(centre):
+                        if z == 0:
+                            below = pltpu.roll(src[h, row + 1, pl.ds(7, 1)], 1, axis=1)
+                            below = jnp.where(sub == 0, 0.0, below)
+                            above = src[h, row + 1, pl.ds(4, 1)]
+                        else:
+                            below = src[h, row + 1, pl.ds(3, 1)]
+                            above = pltpu.roll(src[h, row + 1, pl.ds(0, 1)], SUB - 1, axis=1)
+                            above = jnp.where(sub == SUB - 1, 0.0, above)
+                        total = before[h] + after[h] + sides[h]
+                        total = total + (
+                            jnp.concatenate([below, v[:-1]], axis=0)
+                            + jnp.concatenate([v[1:], above], axis=0)
+                        )
+                        total = total + self.source[h, row, chunk]
+                        new = (1.0 - RELAX_WEIGHT) * v + self.weight[h, row, chunk] * total
+                        pending.append((h, row, new))
+                    before, centre = centre, after
+                    if (k + 1) % together == 0 or k == count - 1:
+                        for h, row, new in pending:
+                            dst[h, row + 1, chunk] = new
+                        pending = []
+
+        over_rows(start, rows, group, body)
 
     def restricted_defect(self, src, rows, out):
         load = self.loader(src)
@@ -276,9 +308,9 @@
     pack_level_2(level.defect_pairs(vb), packed, 0)
 
 
-def coarse_part(tiles, shift_tiles, s_ref, rows2, refs):
+def coarse_part(tiles, shift_tiles, at, rows2, refs):
     va, vb, b2, sh2, w2 = refs
-    has_left, has_right, even = s_ref[2], s_ref[3], s_ref[5] == 1
+    has_left, has_right, even = at.has_left, at.has_right, at.even
     each = rows2 // 4
     unpack_level_2(*tiles, even, 0, each, b2)
     unpack_level_2(*shift_tiles, even, each, each, sh2)
@@ -352,7 +384,7 @@
 
 
 def pack_kernel(s_ref, right_side, terrain, own, first_out, second_out):
-    even = s_ref[5] == 1
+    even = Place(s_ref).even
     apart = matrix_of(lambda a, b: b == lax.div(a, 2) + 64 * lax.rem(a, 2))
     heights = terrain[pl.ds(0, TILE_ROWS), :]
     for z in range(1, 32):
@@ -379,13 +411,13 @@
 
 
 def down_kernel(rows, s_ref, *refs):
-    tiles, refs = refs[:20], refs[20:]
+    at = Place(s_ref)
+    tiles, refs = refs[:16], refs[16:]
     (u0, source_out, weight_out, height_out, u1, b1, sh1, packed,
      source, weight, height, own, beside, heights, va0, vb0, va1, vb1, w1, sems) = refs
-    has_left, has_right = s_ref[2], s_ref[3]
+    has_left, has_right = at.has_left, at.has_right
     chips = rows // (2 * TILE_ROWS)
-    me = lax.div(s_ref[4], TILE_ROWS)
-    z, core = lax.div(me, 2), lax.rem(me, 2)
+    z, core = at.chip, at.core
 
     def device(step, other):
         return 2 * lax.rem(z + step + chips, chips) + (1 - core if other else core)
@@ -395,12 +427,14 @@
     def start_copy(source_ref, target_ref):
         copies.append(pltpu.make_async_copy(source_ref, target_ref, sems.at[len(copies)]))
 
-    for kind in range(2):
-        for other in range(2):
-            w, a, b, c0, c1 = tiles[10 * kind + 5 * other:10 * kind + 5 * other + 5]
-            pieces = [(ref.at[part], device(step, other), part)
-                      for ref, step in ((w, 0), (a, -1), (b, 1)) for part in range(2)]
-            pieces += [(c0, device(2, other), 0), (c1, device(2, other), 1)]
+    for other in range(2):
+        group = tiles[8 * other:8 * other + 8]
+        for kind in range(2):
+            pieces = [
+                (group[3 * kind + n].at[part], device(step, other), part)
+                for n, step in enumerate((0, -1, 1)) for part in range(2)
+            ]
+            pieces += [(group[6 + part].at[kind], device(2, other), part) for part in range(2)]
             for ref, dev, part in pieces:
                 target = own.at[2 * dev + part] if kind == 0 else beside.at[part, dev]
                 start_copy(ref.at[pl.ds(0, 32)], target)
@@ -454,9 +488,9 @@
     for save in saves:
         save.start()
     fine.coarse_shift(rows, sh1)
-    fine.relax(va0, vb0, 0, rows, 16)
-    fine.relax(vb0, va0, 0, rows, 16)
-    fine.relax(va0, vb0, 0, rows, 16)
+    fine.relax(va0, vb0, 0, rows, 8, 4)
+    fine.relax(vb0, va0, 0, rows, 8, 4)
+    fine.relax(va0, vb0, 0, rows, 8, 4)
     saves.append(pltpu.make_async_copy(interior(vb0, rows), u0, sems.at[0]))
     saves[-1].start()
     fine.restricted_defect(vb0, rows, b1)
@@ -472,7 +506,8 @@
 def middle_kernel(rows, s_ref, source_in, weight_in, height_in, u0, u1, b1, sh1, own, second, first,
                   u0_out, u1_out, b1_out, packed,
                   source, weight, height, va0, vb0, va1, vb1, w1, va2, vb2, b2, sh2, w2, sems):
-    has_left, has_right = s_ref[2], s_ref[3]
+    at = Place(s_ref)
+    has_left, has_right = at.has_left, at.has_right
     copies = [
         pltpu.make_async_copy(u0, interior(va0, rows), sems.at[0]),
         pltpu.make_async_copy(source_in, source, sems.at[1]),
@@ -483,7 +518,7 @@
         copy.start()
     for ref in (va1, vb1):
         zero_rim(ref, rows // 2, 1)
-    e2 = coarse_part((own, first, second), (own, first, second), s_ref, rows // 4,
+    e2 = coarse_part((own, first, second), (own, first, second), at, rows // 4,
                      (va2, vb2, b2, sh2, w2))
     level = Coarse(b1, w1, sh1, rows // 2, 16)
     level.set_weight(edge_mask(1, has_left, has_right))
@@ -509,7 +544,8 @@
 def last_kernel(rows, s_ref, source_in, weight_in, u0, u1, b1, sh1,
                 own, second, first, own_s, second_s, first_s,
                 out, source, weight, va0, vb0, va1, vb1, w1, va2, vb2, b2, sh2, w2, sems):
-    start, has_left, has_right, mine = s_ref[1], s_ref[2], s_ref[3], s_ref[4]
+    at = Place(s_ref)
+    start, has_left, has_right, mine = at.start, at.has_left, at.has_right, at.mine
     window = pl.ds(start, WINDOW)
     copies = [
         pltpu.make_async_copy(u0.at[:, window], interior(va0, WINDOW), sems.at[0]),
@@ -520,7 +556,7 @@
         copy.start()
     for ref in (va1, vb1):
         zero_rim(ref, rows // 2, 1)
-    e2 = coarse_part((own, first, second), (own_s, first_s, second_s), s_ref, rows // 4,
+    e2 = coarse_part((own, first, second), (own_s, first_s, second_s), at, rows // 4,
                      (va2, vb2, b2, sh2, w2))
     level = Coarse(b1, w1, sh1, rows // 2, 16)
     level.set_weight(edge_mask(1, has_left, has_right))
@@ -552,6 +588,12 @@
             )
 
 
+class Place:
+    def __init__(self, s_ref):
+        self.start, self.mine, self.chip, self.core = s_ref[0], s_ref[1], s_ref[2], s_ref[3]
+        self.has_left, self.has_right, self.even = s_ref[4], s_ref[5], s_ref[6] == 1
+
+
 def spec(space=pltpu.VMEM):
     return pl.BlockSpec(memory_space=space)
 
@@ -580,11 +622,10 @@
     gx, gy = lax.axis_size("gx"), lax.axis_size("gy")
     rows = TILE_ROWS * gx
     i, j = lax.axis_index("gx"), lax.axis_index("gy")
-    mine = TILE_ROWS * i
-    start = jnp.clip(mine - 4, 0, rows - WINDOW)
-    even = 1 - lax.rem(j, 2)
+    mine, even = TILE_ROWS * i, 1 - lax.rem(j, 2)
     scalars = jnp.stack([
-        jnp.int32(0), start, (j > 0).astype(jnp.int32), (j < gy - 1).astype(jnp.int32), mine, even
+        jnp.clip(mine - 4, 0, rows - WINDOW), mine, lax.div(i, 2), lax.rem(i, 2),
+        (j > 0).astype(jnp.int32), (j < gy - 1).astype(jnp.int32), even,
     ])
 
     def swaps(begin):
@@ -609,21 +650,25 @@
     down = [(k, (k - 2) % gx) for k in range(gx)]
     swap = [(k, k ^ 1) for k in range(gx)]
 
-    def gather_rows(tile):
+    def gather_near(tile):
         below = lax.ppermute(tile, "gx", up)
         above = lax.ppermute(tile, "gx", down)
-        tile_s = lax.ppermute(tile, "gx", swap)
-        far_0 = lax.ppermute(below[0], "gx", up)
-        far_1 = lax.ppermute(above[1], "gx", down)
-        below_s = lax.ppermute(below, "gx", swap)
-        above_s = lax.ppermute(above, "gx", swap)
-        far_0_s = lax.ppermute(far_0, "gx", swap)
-        far_1_s = lax.ppermute(far_1, "gx", swap)
-        return (tile, below, above, far_0, far_1, tile_s, below_s, above_s, far_0_s, far_1_s)
+        return below, above
+
+    def swapped(*arrays):
+        return tuple(lax.ppermute(x, "gx", swap) for x in arrays)
+
+    own_near = gather_near(own)
 
     is_last = first_columns((1, 1, LANES)) != (even == 1)
     halo = jnp.stack([jnp.where(is_last, first, second), jnp.where(is_last, second, first)])
-    tiles = gather_rows(own) + gather_rows(halo)
+    halo_near = gather_near(halo)
+    far = (
+        lax.ppermute(jnp.stack([own_near[0][0], halo_near[0][0]]), "gx", up),
+        lax.ppermute(jnp.stack([own_near[1][1], halo_near[1][1]]), "gx", down),
+    )
+    arrays = (own,) + own_near + (halo,) + halo_near + far
+    tiles = arrays + swapped(*arrays)
 
     each = rows // 16
     level_0, level_1 = shape(2, rows, 8), shape(rows // 2, 4)
@@ -632,7 +677,7 @@
         lambda *refs: down_kernel(rows, *refs),
         out_shape=(level_0, level_0, level_0, shape(2, rows), level_1, level_1, level_1,
                    shape(2 * each, 2)),
-        in_specs=[smem] + [hbm] * 20, out_specs=(hbm,) * 4 + (spec(),) * 4,
+        in_specs=[smem] + [hbm] * 16, out_specs=(hbm,) * 4 + (spec(),) * 4,
         scratch_shapes=[vmem(2, rows, 8), vmem(2, rows, 8), vmem(2, rows),
                         vmem(2 * gx, 32), vmem(2, gx, 32), vmem(2, gx)]
         + fine_rows + level_1_scratch(rows) + [pltpu.SemaphoreType.DMA((48,))],

time: 110 us -> 108 us (0.982)
  waiting for transfers between devices: 28.1 us -> 25 us
  Pallas kernels: 51.8 us -> 53.8 us
    ppermute x18 -> x14, waiting for transfers between devices: 18.7 us -> 14.8 us  [the longest x1 3.69 us: per_device(): lax.ppermute(jnp.stack([own_near[1][1], halo_near[1][1]]), 'gx', down)]
    ppermute x18 -> x14, starting transfers between devices: 12.7 us -> 12.7 us  [the longest x2 8.21 us: gather_near(): above = lax.ppermute(tile, 'gx', down)]
  transfers between devices with their start and end apart: 24 -> 20, of which waited for: 13 -> 11; matrix products, arithmetic and copies ran while one was open for 0% -> 0% of each run, Pallas kernels for 0% -> 0%
where the time goes in v4:
time: 108 us
  Pallas kernels  53.8 us (50%)
  starting transfers between devices  25.8 us (24%)
  waiting for transfers between devices  25 us (23%)
  local copies, waits for them, and re-layouts  2.74 us (3%)
    pallas_call x1, Pallas kernels, per_device(): pl.pallas_call(lambda *refs: middle_kernel(rows, *refs), out_shape=(level...  26.5 us
    pallas_call x1, Pallas kernels, per_device(): pl.pallas_call(lambda *refs: down_kernel(rows, *refs), out_shape=(level_0...  16.7 us
    ppermute x3, starting transfers between devices, exchange(): first = lax.ppermute(first_out, 'gy', swaps(1))  12 us
    ppermute x3, waiting for transfers between devices, exchange(): first = lax.ppermute(first_out, 'gy', swaps(1))  8.88 us
    ppermute x2, starting transfers between devices, gather_near(): above = lax.ppermute(tile, 'gx', down)  8.21 us
    pallas_call x1, Pallas kernels, per_device(): pl.pallas_call(lambda *refs: last_kernel(rows, *refs), out_shape=jax.Shap...  8.06 us
    ppermute x1, starting transfers between devices, per_device(): lax.ppermute(jnp.stack([own_near[1][1], halo_near[1][1]]), 'gx', down)  3.76 us
    ppermute x1, waiting for transfers between devices, per_device(): lax.ppermute(jnp.stack([own_near[1][1], halo_near[1][1]]), 'gx', down)  3.69 us
  transfers between devices with their start and end apart: 20, of which 11 were waited for; matrix products, arithmetic and copies ran while one was open for 0% of the time, Pallas kernels for 0%

profile of v4, /device:TPU:6, one launch (start us, length us, event | category | flops | bytes accessed | tf_op | source)
XLA Modules:
  0.0 107.9 jit_solution(16859079253960923037)
XLA Ops:
  0.0 0.7 stack.54.s_ref.refs_0_
  0.7 2.5 %pack.1 = (f32[2,33,8,128]{3,2,1,0:T(8,128)}, f32[33,8,128]{2,1,0:T(8,128)}, f32[33,8,128]{2,1,0:T(8,128)}) custom-call(s32[7]{0:T(128)} %stack.54.s_ref.refs_0_, f32[512,128]{1,0:T(8,128)} %bitcast.14, s32[512,128]{1,0:T(8,128)} %bitcast.15), custom_call_target="tpu_custom_call" | custom-call | tf_op jit(solution)/shard_map/pack/pallas_call | solution.py:642
  3.2 5.2 %collective-permute-start.2 = (f32[33,8,128]{2,1,0:T(8,128)}, f32[33,8,128]{2,1,0:T(8,128)S(1)}, u32[]{:S(2)}, u32[]{:S(2)}) collective-permute-start(f32[33,8,128]{2,1,0:T(8,128)} %get-tuple-element.21), channel_id=1, source_target_pairs={{1,2},{3,4},{5,6},{7,8},{9,10},{11,12},{13,14},{2,1},{4,3},{6,5},{... | collective-permute-start | bytes 405512 | tf_op jit(solution)/shard_map/ppermute | solution.py:636
  8.4 4.1 %collective-permute-start.1 = (f32[2,33,8,128]{3,2,1,0:T(8,128)}, f32[2,33,8,128]{3,2,1,0:T(8,128)S(1)}, u32[]{:S(2)}, u32[]{:S(2)}) collective-permute-start(f32[2,33,8,128]{3,2,1,0:T(8,128)} %get-tuple-element.20.refs_1_), channel_id=1, source_target_pairs={{0,96},{16,112},{32,0},{48,16},{64,32},{80,48},{96,64},{112,80},{1... | collective-permute-start | bytes 811016 | tf_op jit(solution)/shard_map/ppermute | solution.py:655
  12.7 1.0 collective-permute-done.3
  13.7 4.1 %collective-permute-start.5 = (f32[2,33,8,128]{3,2,1,0:T(8,128)S(1)}, f32[2,33,8,128]{3,2,1,0:T(8,128)S(1)}, u32[]{:S(2)}, u32[]{:S(2)}) collective-permute-start(f32[2,33,8,128]{3,2,1,0:T(8,128)S(1)} %pad_maximum_fusion.refs_4_), channel_id=1, source_target_pairs={{0,96},{16,112},{32,0},{48,16},{64,32},{80,48},{96,64},{112,80},{1... | collective-permute-start | bytes 811016 | tf_op jit(solution)/shard_map/ppermute | solution.py:655
  17.9 1.9 %collective-permute-done.1.refs_3_ = f32[2,33,8,128]{3,2,1,0:T(8,128)S(1)} collective-permute-done((f32[2,33,8,128]{3,2,1,0:T(8,128)}, f32[2,33,8,128]{3,2,1,0:T(8,128)S(1)}, u32[]{:S(2)}, u32[]{:S(2)}) %collective-permute-start.1) | collective-permute-done | bytes 270368 | tf_op jit(solution)/shard_map/ppermute | solution.py:655
  19.8 3.3 %collective-permute-done.refs_2_ = f32[2,33,8,128]{3,2,1,0:T(8,128)S(1)} collective-permute-done((f32[2,33,8,128]{3,2,1,0:T(8,128)}, f32[2,33,8,128]{3,2,1,0:T(8,128)S(1)}, u32[]{:S(2)}, u32[]{:S(2)}) %collective-permute-start) | collective-permute-done | bytes 270368 | tf_op jit(solution)/shard_map/ppermute | solution.py:654
  23.2 0.8 collective-permute-done.5.refs_6_
  24.1 3.8 %collective-permute-start.7 = (f32[2,33,8,128]{3,2,1,0:T(8,128)S(1)}, f32[2,33,8,128]{3,2,1,0:T(8,128)S(1)}, u32[]{:S(2)}, u32[]{:S(2)}) collective-permute-start(f32[2,33,8,128]{3,2,1,0:T(8,128)S(1)} %pad_maximum_fusion.2), channel_id=1, source_target_pairs={{0,96},{16,112},{32,0},{48,16},{64,32},{80,48},{96,64},{112,80},{1... | collective-permute-start | bytes 811016 | tf_op jit(solution)/shard_map/ppermute | solution.py:668
  28.1 0.5 collective-permute-start.13
  28.7 3.7 %collective-permute-done.7.refs_8_ = f32[2,33,8,128]{3,2,1,0:T(8,128)S(1)} collective-permute-done((f32[2,33,8,128]{3,2,1,0:T(8,128)S(1)}, f32[2,33,8,128]{3,2,1,0:T(8,128)S(1)}, u32[]{:S(2)}, u32[]{:S(2)}) %collective-permute-start.7) | collective-permute-done | bytes 270368 | tf_op jit(solution)/shard_map/ppermute | solution.py:668
  32.4 3.5 %collective-permute-done.6.refs_7_ = f32[2,33,8,128]{3,2,1,0:T(8,128)S(1)} collective-permute-done((f32[2,33,8,128]{3,2,1,0:T(8,128)S(1)}, f32[2,33,8,128]{3,2,1,0:T(8,128)S(1)}, u32[]{:S(2)}, u32[]{:S(2)}) %collective-permute-start.6) | collective-permute-done | bytes 270368 | tf_op jit(solution)/shard_map/ppermute | solution.py:667
  36.0 1.5 %collective-permute-done.14.refs_15_ = f32[2,33,8,128]{3,2,1,0:T(8,128)S(1)} collective-permute-done((f32[2,33,8,128]{3,2,1,0:T(8,128)S(1)}, f32[2,33,8,128]{3,2,1,0:T(8,128)S(1)}, u32[]{:S(2)}, u32[]{:S(2)}) %collective-permute-start.14) | collective-permute-done | bytes 270368 | tf_op jit(solution)/shard_map/ppermute | solution.py:659
  37.6 0.7 copy-done.14
  38.3 16.7 %down.1 = (f32[2,64,8,8,128]{4,3,2,1,0:T(8,128)}, f32[2,64,8,8,128]{4,3,2,1,0:T(8,128)}, f32[2,64,8,8,128]{4,3,2,1,0:T(8,128)}, f32[2,64,8,128]{3,2,1,0:T(8,128)...) custom-call(s32[7]{0:T(128)} %stack.54.s_ref.refs_0_, ...), custom_call_target="tpu_custom_call" | custom-call | tf_op jit(solution)/shard_map/down/pallas_call | solution.py:676
  55.0 2.6 %collective-permute-start.17 = (f32[8,2,8,128]{3,2,1,0:T(8,128)}, f32[8,2,8,128]{3,2,1,0:T(8,128)S(1)}, u32[]{:S(2)}, u32[]{:S(2)}) collective-permute-start(f32[8,2,8,128]{3,2,1,0:T(8,128)} %get-tuple-element.30.refs_8_.refs_10_), channel_id=1, source_target_pairs={{1,2},{3,4},{5,6},{7,8},{9,10},{11,12},{13,14},{2,1},{4,3},{6,5},{... | collective-permute-start | bytes 196616 | tf_op jit(solution)/shard_map/ppermute | solution.py:636
  57.6 0.9 collective-permute-start.16
  58.6 4.9 %collective-permute-done.17.refs_10_.refs_12_ = f32[8,2,8,128]{3,2,1,0:T(8,128)S(1)} collective-permute-done((f32[8,2,8,128]{3,2,1,0:T(8,128)}, f32[8,2,8,128]{3,2,1,0:T(8,128)S(1)}, u32[]{:S(2)}, u32[]{:S(2)}) %collective-permute-start.17) | collective-permute-done | bytes 65568 | tf_op jit(solution)/shard_map/ppermute | solution.py:636
  63.5 0.6 copy-done.15
  64.1 26.5 %middle.1 = (f32[2,64,8,8,128]{4,3,2,1,0:T(8,128)}, f32[32,4,8,128]{3,2,1,0:T(8,128)}, f32[32,4,8,128]{3,2,1,0:T(8,128)}, f32[4,2,8,128]{3,2,1,0:T(8,128)}) custom-call(s32[7]{0:T(128)} %stack.54.s_ref.refs_0_, f32[2,64,8,8,128]{4,3,2,1,0:T(8,128)} %get-tuple-element.23.refs_1_, f32[2,64,8,8,128]{4,3,2,1,0:T(8,128)} %get-tuple-element.24.refs_2_, ...), custom_call_target="tpu_custom_call" | custom-call | tf_op jit(solution)/shard_map/middle/pallas_call | solution.py:688
  90.7 4.2 %collective-permute-start.19 = (f32[4,2,8,128]{3,2,1,0:T(8,128)}, f32[4,2,8,128]{3,2,1,0:T(8,128)S(1)}, u32[]{:S(2)}, u32[]{:S(2)}) collective-permute-start(f32[4,2,8,128]{3,2,1,0:T(8,128)} %get-tuple-element.34.refs_7_), channel_id=1, source_target_pairs={{1,2},{3,4},{5,6},{7,8},{9,10},{11,12},{13,14},{2,1},{4,3},{6,5},{... | collective-permute-start | bytes 98312 | tf_op jit(solution)/shard_map/ppermute | solution.py:636
  95.0 3.8 %collective-permute-done.19.refs_9_ = f32[4,2,8,128]{3,2,1,0:T(8,128)S(1)} collective-permute-done((f32[4,2,8,128]{3,2,1,0:T(8,128)}, f32[4,2,8,128]{3,2,1,0:T(8,128)S(1)}, u32[]{:S(2)}, u32[]{:S(2)}) %collective-permute-start.19) | collective-permute-done | bytes 32800 | tf_op jit(solution)/shard_map/ppermute | solution.py:636
  99.7 8.1 %last.1 = f32[512,128]{1,0:T(8,128)} custom-call(s32[7]{0:T(128)} %stack.54.s_ref.refs_0_, f32[2,64,8,8,128]{4,3,2,1,0:T(8,128)} %get-tuple-element.23.refs_1_, f32[2,64,8,8,128]{4,3,2,1,0:T(8,128)} %get-tuple-element.24.refs_2_, f32[2,64,8,8,128]{4,3,2,1,0:T(8,128)} %get-tuple-element.31.refs_3_, f32[32,4,8,128]{3,2,1,0:T(8,128)} %get-tuple-element.32.refs_4_, ...), custom_call_target="tpu_custom_call" | custom-call | tf_op jit(solution)/shard_map/last/pallas_call | solution.py:699
  (68 shorter events, 1.8 us)
Async XLA Ops:
  3.2 9.5 %collective-permute-start.2 = (f32[33,8,128]{2,1,0:T(8,128)}, f32[33,8,128]{2,1,0:T(8,128)S(1)}, u32[]{:S(2)}, u32[]{:S(2)}) collective-permute-start(f32[33,8,128]{2,1,0:T(8,128)} %get-tuple-element.21), channel_id=1, source_target_pairs={{1,2},{3,4},{5,6},{7,8},{9,10},{11,12},{13,14},{2,1},{4,3},{6,5},{... | collective-permute-start | bytes 405512 | tf_op jit(solution)/shard_map/ppermute | solution.py:636
  8.3 5.3 %collective-permute-start.3 = (f32[33,8,128]{2,1,0:T(8,128)}, f32[33,8,128]{2,1,0:T(8,128)S(1)}, u32[]{:S(2)}, u32[]{:S(2)}) collective-permute-start(f32[33,8,128]{2,1,0:T(8,128)} %get-tuple-element.22), channel_id=1, source_target_pairs={{0,1},{2,3},{4,5},{6,7},{8,9},{10,11},{12,13},{14,15},{1,0},{3,2},... | collective-permute-start | bytes 405512 | tf_op jit(solution)/shard_map/ppermute | solution.py:637
  8.4 11.3 %collective-permute-start.1 = (f32[2,33,8,128]{3,2,1,0:T(8,128)}, f32[2,33,8,128]{3,2,1,0:T(8,128)S(1)}, u32[]{:S(2)}, u32[]{:S(2)}) collective-permute-start(f32[2,33,8,128]{3,2,1,0:T(8,128)} %get-tuple-element.20.refs_1_), channel_id=1, source_target_pairs={{0,96},{16,112},{32,0},{48,16},{64,32},{80,48},{96,64},{112,80},{1... | collective-permute-start | bytes 811016 | tf_op jit(solution)/shard_map/ppermute | solution.py:655
  12.5 10.6 %collective-permute-start = (f32[2,33,8,128]{3,2,1,0:T(8,128)}, f32[2,33,8,128]{3,2,1,0:T(8,128)S(1)}, u32[]{:S(2)}, u32[]{:S(2)}) collective-permute-start(f32[2,33,8,128]{3,2,1,0:T(8,128)} %get-tuple-element.20.refs_1_), channel_id=1, source_target_pairs={{0,32},{16,48},{32,64},{48,80},{64,96},{80,112},{96,0},{112,16},{1... | collective-permute-start | bytes 811016 | tf_op jit(solution)/shard_map/ppermute | solution.py:654
  13.7 23.7 %copy-start = (f32[2,33,8,128]{3,2,1,0:T(8,128)}, f32[2,33,8,128]{3,2,1,0:T(8,128)S(1)}, u32[]{:S(2)}) copy-start(f32[2,33,8,128]{3,2,1,0:T(8,128)S(1)} %pad_maximum_fusion.refs_4_) | copy-start | bytes 811012
  13.7 10.3 %collective-permute-start.5 = (f32[2,33,8,128]{3,2,1,0:T(8,128)S(1)}, f32[2,33,8,128]{3,2,1,0:T(8,128)S(1)}, u32[]{:S(2)}, u32[]{:S(2)}) collective-permute-start(f32[2,33,8,128]{3,2,1,0:T(8,128)S(1)} %pad_maximum_fusion.refs_4_), channel_id=1, source_target_pairs={{0,96},{16,112},{32,0},{48,16},{64,32},{80,48},{96,64},{112,80},{1... | collective-permute-start | bytes 811016 | tf_op jit(solution)/shard_map/ppermute | solution.py:655
  17.8 10.0 %collective-permute-start.4 = (f32[2,33,8,128]{3,2,1,0:T(8,128)S(1)}, f32[2,33,8,128]{3,2,1,0:T(8,128)S(1)}, u32[]{:S(2)}, u32[]{:S(2)}) collective-permute-start(f32[2,33,8,128]{3,2,1,0:T(8,128)S(1)} %pad_maximum_fusion.refs_4_), channel_id=1, source_target_pairs={{0,32},{16,48},{32,64},{48,80},{64,96},{80,112},{96,0},{112,16},{1... | collective-permute-start | bytes 811016 | tf_op jit(solution)/shard_map/ppermute | solution.py:654
  17.9 10.1 %collective-permute-start.8 = (f32[2,33,8,128]{3,2,1,0:T(8,128)}, f32[2,33,8,128]{3,2,1,0:T(8,128)S(1)}, u32[]{:S(2)}, u32[]{:S(2)}) collective-permute-start(f32[2,33,8,128]{3,2,1,0:T(8,128)} %get-tuple-element.20.refs_1_), channel_id=1, source_target_pairs={{0,16},{16,0},{32,48},{48,32},{64,80},{80,64},{96,112},{112,96},{1... | collective-permute-start | bytes 811016 | tf_op jit(solution)/shard_map/ppermute | solution.py:659
  19.8 17.7 %copy-start.1 = (f32[2,33,8,128]{3,2,1,0:T(8,128)}, f32[2,33,8,128]{3,2,1,0:T(8,128)S(1)}, u32[]{:S(2)}) copy-start(f32[2,33,8,128]{3,2,1,0:T(8,128)S(1)} %collective-permute-done.1.refs_3_) | copy-start | bytes 811012
  19.8 8.3 %collective-permute-start.11 = (f32[2,33,8,128]{3,2,1,0:T(8,128)S(1)}, f32[2,33,8,128]{3,2,1,0:T(8,128)S(1)}, u32[]{:S(2)}, u32[]{:S(2)}) collective-permute-start(f32[2,33,8,128]{3,2,1,0:T(8,128)S(1)} %pad_maximum_fusion.refs_4_), channel_id=1, source_target_pairs={{0,16},{16,0},{32,48},{48,32},{64,80},{80,64},{96,112},{112,96},{1... | collective-permute-start | bytes 811016 | tf_op jit(solution)/shard_map/ppermute | solution.py:659
  23.1 14.3 %copy-start.2 = (f32[2,33,8,128]{3,2,1,0:T(8,128)}, f32[2,33,8,128]{3,2,1,0:T(8,128)S(1)}, u32[]{:S(2)}) copy-start(f32[2,33,8,128]{3,2,1,0:T(8,128)S(1)} %collective-permute-done.refs_2_) | copy-start | bytes 811012
  23.1 5.4 %collective-permute-start.10 = (f32[2,33,8,128]{3,2,1,0:T(8,128)S(1)}, f32[2,33,8,128]{3,2,1,0:T(8,128)S(1)}, u32[]{:S(2)}, u32[]{:S(2)}) collective-permute-start(f32[2,33,8,128]{3,2,1,0:T(8,128)S(1)} %collective-permute-done.1.refs_3_), channel_id=1, source_target_pairs={{0,16},{16,0},{32,48},{48,32},{64,80},{80,64},{96,112},{112,96},{1... | collective-permute-start | bytes 811016 | tf_op jit(solution)/shard_map/ppermute | solution.py:659
  24.0 13.5 %copy-start.3 = (f32[2,33,8,128]{3,2,1,0:T(8,128)}, f32[2,33,8,128]{3,2,1,0:T(8,128)S(1)}, u32[]{:S(2)}) copy-start(f32[2,33,8,128]{3,2,1,0:T(8,128)S(1)} %collective-permute-done.5.refs_6_) | copy-start | bytes 811012
  24.1 8.3 %collective-permute-start.7 = (f32[2,33,8,128]{3,2,1,0:T(8,128)S(1)}, f32[2,33,8,128]{3,2,1,0:T(8,128)S(1)}, u32[]{:S(2)}, u32[]{:S(2)}) collective-permute-start(f32[2,33,8,128]{3,2,1,0:T(8,128)S(1)} %pad_maximum_fusion.2), channel_id=1, source_target_pairs={{0,96},{16,112},{32,0},{48,16},{64,32},{80,48},{96,64},{112,80},{1... | collective-permute-start | bytes 811016 | tf_op jit(solution)/shard_map/ppermute | solution.py:668
  27.9 8.0 %collective-permute-start.6 = (f32[2,33,8,128]{3,2,1,0:T(8,128)S(1)}, f32[2,33,8,128]{3,2,1,0:T(8,128)S(1)}, u32[]{:S(2)}, u32[]{:S(2)}) collective-permute-start(f32[2,33,8,128]{3,2,1,0:T(8,128)S(1)} %pad_maximum_fusion.1), channel_id=1, source_target_pairs={{0,32},{16,48},{32,64},{48,80},{64,96},{80,112},{96,0},{112,16},{1... | collective-permute-start | bytes 811016 | tf_op jit(solution)/shard_map/ppermute | solution.py:667
  28.0 7.9 %collective-permute-start.9 = (f32[2,33,8,128]{3,2,1,0:T(8,128)S(1)}, f32[2,33,8,128]{3,2,1,0:T(8,128)S(1)}, u32[]{:S(2)}, u32[]{:S(2)}) collective-permute-start(f32[2,33,8,128]{3,2,1,0:T(8,128)S(1)} %collective-permute-done.refs_2_), channel_id=1, source_target_pairs={{0,16},{16,0},{32,48},{48,32},{64,80},{80,64},{96,112},{112,96},{1... | collective-permute-start | bytes 811016 | tf_op jit(solution)/shard_map/ppermute | solution.py:659
  28.1 7.8 %collective-permute-start.13 = (f32[2,33,8,128]{3,2,1,0:T(8,128)S(1)}, f32[2,33,8,128]{3,2,1,0:T(8,128)S(1)}, u32[]{:S(2)}, u32[]{:S(2)}) collective-permute-start(f32[2,33,8,128]{3,2,1,0:T(8,128)S(1)} %collective-permute-done.5.refs_6_), channel_id=1, source_target_pairs={{0,16},{16,0},{32,48},{48,32},{64,80},{80,64},{96,112},{112,96},{1... | collective-permute-start | bytes 811016 | tf_op jit(solution)/shard_map/ppermute | solution.py:659
  28.6 7.4 %collective-permute-start.12 = (f32[2,33,8,128]{3,2,1,0:T(8,128)S(1)}, f32[2,33,8,128]{3,2,1,0:T(8,128)S(1)}, u32[]{:S(2)}, u32[]{:S(2)}) collective-permute-start(f32[2,33,8,128]{3,2,1,0:T(8,128)S(1)} %collective-permute-done.4.refs_5_), channel_id=1, source_target_pairs={{0,16},{16,0},{32,48},{48,32},{64,80},{80,64},{96,112},{112,96},{1... | collective-permute-start | bytes 811016 | tf_op jit(solution)/shard_map/ppermute | solution.py:659
  32.4 3.6 %collective-permute-start.15 = (f32[2,33,8,128]{3,2,1,0:T(8,128)S(1)}, f32[2,33,8,128]{3,2,1,0:T(8,128)S(1)}, u32[]{:S(2)}, u32[]{:S(2)}) collective-permute-start(f32[2,33,8,128]{3,2,1,0:T(8,128)S(1)} %collective-permute-done.7.refs_8_), channel_id=1, source_target_pairs={{0,16},{16,0},{32,48},{48,32},{64,80},{80,64},{96,112},{112,96},{1... | collective-permute-start | bytes 811016 | tf_op jit(solution)/shard_map/ppermute | solution.py:659
  35.9 1.5 %collective-permute-start.14 = (f32[2,33,8,128]{3,2,1,0:T(8,128)S(1)}, f32[2,33,8,128]{3,2,1,0:T(8,128)S(1)}, u32[]{:S(2)}, u32[]{:S(2)}) collective-permute-start(f32[2,33,8,128]{3,2,1,0:T(8,128)S(1)} %collective-permute-done.6.refs_7_), channel_id=1, source_target_pairs={{0,16},{16,0},{32,48},{48,32},{64,80},{80,64},{96,112},{112,96},{1... | collective-permute-start | bytes 811016 | tf_op jit(solution)/shard_map/ppermute | solution.py:659
  55.0 8.5 %collective-permute-start.17 = (f32[8,2,8,128]{3,2,1,0:T(8,128)}, f32[8,2,8,128]{3,2,1,0:T(8,128)S(1)}, u32[]{:S(2)}, u32[]{:S(2)}) collective-permute-start(f32[8,2,8,128]{3,2,1,0:T(8,128)} %get-tuple-element.30.refs_8_.refs_10_), channel_id=1, source_target_pairs={{1,2},{3,4},{5,6},{7,8},{9,10},{11,12},{13,14},{2,1},{4,3},{6,5},{... | collective-permute-start | bytes 196616 | tf_op jit(solution)/shard_map/ppermute | solution.py:636
  57.6 5.9 %collective-permute-start.16 = (f32[8,2,8,128]{3,2,1,0:T(8,128)}, f32[8,2,8,128]{3,2,1,0:T(8,128)S(1)}, u32[]{:S(2)}, u32[]{:S(2)}) collective-permute-start(f32[8,2,8,128]{3,2,1,0:T(8,128)} %get-tuple-element.30.refs_8_.refs_10_), channel_id=1, source_target_pairs={{0,1},{2,3},{4,5},{6,7},{8,9},{10,11},{12,13},{14,15},{1,0},{3,2},... | collective-permute-start | bytes 196616 | tf_op jit(solution)/shard_map/ppermute | solution.py:637
  90.7 8.1 %collective-permute-start.19 = (f32[4,2,8,128]{3,2,1,0:T(8,128)}, f32[4,2,8,128]{3,2,1,0:T(8,128)S(1)}, u32[]{:S(2)}, u32[]{:S(2)}) collective-permute-start(f32[4,2,8,128]{3,2,1,0:T(8,128)} %get-tuple-element.34.refs_7_), channel_id=1, source_target_pairs={{1,2},{3,4},{5,6},{7,8},{9,10},{11,12},{13,14},{2,1},{4,3},{6,5},{... | collective-permute-start | bytes 98312 | tf_op jit(solution)/shard_map/ppermute | solution.py:636
  94.9 4.2 %collective-permute-start.18 = (f32[4,2,8,128]{3,2,1,0:T(8,128)}, f32[4,2,8,128]{3,2,1,0:T(8,128)S(1)}, u32[]{:S(2)}, u32[]{:S(2)}) collective-permute-start(f32[4,2,8,128]{3,2,1,0:T(8,128)} %get-tuple-element.34.refs_7_), channel_id=1, source_target_pairs={{0,1},{2,3},{4,5},{6,7},{8,9},{10,11},{12,13},{14,15},{1,0},{3,2},... | collective-permute-start | bytes 98312 | tf_op jit(solution)/shard_map/ppermute | solution.py:637
  (15 other events, 53.9 us)

commit v5 on v4

--- a/solution.py
+++ b/solution.py
@@ -16,7 +16,7 @@
 LAYERS = 64
 TILE_ROWS = 8
 WINDOW = 16
-VMEM_LIMIT = 56 * 1024 * 1024
+VMEM_LIMIT = 40 * 1024 * 1024
 
 D_AIR = 6.0
 D_TERRAIN = 6.0 + TERRAIN_PENALTY
@@ -113,46 +113,14 @@
         ).astype(F32)
         return layer < self.height[h, row][None]
 
-    def relax(self, src, dst, start, rows, group, together=1):
-        sub = lax.broadcasted_iota(jnp.int32, (1, SUB, LANES), 1)
-
-        def body(first, count):
-            for z in (0, 4):
-                chunk = pl.ds(z, 4)
-
-                def load(row):
-                    return [src[h, row + 1, chunk] for h in range(2)]
-
-                before, centre = load(first - 1), load(first)
-                pending = []
-                for k in range(count):
-                    row = first + k
-                    after = load(row + 1)
-                    sides = column_sum(centre)
-                    for h, v in enumerate(centre):
-                        if z == 0:
-                            below = pltpu.roll(src[h, row + 1, pl.ds(7, 1)], 1, axis=1)
-                            below = jnp.where(sub == 0, 0.0, below)
-                            above = src[h, row + 1, pl.ds(4, 1)]
-                        else:
-                            below = src[h, row + 1, pl.ds(3, 1)]
-                            above = pltpu.roll(src[h, row + 1, pl.ds(0, 1)], SUB - 1, axis=1)
-                            above = jnp.where(sub == SUB - 1, 0.0, above)
-                        total = before[h] + after[h] + sides[h]
-                        total = total + (
-                            jnp.concatenate([below, v[:-1]], axis=0)
-                            + jnp.concatenate([v[1:], above], axis=0)
-                        )
-                        total = total + self.source[h, row, chunk]
-                        new = (1.0 - RELAX_WEIGHT) * v + self.weight[h, row, chunk] * total
-                        pending.append((h, row, new))
-                    before, centre = centre, after
-                    if (k + 1) % together == 0 or k == count - 1:
-                        for h, row, new in pending:
-                            dst[h, row + 1, chunk] = new
-                        pending = []
-
-        over_rows(start, rows, group, body)
+    def relax(self, src, dst, start, rows, group):
+        def emit(row, pairs):
+            for h, (v, total) in enumerate(pairs):
+                total = total + self.source[h, row]
+                dst[h, row + 1] = (1.0 - RELAX_WEIGHT) * v + self.weight[h, row] * total
+
+        over_rows(start, rows, group,
+                  lambda first, count: stencil_group(self.loader(src), first, count, emit))
 
     def restricted_defect(self, src, rows, out):
         load = self.loader(src)
@@ -414,7 +382,7 @@
     at = Place(s_ref)
     tiles, refs = refs[:16], refs[16:]
     (u0, source_out, weight_out, height_out, u1, b1, sh1, packed,
-     source, weight, height, own, beside, heights, va0, vb0, va1, vb1, w1, sems) = refs
+     source, weight, height, va0, vb0, va1, vb1, w1, sems) = refs
     has_left, has_right = at.has_left, at.has_right
     chips = rows // (2 * TILE_ROWS)
     z, core = at.chip, at.core
@@ -422,32 +390,10 @@
     def device(step, other):
         return 2 * lax.rem(z + step + chips, chips) + (1 - core if other else core)
 
-    copies = []
-
-    def start_copy(source_ref, target_ref):
-        copies.append(pltpu.make_async_copy(source_ref, target_ref, sems.at[len(copies)]))
-
-    for other in range(2):
-        group = tiles[8 * other:8 * other + 8]
-        for kind in range(2):
-            pieces = [
-                (group[3 * kind + n].at[part], device(step, other), part)
-                for n, step in enumerate((0, -1, 1)) for part in range(2)
-            ]
-            pieces += [(group[6 + part].at[kind], device(2, other), part) for part in range(2)]
-            for ref, dev, part in pieces:
-                target = own.at[2 * dev + part] if kind == 0 else beside.at[part, dev]
-                start_copy(ref.at[pl.ds(0, 32)], target)
-                if part == 0:
-                    start_copy(ref.at[32], heights.at[kind, dev])
-    for copy in copies:
-        copy.start()
     for ref in (va0, vb0):
         zero_rim(ref, rows, 2)
     for ref in (va1, vb1):
         zero_rim(ref, rows // 2, 1)
-    for copy in copies:
-        copy.wait()
 
     edge = edge_mask(0, has_left, has_right)
     fine = Fine(source, weight, height)
@@ -461,14 +407,14 @@
 
     first = first_columns((4, SUB, LANES))
 
-    def assemble(dev, carry):
-        tall = halves(heights[0, dev], heights[1, dev], low[0])
+    def assemble(dev, mine, side):
+        tall = halves(mine(0)[32], side(0)[32], low[0])
         for r in range(TILE_ROWS):
             row = TILE_ROWS * dev + r
-            upper = beside[1, dev, pl.ds(4 * r, 4)]
+            upper = side(1)[pl.ds(4 * r, 4)]
             upper = jnp.where(first, pltpu.roll(upper, 96, axis=2), pltpu.roll(upper, 32, axis=2))
-            side = jnp.concatenate([beside[0, dev, pl.ds(4 * r, 4)], upper], axis=0)
-            both = halves(own[2 * dev + r // 4, pl.ds(8 * (r % 4), 8)], side, low)
+            beside = jnp.concatenate([side(0)[pl.ds(4 * r, 4)], upper], axis=0)
+            both = halves(mine(r // 4)[pl.ds(8 * (r % 4), 8)], beside, low)
             for h in range(2):
                 source[h, row] = both[h]
                 height[h, row] = jnp.broadcast_to(tall[h][r:r + 1], (SUB, LANES))
@@ -477,9 +423,14 @@
                 )
                 weight[h, row] = now
                 va0[h, row + 1] = now * both[h]
-        return carry
-
-    lax.fori_loop(0, rows // TILE_ROWS, assemble, 0)
+
+    for other in range(2):
+        group = tiles[8 * other:8 * other + 8]
+        for n, step in enumerate((0, -1, 1)):
+            assemble(device(step, other), lambda part: group[n].at[part],
+                     lambda part: group[3 + n].at[part])
+        assemble(device(2, other), lambda part: group[6 + part].at[0],
+                 lambda part: group[6 + part].at[1])
     saves = [
         pltpu.make_async_copy(source, source_out, sems.at[1]),
         pltpu.make_async_copy(weight, weight_out, sems.at[2]),
@@ -488,9 +439,9 @@
     for save in saves:
         save.start()
     fine.coarse_shift(rows, sh1)
-    fine.relax(va0, vb0, 0, rows, 8, 4)
-    fine.relax(vb0, va0, 0, rows, 8, 4)
-    fine.relax(va0, vb0, 0, rows, 8, 4)
+    fine.relax(va0, vb0, 0, rows, 8)
+    fine.relax(vb0, va0, 0, rows, 8)
+    fine.relax(va0, vb0, 0, rows, 8)
     saves.append(pltpu.make_async_copy(interior(vb0, rows), u0, sems.at[0]))
     saves[-1].start()
     fine.restricted_defect(vb0, rows, b1)
@@ -677,10 +628,9 @@
         lambda *refs: down_kernel(rows, *refs),
         out_shape=(level_0, level_0, level_0, shape(2, rows), level_1, level_1, level_1,
                    shape(2 * each, 2)),
-        in_specs=[smem] + [hbm] * 16, out_specs=(hbm,) * 4 + (spec(),) * 4,
-        scratch_shapes=[vmem(2, rows, 8), vmem(2, rows, 8), vmem(2, rows),
-                        vmem(2 * gx, 32), vmem(2, gx, 32), vmem(2, gx)]
-        + fine_rows + level_1_scratch(rows) + [pltpu.SemaphoreType.DMA((48,))],
+        in_specs=[smem] + [spec()] * 16, out_specs=(hbm,) * 4 + (spec(),) * 4,
+        scratch_shapes=[vmem(2, rows, 8), vmem(2, rows, 8), vmem(2, rows)]
+        + fine_rows + level_1_scratch(rows) + [pltpu.SemaphoreType.DMA((4,))],
         compiler_params=params(), name="down",
     )(scalars, *tiles)
 

time: 108 us -> 107 us (level)
  Pallas kernels: 53.8 us -> 49 us
  local copies, waits for them, and re-layouts: 2.74 us -> 6.42 us
    unnamed x38 -> x10, local copies, waits for them, and re-layouts: 2.03 us -> 5.76 us
    pallas_call x1, Pallas kernels: 26.5 us -> 23.8 us  [per_device(): pl.pallas_call(lambda *refs: middle_kernel(rows, *refs), out_shape=(level...]
    pallas_call x1, Pallas kernels: 16.7 us -> 15.3 us  [per_device(): pl.pallas_call(lambda *refs: down_kernel(rows, *refs), out_shape=(level_0...]
where the time goes in v5:
time: 107 us; the launch traced here: 106 us
  Pallas kernels  49 us (46%)
  starting transfers between devices  25.8 us (24%)
  waiting for transfers between devices  24.6 us (23%)
  local copies, waits for them, and re-layouts  6.42 us (6%)
    pallas_call x1, Pallas kernels, per_device(): pl.pallas_call(lambda *refs: middle_kernel(rows, *refs), out_shape=(level...  23.8 us
    pallas_call x1, Pallas kernels, per_device(): pl.pallas_call(lambda *refs: down_kernel(rows, *refs), out_shape=(level_0...  15.3 us
    ppermute x3, starting transfers between devices, exchange(): first = lax.ppermute(first_out, 'gy', swaps(1))  12 us
    ppermute x3, waiting for transfers between devices, exchange(): first = lax.ppermute(first_out, 'gy', swaps(1))  8.44 us
    ppermute x2, starting transfers between devices, gather_near(): above = lax.ppermute(tile, 'gx', down)  8.21 us
    pallas_call x1, Pallas kernels, per_device(): pl.pallas_call(lambda *refs: last_kernel(rows, *refs), out_shape=jax.Shap...  7.34 us
    unnamed x10, local copies, waits for them, and re-layouts  5.76 us
    ppermute x1, starting transfers between devices, per_device(): lax.ppermute(jnp.stack([own_near[1][1], halo_near[1][1]]), 'gx', down)  3.76 us
  transfers between devices with their start and end apart: 20, of which 11 were waited for; matrix products, arithmetic and copies ran while one was open for 0% of the time, Pallas kernels for 0%

profile of v5, /device:TPU:6, one launch (start us, length us, event | category | flops | bytes accessed | tf_op | source)
XLA Modules:
  0.0 106.3 jit_solution(11794484180241684614)
XLA Ops:
  0.0 0.6 stack.54.s_ref.refs_0_
  0.6 2.5 %pack.1 = (f32[2,33,8,128]{3,2,1,0:T(8,128)}, f32[33,8,128]{2,1,0:T(8,128)}, f32[33,8,128]{2,1,0:T(8,128)}) custom-call(s32[7]{0:T(128)} %stack.54.s_ref.refs_0_, f32[512,128]{1,0:T(8,128)} %bitcast.14, s32[512,128]{1,0:T(8,128)} %bitcast.15), custom_call_target="tpu_custom_call" | custom-call | tf_op jit(solution)/shard_map/pack/pallas_call | solution.py:593
  3.1 5.2 %collective-permute-start.2 = (f32[33,8,128]{2,1,0:T(8,128)}, f32[33,8,128]{2,1,0:T(8,128)S(1)}, u32[]{:S(2)}, u32[]{:S(2)}) collective-permute-start(f32[33,8,128]{2,1,0:T(8,128)} %get-tuple-element.21), channel_id=1, source_target_pairs={{1,2},{3,4},{5,6},{7,8},{9,10},{11,12},{13,14},{2,1},{4,3},{6,5},{... | collective-permute-start | bytes 405512 | tf_op jit(solution)/shard_map/ppermute | solution.py:587
  8.4 4.1 %collective-permute-start.1 = (f32[2,33,8,128]{3,2,1,0:T(8,128)}, f32[2,33,8,128]{3,2,1,0:T(8,128)S(1)}, u32[]{:S(2)}, u32[]{:S(2)}) collective-permute-start(f32[2,33,8,128]{3,2,1,0:T(8,128)} %get-tuple-element.20.refs_1_), channel_id=1, source_target_pairs={{0,96},{16,112},{32,0},{48,16},{64,32},{80,48},{96,64},{112,80},{1... | collective-permute-start | bytes 811016 | tf_op jit(solution)/shard_map/ppermute | solution.py:606
  12.6 1.0 collective-permute-done.3
  13.7 4.1 %collective-permute-start.5 = (f32[2,33,8,128]{3,2,1,0:T(8,128)S(1)}, f32[2,33,8,128]{3,2,1,0:T(8,128)S(1)}, u32[]{:S(2)}, u32[]{:S(2)}) collective-permute-start(f32[2,33,8,128]{3,2,1,0:T(8,128)S(1)} %pad_maximum_fusion.refs_4_), channel_id=1, source_target_pairs={{0,96},{16,112},{32,0},{48,16},{64,32},{80,48},{96,64},{112,80},{1... | collective-permute-start | bytes 811016 | tf_op jit(solution)/shard_map/ppermute | solution.py:606
  17.8 1.9 %collective-permute-done.1.refs_3_ = f32[2,33,8,128]{3,2,1,0:T(8,128)S(1)} collective-permute-done((f32[2,33,8,128]{3,2,1,0:T(8,128)}, f32[2,33,8,128]{3,2,1,0:T(8,128)S(1)}, u32[]{:S(2)}, u32[]{:S(2)}) %collective-permute-start.1) | collective-permute-done | bytes 270368 | tf_op jit(solution)/shard_map/ppermute | solution.py:606
  19.8 3.3 %collective-permute-done.refs_2_ = f32[2,33,8,128]{3,2,1,0:T(8,128)S(1)} collective-permute-done((f32[2,33,8,128]{3,2,1,0:T(8,128)}, f32[2,33,8,128]{3,2,1,0:T(8,128)S(1)}, u32[]{:S(2)}, u32[]{:S(2)}) %collective-permute-start) | collective-permute-done | bytes 270368 | tf_op jit(solution)/shard_map/ppermute | solution.py:605
  23.1 0.8 collective-permute-done.5.refs_6_
  24.0 3.8 %collective-permute-start.7 = (f32[2,33,8,128]{3,2,1,0:T(8,128)S(1)}, f32[2,33,8,128]{3,2,1,0:T(8,128)S(1)}, u32[]{:S(2)}, u32[]{:S(2)}) collective-permute-start(f32[2,33,8,128]{3,2,1,0:T(8,128)S(1)} %pad_maximum_fusion.2), channel_id=1, source_target_pairs={{0,96},{16,112},{32,0},{48,16},{64,32},{80,48},{96,64},{112,80},{1... | collective-permute-start | bytes 811016 | tf_op jit(solution)/shard_map/ppermute | solution.py:619
  28.6 3.7 %collective-permute-done.7.refs_8_ = f32[2,33,8,128]{3,2,1,0:T(8,128)S(1)} collective-permute-done((f32[2,33,8,128]{3,2,1,0:T(8,128)S(1)}, f32[2,33,8,128]{3,2,1,0:T(8,128)S(1)}, u32[]{:S(2)}, u32[]{:S(2)}) %collective-permute-start.7) | collective-permute-done | bytes 270368 | tf_op jit(solution)/shard_map/ppermute | solution.py:619
  32.3 3.5 %collective-permute-done.6.refs_7_ = f32[2,33,8,128]{3,2,1,0:T(8,128)S(1)} collective-permute-done((f32[2,33,8,128]{3,2,1,0:T(8,128)S(1)}, f32[2,33,8,128]{3,2,1,0:T(8,128)S(1)}, u32[]{:S(2)}, u32[]{:S(2)}) %collective-permute-start.6) | collective-permute-done | bytes 270368 | tf_op jit(solution)/shard_map/ppermute | solution.py:618
  35.9 1.5 %collective-permute-done.14.refs_15_ = f32[2,33,8,128]{3,2,1,0:T(8,128)S(1)} collective-permute-done((f32[2,33,8,128]{3,2,1,0:T(8,128)S(1)}, f32[2,33,8,128]{3,2,1,0:T(8,128)S(1)}, u32[]{:S(2)}, u32[]{:S(2)}) %collective-permute-start.14) | collective-permute-done | bytes 270368 | tf_op jit(solution)/shard_map/ppermute | solution.py:610
  37.4 1.0 copy-done.3
  39.0 15.3 %down.1 = (f32[2,64,8,8,128]{4,3,2,1,0:T(8,128)S(1)}, f32[2,64,8,8,128]{4,3,2,1,0:T(8,128)}, f32[2,64,8,8,128]{4,3,2,1,0:T(8,128)}, f32[2,64,8,128]{3,2,1,0:T(8,...) custom-call(s32[7]{0:T(128)S(1)} %copy-done.4, ...), custom_call_target="tpu_custom_call" | custom-call | tf_op jit(solution)/shard_map/down/pallas_call | solution.py:627
  54.4 2.0 %copy-done.2 = f32[2,64,8,8,128]{4,3,2,1,0:T(8,128)} copy-done((f32[2,64,8,8,128]{4,3,2,1,0:T(8,128)}, f32[2,64,8,8,128]{4,3,2,1,0:T(8,128)S(1)}, u32[]{:S(2)}) %copy-start.2) | copy-done | bytes 4194328
  56.3 2.6 %collective-permute-start.17 = (f32[8,2,8,128]{3,2,1,0:T(8,128)S(1)}, f32[8,2,8,128]{3,2,1,0:T(8,128)S(1)}, u32[]{:S(2)}, u32[]{:S(2)}) collective-permute-start(f32[8,2,8,128]{3,2,1,0:T(8,128)S(1)} %get-tuple-element.30.refs_8_.refs_10_), channel_id=1, source_target_pairs={{1,2},{3,4},{5,6},{7,8},{9,10},{11,12},{13,14},{2,1},{4,3},{6,5},{... | collective-permute-start | bytes 196616 | tf_op jit(solution)/shard_map/ppermute | solution.py:587
  58.9 0.9 collective-permute-start.16
  59.9 4.7 %collective-permute-done.17.refs_10_.refs_12_ = f32[8,2,8,128]{3,2,1,0:T(8,128)S(1)} collective-permute-done((f32[8,2,8,128]{3,2,1,0:T(8,128)S(1)}, f32[8,2,8,128]{3,2,1,0:T(8,128)S(1)}, u32[]{:S(2)}, u32[]{:S(2)}) %collective-permute-start.17) | collective-permute-done | bytes 65568 | tf_op jit(solution)/shard_map/ppermute | solution.py:587
  64.6 2.2 %copy-done = f32[2,64,8,8,128]{4,3,2,1,0:T(8,128)S(1)} copy-done((f32[2,64,8,8,128]{4,3,2,1,0:T(8,128)S(1)}, f32[2,64,8,8,128]{4,3,2,1,0:T(8,128)}, u32[]{:S(2)}) %copy-start) | copy-done | bytes 4194328
  66.8 23.8 %middle.1 = (f32[2,64,8,8,128]{4,3,2,1,0:T(8,128)S(1)}, f32[32,4,8,128]{3,2,1,0:T(8,128)S(1)}, f32[32,4,8,128]{3,2,1,0:T(8,128)S(1)}, f32[4,2,8,128]{3,2,1,0:T(8,128)S(1)}) custom-call(s32[7]{0:T(128)S(1)} %copy-done.4, f32[2,64,8,8,128]{4,3,2,1,0:T(8,128)S(1)} %copy-done, f32[2,64,8,8,128]{4,3,2,1,0:T(8,128)} %get-tuple-element.24.refs_2_, ...), custom_call_target="tpu_custom_call" | custom-call | tf_op jit(solution)/shard_map/middle/pallas_call | solution.py:638
  90.6 4.2 %collective-permute-start.19 = (f32[4,2,8,128]{3,2,1,0:T(8,128)S(1)}, f32[4,2,8,128]{3,2,1,0:T(8,128)S(1)}, u32[]{:S(2)}, u32[]{:S(2)}) collective-permute-start(f32[4,2,8,128]{3,2,1,0:T(8,128)S(1)} %get-tuple-element.34.refs_7_), channel_id=1, source_target_pairs={{1,2},{3,4},{5,6},{7,8},{9,10},{11,12},{13,14},{2,1},{4,3},{6,5},{... | collective-permute-start | bytes 98312 | tf_op jit(solution)/shard_map/ppermute | solution.py:587
  94.9 3.6 %collective-permute-done.19.refs_9_ = f32[4,2,8,128]{3,2,1,0:T(8,128)S(1)} collective-permute-done((f32[4,2,8,128]{3,2,1,0:T(8,128)S(1)}, f32[4,2,8,128]{3,2,1,0:T(8,128)S(1)}, u32[]{:S(2)}, u32[]{:S(2)}) %collective-permute-start.19) | collective-permute-done | bytes 32800 | tf_op jit(solution)/shard_map/ppermute | solution.py:587
  98.8 7.3 %last.1 = f32[512,128]{1,0:T(8,128)} custom-call(s32[7]{0:T(128)S(1)} %copy-done.4, f32[2,64,8,8,128]{4,3,2,1,0:T(8,128)S(1)} %copy-done, f32[2,64,8,8,128]{4,3,2,1,0:T(8,128)S(1)} %copy-done.1, f32[2,64,8,8,128]{4,3,2,1,0:T(8,128)S(1)} %get-tuple-element.31.refs_3_, f32[32,4,8,128]{3,2,1,0:T(8,128)S(1)} %get-tuple-element.32.refs_4_, ...), custom_call_target="tpu_custom_call" | custom-call | tf_op jit(solution)/shard_map/last/pallas_call | solution.py:649
  (40 shorter events, 2.2 us)
Async XLA Ops:
  3.1 9.5 %collective-permute-start.2 = (f32[33,8,128]{2,1,0:T(8,128)}, f32[33,8,128]{2,1,0:T(8,128)S(1)}, u32[]{:S(2)}, u32[]{:S(2)}) collective-permute-start(f32[33,8,128]{2,1,0:T(8,128)} %get-tuple-element.21), channel_id=1, source_target_pairs={{1,2},{3,4},{5,6},{7,8},{9,10},{11,12},{13,14},{2,1},{4,3},{6,5},{... | collective-permute-start | bytes 405512 | tf_op jit(solution)/shard_map/ppermute | solution.py:587
  8.3 5.3 %collective-permute-start.3 = (f32[33,8,128]{2,1,0:T(8,128)}, f32[33,8,128]{2,1,0:T(8,128)S(1)}, u32[]{:S(2)}, u32[]{:S(2)}) collective-permute-start(f32[33,8,128]{2,1,0:T(8,128)} %get-tuple-element.22), channel_id=1, source_target_pairs={{0,1},{2,3},{4,5},{6,7},{8,9},{10,11},{12,13},{14,15},{1,0},{3,2},... | collective-permute-start | bytes 405512 | tf_op jit(solution)/shard_map/ppermute | solution.py:588
  8.4 11.3 %collective-permute-start.1 = (f32[2,33,8,128]{3,2,1,0:T(8,128)}, f32[2,33,8,128]{3,2,1,0:T(8,128)S(1)}, u32[]{:S(2)}, u32[]{:S(2)}) collective-permute-start(f32[2,33,8,128]{3,2,1,0:T(8,128)} %get-tuple-element.20.refs_1_), channel_id=1, source_target_pairs={{0,96},{16,112},{32,0},{48,16},{64,32},{80,48},{96,64},{112,80},{1... | collective-permute-start | bytes 811016 | tf_op jit(solution)/shard_map/ppermute | solution.py:606
  12.5 10.6 %collective-permute-start = (f32[2,33,8,128]{3,2,1,0:T(8,128)}, f32[2,33,8,128]{3,2,1,0:T(8,128)S(1)}, u32[]{:S(2)}, u32[]{:S(2)}) collective-permute-start(f32[2,33,8,128]{3,2,1,0:T(8,128)} %get-tuple-element.20.refs_1_), channel_id=1, source_target_pairs={{0,32},{16,48},{32,64},{48,80},{64,96},{80,112},{96,0},{112,16},{1... | collective-permute-start | bytes 811016 | tf_op jit(solution)/shard_map/ppermute | solution.py:605
  13.7 10.3 %collective-permute-start.5 = (f32[2,33,8,128]{3,2,1,0:T(8,128)S(1)}, f32[2,33,8,128]{3,2,1,0:T(8,128)S(1)}, u32[]{:S(2)}, u32[]{:S(2)}) collective-permute-start(f32[2,33,8,128]{3,2,1,0:T(8,128)S(1)} %pad_maximum_fusion.refs_4_), channel_id=1, source_target_pairs={{0,96},{16,112},{32,0},{48,16},{64,32},{80,48},{96,64},{112,80},{1... | collective-permute-start | bytes 811016 | tf_op jit(solution)/shard_map/ppermute | solution.py:606
  17.8 10.0 %collective-permute-start.4 = (f32[2,33,8,128]{3,2,1,0:T(8,128)S(1)}, f32[2,33,8,128]{3,2,1,0:T(8,128)S(1)}, u32[]{:S(2)}, u32[]{:S(2)}) collective-permute-start(f32[2,33,8,128]{3,2,1,0:T(8,128)S(1)} %pad_maximum_fusion.refs_4_), channel_id=1, source_target_pairs={{0,32},{16,48},{32,64},{48,80},{64,96},{80,112},{96,0},{112,16},{1... | collective-permute-start | bytes 811016 | tf_op jit(solution)/shard_map/ppermute | solution.py:605
  17.8 10.1 %collective-permute-start.8 = (f32[2,33,8,128]{3,2,1,0:T(8,128)}, f32[2,33,8,128]{3,2,1,0:T(8,128)S(1)}, u32[]{:S(2)}, u32[]{:S(2)}) collective-permute-start(f32[2,33,8,128]{3,2,1,0:T(8,128)} %get-tuple-element.20.refs_1_), channel_id=1, source_target_pairs={{0,16},{16,0},{32,48},{48,32},{64,80},{80,64},{96,112},{112,96},{1... | collective-permute-start | bytes 811016 | tf_op jit(solution)/shard_map/ppermute | solution.py:610
  19.7 8.3 %collective-permute-start.11 = (f32[2,33,8,128]{3,2,1,0:T(8,128)S(1)}, f32[2,33,8,128]{3,2,1,0:T(8,128)S(1)}, u32[]{:S(2)}, u32[]{:S(2)}) collective-permute-start(f32[2,33,8,128]{3,2,1,0:T(8,128)S(1)} %pad_maximum_fusion.refs_4_), channel_id=1, source_target_pairs={{0,16},{16,0},{32,48},{48,32},{64,80},{80,64},{96,112},{112,96},{1... | collective-permute-start | bytes 811016 | tf_op jit(solution)/shard_map/ppermute | solution.py:610
  23.1 5.4 %collective-permute-start.10 = (f32[2,33,8,128]{3,2,1,0:T(8,128)S(1)}, f32[2,33,8,128]{3,2,1,0:T(8,128)S(1)}, u32[]{:S(2)}, u32[]{:S(2)}) collective-permute-start(f32[2,33,8,128]{3,2,1,0:T(8,128)S(1)} %collective-permute-done.1.refs_3_), channel_id=1, source_target_pairs={{0,16},{16,0},{32,48},{48,32},{64,80},{80,64},{96,112},{112,96},{1... | collective-permute-start | bytes 811016 | tf_op jit(solution)/shard_map/ppermute | solution.py:610
  24.0 8.3 %collective-permute-start.7 = (f32[2,33,8,128]{3,2,1,0:T(8,128)S(1)}, f32[2,33,8,128]{3,2,1,0:T(8,128)S(1)}, u32[]{:S(2)}, u32[]{:S(2)}) collective-permute-start(f32[2,33,8,128]{3,2,1,0:T(8,128)S(1)} %pad_maximum_fusion.2), channel_id=1, source_target_pairs={{0,96},{16,112},{32,0},{48,16},{64,32},{80,48},{96,64},{112,80},{1... | collective-permute-start | bytes 811016 | tf_op jit(solution)/shard_map/ppermute | solution.py:619
  27.8 8.0 %collective-permute-start.6 = (f32[2,33,8,128]{3,2,1,0:T(8,128)S(1)}, f32[2,33,8,128]{3,2,1,0:T(8,128)S(1)}, u32[]{:S(2)}, u32[]{:S(2)}) collective-permute-start(f32[2,33,8,128]{3,2,1,0:T(8,128)S(1)} %pad_maximum_fusion.1), channel_id=1, source_target_pairs={{0,32},{16,48},{32,64},{48,80},{64,96},{80,112},{96,0},{112,16},{1... | collective-permute-start | bytes 811016 | tf_op jit(solution)/shard_map/ppermute | solution.py:618
  27.9 7.9 %collective-permute-start.9 = (f32[2,33,8,128]{3,2,1,0:T(8,128)S(1)}, f32[2,33,8,128]{3,2,1,0:T(8,128)S(1)}, u32[]{:S(2)}, u32[]{:S(2)}) collective-permute-start(f32[2,33,8,128]{3,2,1,0:T(8,128)S(1)} %collective-permute-done.refs_2_), channel_id=1, source_target_pairs={{0,16},{16,0},{32,48},{48,32},{64,80},{80,64},{96,112},{112,96},{1... | collective-permute-start | bytes 811016 | tf_op jit(solution)/shard_map/ppermute | solution.py:610
  28.0 7.8 %collective-permute-start.13 = (f32[2,33,8,128]{3,2,1,0:T(8,128)S(1)}, f32[2,33,8,128]{3,2,1,0:T(8,128)S(1)}, u32[]{:S(2)}, u32[]{:S(2)}) collective-permute-start(f32[2,33,8,128]{3,2,1,0:T(8,128)S(1)} %collective-permute-done.5.refs_6_), channel_id=1, source_target_pairs={{0,16},{16,0},{32,48},{48,32},{64,80},{80,64},{96,112},{112,96},{1... | collective-permute-start | bytes 811016 | tf_op jit(solution)/shard_map/ppermute | solution.py:610
  28.5 7.4 %collective-permute-start.12 = (f32[2,33,8,128]{3,2,1,0:T(8,128)S(1)}, f32[2,33,8,128]{3,2,1,0:T(8,128)S(1)}, u32[]{:S(2)}, u32[]{:S(2)}) collective-permute-start(f32[2,33,8,128]{3,2,1,0:T(8,128)S(1)} %collective-permute-done.4.refs_5_), channel_id=1, source_target_pairs={{0,16},{16,0},{32,48},{48,32},{64,80},{80,64},{96,112},{112,96},{1... | collective-permute-start | bytes 811016 | tf_op jit(solution)/shard_map/ppermute | solution.py:610
  32.3 3.6 %collective-permute-start.15 = (f32[2,33,8,128]{3,2,1,0:T(8,128)S(1)}, f32[2,33,8,128]{3,2,1,0:T(8,128)S(1)}, u32[]{:S(2)}, u32[]{:S(2)}) collective-permute-start(f32[2,33,8,128]{3,2,1,0:T(8,128)S(1)} %collective-permute-done.7.refs_8_), channel_id=1, source_target_pairs={{0,16},{16,0},{32,48},{48,32},{64,80},{80,64},{96,112},{112,96},{1... | collective-permute-start | bytes 811016 | tf_op jit(solution)/shard_map/ppermute | solution.py:610
  35.9 1.5 %collective-permute-start.14 = (f32[2,33,8,128]{3,2,1,0:T(8,128)S(1)}, f32[2,33,8,128]{3,2,1,0:T(8,128)S(1)}, u32[]{:S(2)}, u32[]{:S(2)}) collective-permute-start(f32[2,33,8,128]{3,2,1,0:T(8,128)S(1)} %collective-permute-done.6.refs_7_), channel_id=1, source_target_pairs={{0,16},{16,0},{32,48},{48,32},{64,80},{80,64},{96,112},{112,96},{1... | collective-permute-start | bytes 811016 | tf_op jit(solution)/shard_map/ppermute | solution.py:610
  37.4 1.0 copy-start.3
  54.3 2.0 %copy-start.2 = (f32[2,64,8,8,128]{4,3,2,1,0:T(8,128)}, f32[2,64,8,8,128]{4,3,2,1,0:T(8,128)S(1)}, u32[]{:S(2)}) copy-start(f32[2,64,8,8,128]{4,3,2,1,0:T(8,128)S(1)} %get-tuple-element.26.refs_4_) | copy-start | bytes 12582916
  56.3 8.3 %collective-permute-start.17 = (f32[8,2,8,128]{3,2,1,0:T(8,128)S(1)}, f32[8,2,8,128]{3,2,1,0:T(8,128)S(1)}, u32[]{:S(2)}, u32[]{:S(2)}) collective-permute-start(f32[8,2,8,128]{3,2,1,0:T(8,128)S(1)} %get-tuple-element.30.refs_8_.refs_10_), channel_id=1, source_target_pairs={{1,2},{3,4},{5,6},{7,8},{9,10},{11,12},{13,14},{2,1},{4,3},{6,5},{... | collective-permute-start | bytes 196616 | tf_op jit(solution)/shard_map/ppermute | solution.py:587
  58.9 5.7 %collective-permute-start.16 = (f32[8,2,8,128]{3,2,1,0:T(8,128)S(1)}, f32[8,2,8,128]{3,2,1,0:T(8,128)S(1)}, u32[]{:S(2)}, u32[]{:S(2)}) collective-permute-start(f32[8,2,8,128]{3,2,1,0:T(8,128)S(1)} %get-tuple-element.30.refs_8_.refs_10_), channel_id=1, source_target_pairs={{0,1},{2,3},{4,5},{6,7},{8,9},{10,11},{12,13},{14,15},{1,0},{3,2},... | collective-permute-start | bytes 196616 | tf_op jit(solution)/shard_map/ppermute | solution.py:588
  64.6 2.2 %copy-start = (f32[2,64,8,8,128]{4,3,2,1,0:T(8,128)S(1)}, f32[2,64,8,8,128]{4,3,2,1,0:T(8,128)}, u32[]{:S(2)}) copy-start(f32[2,64,8,8,128]{4,3,2,1,0:T(8,128)} %get-tuple-element.23.refs_1_) | copy-start | bytes 12582916
  66.8 32.0 %copy-start.1 = (f32[2,64,8,8,128]{4,3,2,1,0:T(8,128)S(1)}, f32[2,64,8,8,128]{4,3,2,1,0:T(8,128)}, u32[]{:S(2)}) copy-start(f32[2,64,8,8,128]{4,3,2,1,0:T(8,128)} %get-tuple-element.24.refs_2_) | copy-start | bytes 12582916
  90.6 7.9 %collective-permute-start.19 = (f32[4,2,8,128]{3,2,1,0:T(8,128)S(1)}, f32[4,2,8,128]{3,2,1,0:T(8,128)S(1)}, u32[]{:S(2)}, u32[]{:S(2)}) collective-permute-start(f32[4,2,8,128]{3,2,1,0:T(8,128)S(1)} %get-tuple-element.34.refs_7_), channel_id=1, source_target_pairs={{1,2},{3,4},{5,6},{7,8},{9,10},{11,12},{13,14},{2,1},{4,3},{6,5},{... | collective-permute-start | bytes 98312 | tf_op jit(solution)/shard_map/ppermute | solution.py:587
  94.8 4.0 %collective-permute-start.18 = (f32[4,2,8,128]{3,2,1,0:T(8,128)S(1)}, f32[4,2,8,128]{3,2,1,0:T(8,128)S(1)}, u32[]{:S(2)}, u32[]{:S(2)}) collective-permute-start(f32[4,2,8,128]{3,2,1,0:T(8,128)S(1)} %get-tuple-element.34.refs_7_), channel_id=1, source_target_pairs={{0,1},{2,3},{4,5},{6,7},{8,9},{10,11},{12,13},{14,15},{1,0},{3,2},... | collective-permute-start | bytes 98312 | tf_op jit(solution)/shard_map/ppermute | solution.py:588
  (1 other events, 0.6 us)

commit v6 on v5

--- a/solution.py
+++ b/solution.py
@@ -16,7 +16,8 @@
 LAYERS = 64
 TILE_ROWS = 8
 WINDOW = 16
-VMEM_LIMIT = 40 * 1024 * 1024
+DOWN_VMEM = 48
+OTHER_VMEM = 56
 
 D_AIR = 6.0
 D_TERRAIN = 6.0 + TERRAIN_PENALTY
@@ -549,8 +550,8 @@
     return pl.BlockSpec(memory_space=space)
 
 
-def params():
-    return pltpu.CompilerParams(vmem_limit_bytes=VMEM_LIMIT)
+def params(mebibytes):
+    return pltpu.CompilerParams(vmem_limit_bytes=mebibytes * 1024 * 1024)
 
 
 def shape(*dims):
@@ -631,7 +632,7 @@
         in_specs=[smem] + [spec()] * 16, out_specs=(hbm,) * 4 + (spec(),) * 4,
         scratch_shapes=[vmem(2, rows, 8), vmem(2, rows, 8), vmem(2, rows)]
         + fine_rows + level_1_scratch(rows) + [pltpu.SemaphoreType.DMA((4,))],
-        compiler_params=params(), name="down",
+        compiler_params=params(DOWN_VMEM), name="down",
     )(scalars, *tiles)
 
     first, second = exchange(packed, packed)
@@ -642,7 +643,7 @@
         scratch_shapes=[vmem(2, rows, 8), vmem(2, rows, 8), vmem(2, rows)]
         + fine_rows + level_1_scratch(rows) + level_2_scratch(rows)
         + [pltpu.SemaphoreType.DMA((4,))],
-        compiler_params=params(), name="middle",
+        compiler_params=params(OTHER_VMEM), name="middle",
     )(scalars, source, weight, height, u0, u1, b1, sh1, packed, second, first)
 
     first_2, second_2 = exchange(packed_2, packed_2)
@@ -653,7 +654,7 @@
         scratch_shapes=[vmem(2, WINDOW, 8), vmem(2, WINDOW, 8)]
         + [vmem(2, WINDOW + 2, 8)] * 2 + level_1_scratch(rows) + level_2_scratch(rows)
         + [pltpu.SemaphoreType.DMA((3,))],
-        compiler_params=params(), name="last",
+        compiler_params=params(OTHER_VMEM), name="last",
     )(scalars, source, weight, u0, u1, b1, sh1,
       packed_2, second_2, first_2, packed, second, first)
     return out.reshape(LAYERS, TILE_ROWS, LANES)

time: 107 us -> 109 us (1.019)
  Pallas kernels: 49 us -> 52 us
    pallas_call x1, Pallas kernels: 23.8 us -> 25.7 us  [per_device(): pl.pallas_call(lambda *refs: middle_kernel(rows, *refs), out_shape=(level...]
    unnamed x10 -> x20, local copies, waits for them, and re-layouts: 5.76 us -> 5.21 us
where the time goes in v6:
time: 109 us
  Pallas kernels  52 us (48%)
  starting transfers between devices  25.8 us (24%)
  waiting for transfers between devices  24.8 us (23%)
  local copies, waits for them, and re-layouts  5.88 us (5%)
    pallas_call x1, Pallas kernels, per_device(): pl.pallas_call(lambda *refs: middle_kernel(rows, *refs), out_shape=(level...  25.7 us
    pallas_call x1, Pallas kernels, per_device(): pl.pallas_call(lambda *refs: down_kernel(rows, *refs), out_shape=(level_0...  15.8 us
    ppermute x3, starting transfers between devices, exchange(): first = lax.ppermute(first_out, 'gy', swaps(1))  12 us
    ppermute x3, waiting for transfers between devices, exchange(): first = lax.ppermute(first_out, 'gy', swaps(1))  8.68 us
    ppermute x2, starting transfers between devices, gather_near(): above = lax.ppermute(tile, 'gx', down)  8.21 us
    pallas_call x1, Pallas kernels, per_device(): pl.pallas_call(lambda *refs: last_kernel(rows, *refs), out_shape=jax.Shap...  7.97 us
    unnamed x20, local copies, waits for them, and re-layouts  5.21 us
    ppermute x1, starting transfers between devices, per_device(): lax.ppermute(jnp.stack([own_near[1][1], halo_near[1][1]]), 'gx', down)  3.76 us
  transfers between devices with their start and end apart: 20, of which 11 were waited for; matrix products, arithmetic and copies ran while one was open for 0% of the time, Pallas kernels for 0%

profile of v6, /device:TPU:6, one launch (start us, length us, event | category | flops | bytes accessed | tf_op | source)
XLA Modules:
  0.0 108.9 jit_solution(6906558597352907175)
XLA Ops:
  0.6 2.5 %pack.1 = (f32[2,33,8,128]{3,2,1,0:T(8,128)}, f32[33,8,128]{2,1,0:T(8,128)}, f32[33,8,128]{2,1,0:T(8,128)}) custom-call(s32[7]{0:T(128)} %stack.54.s_ref.refs_0_, f32[512,128]{1,0:T(8,128)} %bitcast.14, s32[512,128]{1,0:T(8,128)} %bitcast.15), custom_call_target="tpu_custom_call" | custom-call | tf_op jit(solution)/shard_map/pack/pallas_call | solution.py:594
  3.1 5.2 %collective-permute-start.2 = (f32[33,8,128]{2,1,0:T(8,128)}, f32[33,8,128]{2,1,0:T(8,128)S(1)}, u32[]{:S(2)}, u32[]{:S(2)}) collective-permute-start(f32[33,8,128]{2,1,0:T(8,128)} %get-tuple-element.21), channel_id=1, source_target_pairs={{1,2},{3,4},{5,6},{7,8},{9,10},{11,12},{13,14},{2,1},{4,3},{6,5},{... | collective-permute-start | bytes 405512 | tf_op jit(solution)/shard_map/ppermute | solution.py:588
  8.4 4.1 %collective-permute-start.1 = (f32[2,33,8,128]{3,2,1,0:T(8,128)}, f32[2,33,8,128]{3,2,1,0:T(8,128)S(1)}, u32[]{:S(2)}, u32[]{:S(2)}) collective-permute-start(f32[2,33,8,128]{3,2,1,0:T(8,128)} %get-tuple-element.20.refs_1_), channel_id=1, source_target_pairs={{0,96},{16,112},{32,0},{48,16},{64,32},{80,48},{96,64},{112,80},{1... | collective-permute-start | bytes 811016 | tf_op jit(solution)/shard_map/ppermute | solution.py:607
  12.7 1.0 collective-permute-done.3
  13.7 4.1 %collective-permute-start.5 = (f32[2,33,8,128]{3,2,1,0:T(8,128)S(1)}, f32[2,33,8,128]{3,2,1,0:T(8,128)S(1)}, u32[]{:S(2)}, u32[]{:S(2)}) collective-permute-start(f32[2,33,8,128]{3,2,1,0:T(8,128)S(1)} %pad_maximum_fusion.refs_4_), channel_id=1, source_target_pairs={{0,96},{16,112},{32,0},{48,16},{64,32},{80,48},{96,64},{112,80},{1... | collective-permute-start | bytes 811016 | tf_op jit(solution)/shard_map/ppermute | solution.py:607
  17.8 1.9 %collective-permute-done.1.refs_3_ = f32[2,33,8,128]{3,2,1,0:T(8,128)S(1)} collective-permute-done((f32[2,33,8,128]{3,2,1,0:T(8,128)}, f32[2,33,8,128]{3,2,1,0:T(8,128)S(1)}, u32[]{:S(2)}, u32[]{:S(2)}) %collective-permute-start.1) | collective-permute-done | bytes 270368 | tf_op jit(solution)/shard_map/ppermute | solution.py:607
  19.8 3.3 %collective-permute-done.refs_2_ = f32[2,33,8,128]{3,2,1,0:T(8,128)S(1)} collective-permute-done((f32[2,33,8,128]{3,2,1,0:T(8,128)}, f32[2,33,8,128]{3,2,1,0:T(8,128)S(1)}, u32[]{:S(2)}, u32[]{:S(2)}) %collective-permute-start) | collective-permute-done | bytes 270368 | tf_op jit(solution)/shard_map/ppermute | solution.py:606
  23.1 0.8 collective-permute-done.5.refs_6_
  24.0 3.8 %collective-permute-start.7 = (f32[2,33,8,128]{3,2,1,0:T(8,128)S(1)}, f32[2,33,8,128]{3,2,1,0:T(8,128)S(1)}, u32[]{:S(2)}, u32[]{:S(2)}) collective-permute-start(f32[2,33,8,128]{3,2,1,0:T(8,128)S(1)} %pad_maximum_fusion.2), channel_id=1, source_target_pairs={{0,96},{16,112},{32,0},{48,16},{64,32},{80,48},{96,64},{112,80},{1... | collective-permute-start | bytes 811016 | tf_op jit(solution)/shard_map/ppermute | solution.py:620
  28.6 3.7 %collective-permute-done.7.refs_8_ = f32[2,33,8,128]{3,2,1,0:T(8,128)S(1)} collective-permute-done((f32[2,33,8,128]{3,2,1,0:T(8,128)S(1)}, f32[2,33,8,128]{3,2,1,0:T(8,128)S(1)}, u32[]{:S(2)}, u32[]{:S(2)}) %collective-permute-start.7) | collective-permute-done | bytes 270368 | tf_op jit(solution)/shard_map/ppermute | solution.py:620
  32.3 3.5 %collective-permute-done.6.refs_7_ = f32[2,33,8,128]{3,2,1,0:T(8,128)S(1)} collective-permute-done((f32[2,33,8,128]{3,2,1,0:T(8,128)S(1)}, f32[2,33,8,128]{3,2,1,0:T(8,128)S(1)}, u32[]{:S(2)}, u32[]{:S(2)}) %collective-permute-start.6) | collective-permute-done | bytes 270368 | tf_op jit(solution)/shard_map/ppermute | solution.py:619
  35.9 1.5 %collective-permute-done.14.refs_15_ = f32[2,33,8,128]{3,2,1,0:T(8,128)S(1)} collective-permute-done((f32[2,33,8,128]{3,2,1,0:T(8,128)S(1)}, f32[2,33,8,128]{3,2,1,0:T(8,128)S(1)}, u32[]{:S(2)}, u32[]{:S(2)}) %collective-permute-start.14) | collective-permute-done | bytes 270368 | tf_op jit(solution)/shard_map/ppermute | solution.py:611
  37.4 1.0 copy-done.3
  39.0 15.8 %down.1 = (f32[2,64,8,8,128]{4,3,2,1,0:T(8,128)}, f32[2,64,8,8,128]{4,3,2,1,0:T(8,128)}, f32[2,64,8,8,128]{4,3,2,1,0:T(8,128)}, f32[2,64,8,128]{3,2,1,0:T(8,128)...) custom-call(s32[7]{0:T(128)S(1)} %copy-done.5, ...), custom_call_target="tpu_custom_call" | custom-call | tf_op jit(solution)/shard_map/down/pallas_call | solution.py:628
  54.8 0.8 copy-done
  55.6 0.8 copy-done.1
  56.4 0.8 copy-done.2
  57.2 2.6 %collective-permute-start.17 = (f32[8,2,8,128]{3,2,1,0:T(8,128)S(1)}, f32[8,2,8,128]{3,2,1,0:T(8,128)S(1)}, u32[]{:S(2)}, u32[]{:S(2)}) collective-permute-start(f32[8,2,8,128]{3,2,1,0:T(8,128)S(1)} %get-tuple-element.30.refs_8_.refs_10_), channel_id=1, source_target_pairs={{1,2},{3,4},{5,6},{7,8},{9,10},{11,12},{13,14},{2,1},{4,3},{6,5},{... | collective-permute-start | bytes 196616 | tf_op jit(solution)/shard_map/ppermute | solution.py:588
  59.8 0.9 collective-permute-start.16
  60.7 4.7 %collective-permute-done.17.refs_10_.refs_12_ = f32[8,2,8,128]{3,2,1,0:T(8,128)S(1)} collective-permute-done((f32[8,2,8,128]{3,2,1,0:T(8,128)S(1)}, f32[8,2,8,128]{3,2,1,0:T(8,128)S(1)}, u32[]{:S(2)}, u32[]{:S(2)}) %collective-permute-start.17) | collective-permute-done | bytes 65568 | tf_op jit(solution)/shard_map/ppermute | solution.py:588
  66.1 25.7 %middle.1 = (f32[2,64,8,8,128]{4,3,2,1,0:T(8,128)}, f32[32,4,8,128]{3,2,1,0:T(8,128)}, f32[32,4,8,128]{3,2,1,0:T(8,128)}, f32[4,2,8,128]{3,2,1,0:T(8,128)}) custom-call(s32[7]{0:T(128)} %stack.54.s_ref.refs_0_, f32[2,64,8,8,128]{4,3,2,1,0:T(8,128)} %get-tuple-element.23.refs_1_, f32[2,64,8,8,128]{4,3,2,1,0:T(8,128)} %get-tuple-element.24.refs_2_, ...), custom_call_target="tpu_custom_call" | custom-call | tf_op jit(solution)/shard_map/middle/pallas_call | solution.py:639
  91.8 4.2 %collective-permute-start.19 = (f32[4,2,8,128]{3,2,1,0:T(8,128)}, f32[4,2,8,128]{3,2,1,0:T(8,128)S(1)}, u32[]{:S(2)}, u32[]{:S(2)}) collective-permute-start(f32[4,2,8,128]{3,2,1,0:T(8,128)} %get-tuple-element.34.refs_7_), channel_id=1, source_target_pairs={{1,2},{3,4},{5,6},{7,8},{9,10},{11,12},{13,14},{2,1},{4,3},{6,5},{... | collective-permute-start | bytes 98312 | tf_op jit(solution)/shard_map/ppermute | solution.py:588
  96.1 3.8 %collective-permute-done.19.refs_9_ = f32[4,2,8,128]{3,2,1,0:T(8,128)S(1)} collective-permute-done((f32[4,2,8,128]{3,2,1,0:T(8,128)}, f32[4,2,8,128]{3,2,1,0:T(8,128)S(1)}, u32[]{:S(2)}, u32[]{:S(2)}) %collective-permute-start.19) | collective-permute-done | bytes 32800 | tf_op jit(solution)/shard_map/ppermute | solution.py:588
  100.8 8.0 %last.1 = f32[512,128]{1,0:T(8,128)} custom-call(s32[7]{0:T(128)} %stack.54.s_ref.refs_0_, f32[2,64,8,8,128]{4,3,2,1,0:T(8,128)} %get-tuple-element.23.refs_1_, f32[2,64,8,8,128]{4,3,2,1,0:T(8,128)} %get-tuple-element.24.refs_2_, f32[2,64,8,8,128]{4,3,2,1,0:T(8,128)} %get-tuple-element.31.refs_3_, f32[32,4,8,128]{3,2,1,0:T(8,128)} %get-tuple-element.32.refs_4_, ...), custom_call_target="tpu_custom_call" | custom-call | tf_op jit(solution)/shard_map/last/pallas_call | solution.py:650
  (50 shorter events, 4.1 us)
Async XLA Ops:
  3.1 9.5 %collective-permute-start.2 = (f32[33,8,128]{2,1,0:T(8,128)}, f32[33,8,128]{2,1,0:T(8,128)S(1)}, u32[]{:S(2)}, u32[]{:S(2)}) collective-permute-start(f32[33,8,128]{2,1,0:T(8,128)} %get-tuple-element.21), channel_id=1, source_target_pairs={{1,2},{3,4},{5,6},{7,8},{9,10},{11,12},{13,14},{2,1},{4,3},{6,5},{... | collective-permute-start | bytes 405512 | tf_op jit(solution)/shard_map/ppermute | solution.py:588
  8.3 5.3 %collective-permute-start.3 = (f32[33,8,128]{2,1,0:T(8,128)}, f32[33,8,128]{2,1,0:T(8,128)S(1)}, u32[]{:S(2)}, u32[]{:S(2)}) collective-permute-start(f32[33,8,128]{2,1,0:T(8,128)} %get-tuple-element.22), channel_id=1, source_target_pairs={{0,1},{2,3},{4,5},{6,7},{8,9},{10,11},{12,13},{14,15},{1,0},{3,2},... | collective-permute-start | bytes 405512 | tf_op jit(solution)/shard_map/ppermute | solution.py:589
  8.4 11.3 %collective-permute-start.1 = (f32[2,33,8,128]{3,2,1,0:T(8,128)}, f32[2,33,8,128]{3,2,1,0:T(8,128)S(1)}, u32[]{:S(2)}, u32[]{:S(2)}) collective-permute-start(f32[2,33,8,128]{3,2,1,0:T(8,128)} %get-tuple-element.20.refs_1_), channel_id=1, source_target_pairs={{0,96},{16,112},{32,0},{48,16},{64,32},{80,48},{96,64},{112,80},{1... | collective-permute-start | bytes 811016 | tf_op jit(solution)/shard_map/ppermute | solution.py:607
  12.5 10.6 %collective-permute-start = (f32[2,33,8,128]{3,2,1,0:T(8,128)}, f32[2,33,8,128]{3,2,1,0:T(8,128)S(1)}, u32[]{:S(2)}, u32[]{:S(2)}) collective-permute-start(f32[2,33,8,128]{3,2,1,0:T(8,128)} %get-tuple-element.20.refs_1_), channel_id=1, source_target_pairs={{0,32},{16,48},{32,64},{48,80},{64,96},{80,112},{96,0},{112,16},{1... | collective-permute-start | bytes 811016 | tf_op jit(solution)/shard_map/ppermute | solution.py:606
  13.7 10.3 %collective-permute-start.5 = (f32[2,33,8,128]{3,2,1,0:T(8,128)S(1)}, f32[2,33,8,128]{3,2,1,0:T(8,128)S(1)}, u32[]{:S(2)}, u32[]{:S(2)}) collective-permute-start(f32[2,33,8,128]{3,2,1,0:T(8,128)S(1)} %pad_maximum_fusion.refs_4_), channel_id=1, source_target_pairs={{0,96},{16,112},{32,0},{48,16},{64,32},{80,48},{96,64},{112,80},{1... | collective-permute-start | bytes 811016 | tf_op jit(solution)/shard_map/ppermute | solution.py:607
  17.8 10.0 %collective-permute-start.4 = (f32[2,33,8,128]{3,2,1,0:T(8,128)S(1)}, f32[2,33,8,128]{3,2,1,0:T(8,128)S(1)}, u32[]{:S(2)}, u32[]{:S(2)}) collective-permute-start(f32[2,33,8,128]{3,2,1,0:T(8,128)S(1)} %pad_maximum_fusion.refs_4_), channel_id=1, source_target_pairs={{0,32},{16,48},{32,64},{48,80},{64,96},{80,112},{96,0},{112,16},{1... | collective-permute-start | bytes 811016 | tf_op jit(solution)/shard_map/ppermute | solution.py:606
  17.8 10.1 %collective-permute-start.8 = (f32[2,33,8,128]{3,2,1,0:T(8,128)}, f32[2,33,8,128]{3,2,1,0:T(8,128)S(1)}, u32[]{:S(2)}, u32[]{:S(2)}) collective-permute-start(f32[2,33,8,128]{3,2,1,0:T(8,128)} %get-tuple-element.20.refs_1_), channel_id=1, source_target_pairs={{0,16},{16,0},{32,48},{48,32},{64,80},{80,64},{96,112},{112,96},{1... | collective-permute-start | bytes 811016 | tf_op jit(solution)/shard_map/ppermute | solution.py:611
  19.8 8.3 %collective-permute-start.11 = (f32[2,33,8,128]{3,2,1,0:T(8,128)S(1)}, f32[2,33,8,128]{3,2,1,0:T(8,128)S(1)}, u32[]{:S(2)}, u32[]{:S(2)}) collective-permute-start(f32[2,33,8,128]{3,2,1,0:T(8,128)S(1)} %pad_maximum_fusion.refs_4_), channel_id=1, source_target_pairs={{0,16},{16,0},{32,48},{48,32},{64,80},{80,64},{96,112},{112,96},{1... | collective-permute-start | bytes 811016 | tf_op jit(solution)/shard_map/ppermute | solution.py:611
  23.1 5.4 %collective-permute-start.10 = (f32[2,33,8,128]{3,2,1,0:T(8,128)S(1)}, f32[2,33,8,128]{3,2,1,0:T(8,128)S(1)}, u32[]{:S(2)}, u32[]{:S(2)}) collective-permute-start(f32[2,33,8,128]{3,2,1,0:T(8,128)S(1)} %collective-permute-done.1.refs_3_), channel_id=1, source_target_pairs={{0,16},{16,0},{32,48},{48,32},{64,80},{80,64},{96,112},{112,96},{1... | collective-permute-start | bytes 811016 | tf_op jit(solution)/shard_map/ppermute | solution.py:611
  24.0 8.3 %collective-permute-start.7 = (f32[2,33,8,128]{3,2,1,0:T(8,128)S(1)}, f32[2,33,8,128]{3,2,1,0:T(8,128)S(1)}, u32[]{:S(2)}, u32[]{:S(2)}) collective-permute-start(f32[2,33,8,128]{3,2,1,0:T(8,128)S(1)} %pad_maximum_fusion.2), channel_id=1, source_target_pairs={{0,96},{16,112},{32,0},{48,16},{64,32},{80,48},{96,64},{112,80},{1... | collective-permute-start | bytes 811016 | tf_op jit(solution)/shard_map/ppermute | solution.py:620
  27.8 8.0 %collective-permute-start.6 = (f32[2,33,8,128]{3,2,1,0:T(8,128)S(1)}, f32[2,33,8,128]{3,2,1,0:T(8,128)S(1)}, u32[]{:S(2)}, u32[]{:S(2)}) collective-permute-start(f32[2,33,8,128]{3,2,1,0:T(8,128)S(1)} %pad_maximum_fusion.1), channel_id=1, source_target_pairs={{0,32},{16,48},{32,64},{48,80},{64,96},{80,112},{96,0},{112,16},{1... | collective-permute-start | bytes 811016 | tf_op jit(solution)/shard_map/ppermute | solution.py:619
  27.9 7.9 %collective-permute-start.9 = (f32[2,33,8,128]{3,2,1,0:T(8,128)S(1)}, f32[2,33,8,128]{3,2,1,0:T(8,128)S(1)}, u32[]{:S(2)}, u32[]{:S(2)}) collective-permute-start(f32[2,33,8,128]{3,2,1,0:T(8,128)S(1)} %collective-permute-done.refs_2_), channel_id=1, source_target_pairs={{0,16},{16,0},{32,48},{48,32},{64,80},{80,64},{96,112},{112,96},{1... | collective-permute-start | bytes 811016 | tf_op jit(solution)/shard_map/ppermute | solution.py:611
  28.0 7.8 %collective-permute-start.13 = (f32[2,33,8,128]{3,2,1,0:T(8,128)S(1)}, f32[2,33,8,128]{3,2,1,0:T(8,128)S(1)}, u32[]{:S(2)}, u32[]{:S(2)}) collective-permute-start(f32[2,33,8,128]{3,2,1,0:T(8,128)S(1)} %collective-permute-done.5.refs_6_), channel_id=1, source_target_pairs={{0,16},{16,0},{32,48},{48,32},{64,80},{80,64},{96,112},{112,96},{1... | collective-permute-start | bytes 811016 | tf_op jit(solution)/shard_map/ppermute | solution.py:611
  28.5 7.4 %collective-permute-start.12 = (f32[2,33,8,128]{3,2,1,0:T(8,128)S(1)}, f32[2,33,8,128]{3,2,1,0:T(8,128)S(1)}, u32[]{:S(2)}, u32[]{:S(2)}) collective-permute-start(f32[2,33,8,128]{3,2,1,0:T(8,128)S(1)} %collective-permute-done.4.refs_5_), channel_id=1, source_target_pairs={{0,16},{16,0},{32,48},{48,32},{64,80},{80,64},{96,112},{112,96},{1... | collective-permute-start | bytes 811016 | tf_op jit(solution)/shard_map/ppermute | solution.py:611
  32.3 3.6 %collective-permute-start.15 = (f32[2,33,8,128]{3,2,1,0:T(8,128)S(1)}, f32[2,33,8,128]{3,2,1,0:T(8,128)S(1)}, u32[]{:S(2)}, u32[]{:S(2)}) collective-permute-start(f32[2,33,8,128]{3,2,1,0:T(8,128)S(1)} %collective-permute-done.7.refs_8_), channel_id=1, source_target_pairs={{0,16},{16,0},{32,48},{48,32},{64,80},{80,64},{96,112},{112,96},{1... | collective-permute-start | bytes 811016 | tf_op jit(solution)/shard_map/ppermute | solution.py:611
  35.9 1.5 %collective-permute-start.14 = (f32[2,33,8,128]{3,2,1,0:T(8,128)S(1)}, f32[2,33,8,128]{3,2,1,0:T(8,128)S(1)}, u32[]{:S(2)}, u32[]{:S(2)}) collective-permute-start(f32[2,33,8,128]{3,2,1,0:T(8,128)S(1)} %collective-permute-done.6.refs_7_), channel_id=1, source_target_pairs={{0,16},{16,0},{32,48},{48,32},{64,80},{80,64},{96,112},{112,96},{1... | collective-permute-start | bytes 811016 | tf_op jit(solution)/shard_map/ppermute | solution.py:611
  37.4 1.0 copy-start.3
  54.8 0.8 copy-start
  55.6 0.8 copy-start.1
  57.2 8.3 %copy-start.4 = (f32[8,2,8,128]{3,2,1,0:T(8,128)}, f32[8,2,8,128]{3,2,1,0:T(8,128)S(1)}, u32[]{:S(2)}) copy-start(f32[8,2,8,128]{3,2,1,0:T(8,128)S(1)} %get-tuple-element.30.refs_8_.refs_10_) | copy-start | bytes 196612
  57.2 8.3 %collective-permute-start.17 = (f32[8,2,8,128]{3,2,1,0:T(8,128)S(1)}, f32[8,2,8,128]{3,2,1,0:T(8,128)S(1)}, u32[]{:S(2)}, u32[]{:S(2)}) collective-permute-start(f32[8,2,8,128]{3,2,1,0:T(8,128)S(1)} %get-tuple-element.30.refs_8_.refs_10_), channel_id=1, source_target_pairs={{1,2},{3,4},{5,6},{7,8},{9,10},{11,12},{13,14},{2,1},{4,3},{6,5},{... | collective-permute-start | bytes 196616 | tf_op jit(solution)/shard_map/ppermute | solution.py:588
  59.8 5.7 %collective-permute-start.16 = (f32[8,2,8,128]{3,2,1,0:T(8,128)S(1)}, f32[8,2,8,128]{3,2,1,0:T(8,128)S(1)}, u32[]{:S(2)}, u32[]{:S(2)}) collective-permute-start(f32[8,2,8,128]{3,2,1,0:T(8,128)S(1)} %get-tuple-element.30.refs_8_.refs_10_), channel_id=1, source_target_pairs={{0,1},{2,3},{4,5},{6,7},{8,9},{10,11},{12,13},{14,15},{1,0},{3,2},... | collective-permute-start | bytes 196616 | tf_op jit(solution)/shard_map/ppermute | solution.py:589
  91.8 8.1 %collective-permute-start.19 = (f32[4,2,8,128]{3,2,1,0:T(8,128)}, f32[4,2,8,128]{3,2,1,0:T(8,128)S(1)}, u32[]{:S(2)}, u32[]{:S(2)}) collective-permute-start(f32[4,2,8,128]{3,2,1,0:T(8,128)} %get-tuple-element.34.refs_7_), channel_id=1, source_target_pairs={{1,2},{3,4},{5,6},{7,8},{9,10},{11,12},{13,14},{2,1},{4,3},{6,5},{... | collective-permute-start | bytes 98312 | tf_op jit(solution)/shard_map/ppermute | solution.py:588
  96.0 4.2 %collective-permute-start.18 = (f32[4,2,8,128]{3,2,1,0:T(8,128)}, f32[4,2,8,128]{3,2,1,0:T(8,128)S(1)}, u32[]{:S(2)}, u32[]{:S(2)}) collective-permute-start(f32[4,2,8,128]{3,2,1,0:T(8,128)} %get-tuple-element.34.refs_7_), channel_id=1, source_target_pairs={{0,1},{2,3},{4,5},{6,7},{8,9},{10,11},{12,13},{14,15},{1,0},{3,2},... | collective-permute-start | bytes 98312 | tf_op jit(solution)/shard_map/ppermute | solution.py:589
  (6 other events, 3.9 us)

commit v7 on v5

--- a/solution.py
+++ b/solution.py
@@ -16,7 +16,7 @@
 LAYERS = 64
 TILE_ROWS = 8
 WINDOW = 16
-VMEM_LIMIT = 40 * 1024 * 1024
+VMEM_LIMIT = 28 * 1024 * 1024
 
 D_AIR = 6.0
 D_TERRAIN = 6.0 + TERRAIN_PENALTY

time: 107 us -> 103 us (0.963)
  local copies, waits for them, and re-layouts: 6.42 us -> 2.3 us
  Pallas kernels: 49 us -> 50.1 us
    unnamed x10 -> x4, local copies, waits for them, and re-layouts: 5.76 us -> 1.61 us
where the time goes in v7:
time: 103 us
  Pallas kernels  50.1 us (49%)
  starting transfers between devices  25.8 us (25%)
  waiting for transfers between devices  24.6 us (24%)
  local copies, waits for them, and re-layouts  2.3 us (2%)
    pallas_call x1, Pallas kernels, per_device(): pl.pallas_call(lambda *refs: middle_kernel(rows, *refs), out_shape=(level...  24.3 us
    pallas_call x1, Pallas kernels, per_device(): pl.pallas_call(lambda *refs: down_kernel(rows, *refs), out_shape=(level_0...  15.9 us
    ppermute x3, starting transfers between devices, exchange(): first = lax.ppermute(first_out, 'gy', swaps(1))  12 us
    ppermute x3, waiting for transfers between devices, exchange(): first = lax.ppermute(first_out, 'gy', swaps(1))  8.44 us
    ppermute x2, starting transfers between devices, gather_near(): above = lax.ppermute(tile, 'gx', down)  8.21 us
    pallas_call x1, Pallas kernels, per_device(): pl.pallas_call(lambda *refs: last_kernel(rows, *refs), out_shape=jax.Shap...  7.34 us
    ppermute x1, starting transfers between devices, per_device(): lax.ppermute(jnp.stack([own_near[1][1], halo_near[1][1]]), 'gx', down)  3.76 us
    ppermute x1, waiting for transfers between devices, per_device(): lax.ppermute(jnp.stack([own_near[1][1], halo_near[1][1]]), 'gx', down)  3.71 us
  transfers between devices with their start and end apart: 20, of which 11 were waited for; matrix products, arithmetic and copies ran while one was open for 0% of the time, Pallas kernels for 0%

profile of v7, /device:TPU:6, one launch (start us, length us, event | category | flops | bytes accessed | tf_op | source)
XLA Modules:
  0.0 103.3 jit_solution(496831661920572882)
XLA Ops:
  0.0 0.7 stack.54.s_ref.refs_0_
  0.7 2.5 %pack.1 = (f32[2,33,8,128]{3,2,1,0:T(8,128)}, f32[33,8,128]{2,1,0:T(8,128)}, f32[33,8,128]{2,1,0:T(8,128)}) custom-call(s32[7]{0:T(128)} %stack.54.s_ref.refs_0_, f32[512,128]{1,0:T(8,128)} %bitcast.14, s32[512,128]{1,0:T(8,128)} %bitcast.15), custom_call_target="tpu_custom_call" | custom-call | tf_op jit(solution)/shard_map/pack/pallas_call | solution.py:593
  3.1 5.2 %collective-permute-start.2 = (f32[33,8,128]{2,1,0:T(8,128)}, f32[33,8,128]{2,1,0:T(8,128)S(1)}, u32[]{:S(2)}, u32[]{:S(2)}) collective-permute-start(f32[33,8,128]{2,1,0:T(8,128)} %get-tuple-element.21), channel_id=1, source_target_pairs={{1,2},{3,4},{5,6},{7,8},{9,10},{11,12},{13,14},{2,1},{4,3},{6,5},{... | collective-permute-start | bytes 405512 | tf_op jit(solution)/shard_map/ppermute | solution.py:587
  8.4 4.1 %collective-permute-start.1 = (f32[2,33,8,128]{3,2,1,0:T(8,128)}, f32[2,33,8,128]{3,2,1,0:T(8,128)S(1)}, u32[]{:S(2)}, u32[]{:S(2)}) collective-permute-start(f32[2,33,8,128]{3,2,1,0:T(8,128)} %get-tuple-element.20.refs_1_), channel_id=1, source_target_pairs={{0,96},{16,112},{32,0},{48,16},{64,32},{80,48},{96,64},{112,80},{1... | collective-permute-start | bytes 811016 | tf_op jit(solution)/shard_map/ppermute | solution.py:606
  12.7 1.0 collective-permute-done.3
  13.7 4.1 %collective-permute-start.5 = (f32[2,33,8,128]{3,2,1,0:T(8,128)S(1)}, f32[2,33,8,128]{3,2,1,0:T(8,128)S(1)}, u32[]{:S(2)}, u32[]{:S(2)}) collective-permute-start(f32[2,33,8,128]{3,2,1,0:T(8,128)S(1)} %pad_maximum_fusion.refs_4_), channel_id=1, source_target_pairs={{0,96},{16,112},{32,0},{48,16},{64,32},{80,48},{96,64},{112,80},{1... | collective-permute-start | bytes 811016 | tf_op jit(solution)/shard_map/ppermute | solution.py:606
  17.8 1.9 %collective-permute-done.1.refs_3_ = f32[2,33,8,128]{3,2,1,0:T(8,128)S(1)} collective-permute-done((f32[2,33,8,128]{3,2,1,0:T(8,128)}, f32[2,33,8,128]{3,2,1,0:T(8,128)S(1)}, u32[]{:S(2)}, u32[]{:S(2)}) %collective-permute-start.1) | collective-permute-done | bytes 270368 | tf_op jit(solution)/shard_map/ppermute | solution.py:606
  19.8 3.3 %collective-permute-done.refs_2_ = f32[2,33,8,128]{3,2,1,0:T(8,128)S(1)} collective-permute-done((f32[2,33,8,128]{3,2,1,0:T(8,128)}, f32[2,33,8,128]{3,2,1,0:T(8,128)S(1)}, u32[]{:S(2)}, u32[]{:S(2)}) %collective-permute-start) | collective-permute-done | bytes 270368 | tf_op jit(solution)/shard_map/ppermute | solution.py:605
  23.1 0.8 collective-permute-done.5.refs_6_
  24.0 3.8 %collective-permute-start.7 = (f32[2,33,8,128]{3,2,1,0:T(8,128)S(1)}, f32[2,33,8,128]{3,2,1,0:T(8,128)S(1)}, u32[]{:S(2)}, u32[]{:S(2)}) collective-permute-start(f32[2,33,8,128]{3,2,1,0:T(8,128)S(1)} %pad_maximum_fusion.2), channel_id=1, source_target_pairs={{0,96},{16,112},{32,0},{48,16},{64,32},{80,48},{96,64},{112,80},{1... | collective-permute-start | bytes 811016 | tf_op jit(solution)/shard_map/ppermute | solution.py:619
  28.0 0.5 collective-permute-start.13
  28.6 3.7 %collective-permute-done.7.refs_8_ = f32[2,33,8,128]{3,2,1,0:T(8,128)S(1)} collective-permute-done((f32[2,33,8,128]{3,2,1,0:T(8,128)S(1)}, f32[2,33,8,128]{3,2,1,0:T(8,128)S(1)}, u32[]{:S(2)}, u32[]{:S(2)}) %collective-permute-start.7) | collective-permute-done | bytes 270368 | tf_op jit(solution)/shard_map/ppermute | solution.py:619
  32.3 3.5 %collective-permute-done.6.refs_7_ = f32[2,33,8,128]{3,2,1,0:T(8,128)S(1)} collective-permute-done((f32[2,33,8,128]{3,2,1,0:T(8,128)S(1)}, f32[2,33,8,128]{3,2,1,0:T(8,128)S(1)}, u32[]{:S(2)}, u32[]{:S(2)}) %collective-permute-start.6) | collective-permute-done | bytes 270368 | tf_op jit(solution)/shard_map/ppermute | solution.py:618
  35.9 1.5 %collective-permute-done.14.refs_15_ = f32[2,33,8,128]{3,2,1,0:T(8,128)S(1)} collective-permute-done((f32[2,33,8,128]{3,2,1,0:T(8,128)S(1)}, f32[2,33,8,128]{3,2,1,0:T(8,128)S(1)}, u32[]{:S(2)}, u32[]{:S(2)}) %collective-permute-start.14) | collective-permute-done | bytes 270368 | tf_op jit(solution)/shard_map/ppermute | solution.py:610
  37.4 1.0 copy-done
  38.4 0.7 copy-done.1
  39.0 15.9 %down.1 = (f32[2,64,8,8,128]{4,3,2,1,0:T(8,128)S(1)}, f32[2,64,8,8,128]{4,3,2,1,0:T(8,128)S(1)}, f32[2,64,8,8,128]{4,3,2,1,0:T(8,128)S(1)}, f32[2,64,8,128]{3,2,...) custom-call(s32[7]{0:T(128)S(1)} %copy-done.1, ...), custom_call_target="tpu_custom_call" | custom-call | tf_op jit(solution)/shard_map/down/pallas_call | solution.py:627
  54.9 2.6 %collective-permute-start.17 = (f32[8,2,8,128]{3,2,1,0:T(8,128)S(1)}, f32[8,2,8,128]{3,2,1,0:T(8,128)S(1)}, u32[]{:S(2)}, u32[]{:S(2)}) collective-permute-start(f32[8,2,8,128]{3,2,1,0:T(8,128)S(1)} %get-tuple-element.30.refs_8_.refs_10_), channel_id=1, source_target_pairs={{1,2},{3,4},{5,6},{7,8},{9,10},{11,12},{13,14},{2,1},{4,3},{6,5},{... | collective-permute-start | bytes 196616 | tf_op jit(solution)/shard_map/ppermute | solution.py:587
  57.6 0.9 collective-permute-start.16
  58.5 4.7 %collective-permute-done.17.refs_10_.refs_12_ = f32[8,2,8,128]{3,2,1,0:T(8,128)S(1)} collective-permute-done((f32[8,2,8,128]{3,2,1,0:T(8,128)S(1)}, f32[8,2,8,128]{3,2,1,0:T(8,128)S(1)}, u32[]{:S(2)}, u32[]{:S(2)}) %collective-permute-start.17) | collective-permute-done | bytes 65568 | tf_op jit(solution)/shard_map/ppermute | solution.py:587
  63.2 24.3 %middle.1 = (f32[2,64,8,8,128]{4,3,2,1,0:T(8,128)S(1)}, f32[32,4,8,128]{3,2,1,0:T(8,128)S(1)}, f32[32,4,8,128]{3,2,1,0:T(8,128)S(1)}, f32[4,2,8,128]{3,2,1,0:T(8,128)S(1)}) custom-call(s32[7]{0:T(128)S(1)} %copy-done.1, f32[2,64,8,8,128]{4,3,2,1,0:T(8,128)S(1)} %get-tuple-element.23.refs_1_, f32[2,64,8,8,128]{4,3,2,1,0:T(8,128)S(1)} %get-tuple-element.24.refs_2_, ...), custom_call_target="tpu_custom_call" | custom-call | tf_op jit(solution)/shard_map/middle/pallas_call | solution.py:638
  87.6 4.2 %collective-permute-start.19 = (f32[4,2,8,128]{3,2,1,0:T(8,128)S(1)}, f32[4,2,8,128]{3,2,1,0:T(8,128)S(1)}, u32[]{:S(2)}, u32[]{:S(2)}) collective-permute-start(f32[4,2,8,128]{3,2,1,0:T(8,128)S(1)} %get-tuple-element.34.refs_7_), channel_id=1, source_target_pairs={{1,2},{3,4},{5,6},{7,8},{9,10},{11,12},{13,14},{2,1},{4,3},{6,5},{... | collective-permute-start | bytes 98312 | tf_op jit(solution)/shard_map/ppermute | solution.py:587
  91.9 3.6 %collective-permute-done.19.refs_9_ = f32[4,2,8,128]{3,2,1,0:T(8,128)S(1)} collective-permute-done((f32[4,2,8,128]{3,2,1,0:T(8,128)S(1)}, f32[4,2,8,128]{3,2,1,0:T(8,128)S(1)}, u32[]{:S(2)}, u32[]{:S(2)}) %collective-permute-start.19) | collective-permute-done | bytes 32800 | tf_op jit(solution)/shard_map/ppermute | solution.py:587
  95.8 7.3 %last.1 = f32[512,128]{1,0:T(8,128)} custom-call(s32[7]{0:T(128)S(1)} %copy-done.1, f32[2,64,8,8,128]{4,3,2,1,0:T(8,128)S(1)} %get-tuple-element.23.refs_1_, f32[2,64,8,8,128]{4,3,2,1,0:T(8,128)S(1)} %get-tuple-element.24.refs_2_, f32[2,64,8,8,128]{4,3,2,1,0:T(8,128)S(1)} %get-tuple-element.31.refs_3_, f32[32,4,8,128]{3,2,1,0:T(8,128)S(1)} %get-tuple-element.32.refs_4_, ...), custom_call_target="tpu_custom_call" | custom-call | tf_op jit(solution)/shard_map/last/pallas_call | solution.py:649
  (34 shorter events, 1.1 us)
Async XLA Ops:
  3.1 9.5 %collective-permute-start.2 = (f32[33,8,128]{2,1,0:T(8,128)}, f32[33,8,128]{2,1,0:T(8,128)S(1)}, u32[]{:S(2)}, u32[]{:S(2)}) collective-permute-start(f32[33,8,128]{2,1,0:T(8,128)} %get-tuple-element.21), channel_id=1, source_target_pairs={{1,2},{3,4},{5,6},{7,8},{9,10},{11,12},{13,14},{2,1},{4,3},{6,5},{... | collective-permute-start | bytes 405512 | tf_op jit(solution)/shard_map/ppermute | solution.py:587
  8.3 5.3 %collective-permute-start.3 = (f32[33,8,128]{2,1,0:T(8,128)}, f32[33,8,128]{2,1,0:T(8,128)S(1)}, u32[]{:S(2)}, u32[]{:S(2)}) collective-permute-start(f32[33,8,128]{2,1,0:T(8,128)} %get-tuple-element.22), channel_id=1, source_target_pairs={{0,1},{2,3},{4,5},{6,7},{8,9},{10,11},{12,13},{14,15},{1,0},{3,2},... | collective-permute-start | bytes 405512 | tf_op jit(solution)/shard_map/ppermute | solution.py:588
  8.4 11.3 %collective-permute-start.1 = (f32[2,33,8,128]{3,2,1,0:T(8,128)}, f32[2,33,8,128]{3,2,1,0:T(8,128)S(1)}, u32[]{:S(2)}, u32[]{:S(2)}) collective-permute-start(f32[2,33,8,128]{3,2,1,0:T(8,128)} %get-tuple-element.20.refs_1_), channel_id=1, source_target_pairs={{0,96},{16,112},{32,0},{48,16},{64,32},{80,48},{96,64},{112,80},{1... | collective-permute-start | bytes 811016 | tf_op jit(solution)/shard_map/ppermute | solution.py:606
  12.5 10.6 %collective-permute-start = (f32[2,33,8,128]{3,2,1,0:T(8,128)}, f32[2,33,8,128]{3,2,1,0:T(8,128)S(1)}, u32[]{:S(2)}, u32[]{:S(2)}) collective-permute-start(f32[2,33,8,128]{3,2,1,0:T(8,128)} %get-tuple-element.20.refs_1_), channel_id=1, source_target_pairs={{0,32},{16,48},{32,64},{48,80},{64,96},{80,112},{96,0},{112,16},{1... | collective-permute-start | bytes 811016 | tf_op jit(solution)/shard_map/ppermute | solution.py:605
  13.7 10.3 %collective-permute-start.5 = (f32[2,33,8,128]{3,2,1,0:T(8,128)S(1)}, f32[2,33,8,128]{3,2,1,0:T(8,128)S(1)}, u32[]{:S(2)}, u32[]{:S(2)}) collective-permute-start(f32[2,33,8,128]{3,2,1,0:T(8,128)S(1)} %pad_maximum_fusion.refs_4_), channel_id=1, source_target_pairs={{0,96},{16,112},{32,0},{48,16},{64,32},{80,48},{96,64},{112,80},{1... | collective-permute-start | bytes 811016 | tf_op jit(solution)/shard_map/ppermute | solution.py:606
  17.8 10.0 %collective-permute-start.4 = (f32[2,33,8,128]{3,2,1,0:T(8,128)S(1)}, f32[2,33,8,128]{3,2,1,0:T(8,128)S(1)}, u32[]{:S(2)}, u32[]{:S(2)}) collective-permute-start(f32[2,33,8,128]{3,2,1,0:T(8,128)S(1)} %pad_maximum_fusion.refs_4_), channel_id=1, source_target_pairs={{0,32},{16,48},{32,64},{48,80},{64,96},{80,112},{96,0},{112,16},{1... | collective-permute-start | bytes 811016 | tf_op jit(solution)/shard_map/ppermute | solution.py:605
  17.8 10.1 %collective-permute-start.8 = (f32[2,33,8,128]{3,2,1,0:T(8,128)}, f32[2,33,8,128]{3,2,1,0:T(8,128)S(1)}, u32[]{:S(2)}, u32[]{:S(2)}) collective-permute-start(f32[2,33,8,128]{3,2,1,0:T(8,128)} %get-tuple-element.20.refs_1_), channel_id=1, source_target_pairs={{0,16},{16,0},{32,48},{48,32},{64,80},{80,64},{96,112},{112,96},{1... | collective-permute-start | bytes 811016 | tf_op jit(solution)/shard_map/ppermute | solution.py:610
  19.8 8.3 %collective-permute-start.11 = (f32[2,33,8,128]{3,2,1,0:T(8,128)S(1)}, f32[2,33,8,128]{3,2,1,0:T(8,128)S(1)}, u32[]{:S(2)}, u32[]{:S(2)}) collective-permute-start(f32[2,33,8,128]{3,2,1,0:T(8,128)S(1)} %pad_maximum_fusion.refs_4_), channel_id=1, source_target_pairs={{0,16},{16,0},{32,48},{48,32},{64,80},{80,64},{96,112},{112,96},{1... | collective-permute-start | bytes 811016 | tf_op jit(solution)/shard_map/ppermute | solution.py:610
  23.1 5.4 %collective-permute-start.10 = (f32[2,33,8,128]{3,2,1,0:T(8,128)S(1)}, f32[2,33,8,128]{3,2,1,0:T(8,128)S(1)}, u32[]{:S(2)}, u32[]{:S(2)}) collective-permute-start(f32[2,33,8,128]{3,2,1,0:T(8,128)S(1)} %collective-permute-done.1.refs_3_), channel_id=1, source_target_pairs={{0,16},{16,0},{32,48},{48,32},{64,80},{80,64},{96,112},{112,96},{1... | collective-permute-start | bytes 811016 | tf_op jit(solution)/shard_map/ppermute | solution.py:610
  24.0 8.3 %collective-permute-start.7 = (f32[2,33,8,128]{3,2,1,0:T(8,128)S(1)}, f32[2,33,8,128]{3,2,1,0:T(8,128)S(1)}, u32[]{:S(2)}, u32[]{:S(2)}) collective-permute-start(f32[2,33,8,128]{3,2,1,0:T(8,128)S(1)} %pad_maximum_fusion.2), channel_id=1, source_target_pairs={{0,96},{16,112},{32,0},{48,16},{64,32},{80,48},{96,64},{112,80},{1... | collective-permute-start | bytes 811016 | tf_op jit(solution)/shard_map/ppermute | solution.py:619
  27.8 8.0 %collective-permute-start.6 = (f32[2,33,8,128]{3,2,1,0:T(8,128)S(1)}, f32[2,33,8,128]{3,2,1,0:T(8,128)S(1)}, u32[]{:S(2)}, u32[]{:S(2)}) collective-permute-start(f32[2,33,8,128]{3,2,1,0:T(8,128)S(1)} %pad_maximum_fusion.1), channel_id=1, source_target_pairs={{0,32},{16,48},{32,64},{48,80},{64,96},{80,112},{96,0},{112,16},{1... | collective-permute-start | bytes 811016 | tf_op jit(solution)/shard_map/ppermute | solution.py:618
  27.9 7.9 %collective-permute-start.9 = (f32[2,33,8,128]{3,2,1,0:T(8,128)S(1)}, f32[2,33,8,128]{3,2,1,0:T(8,128)S(1)}, u32[]{:S(2)}, u32[]{:S(2)}) collective-permute-start(f32[2,33,8,128]{3,2,1,0:T(8,128)S(1)} %collective-permute-done.refs_2_), channel_id=1, source_target_pairs={{0,16},{16,0},{32,48},{48,32},{64,80},{80,64},{96,112},{112,96},{1... | collective-permute-start | bytes 811016 | tf_op jit(solution)/shard_map/ppermute | solution.py:610
  28.0 7.8 %collective-permute-start.13 = (f32[2,33,8,128]{3,2,1,0:T(8,128)S(1)}, f32[2,33,8,128]{3,2,1,0:T(8,128)S(1)}, u32[]{:S(2)}, u32[]{:S(2)}) collective-permute-start(f32[2,33,8,128]{3,2,1,0:T(8,128)S(1)} %collective-permute-done.5.refs_6_), channel_id=1, source_target_pairs={{0,16},{16,0},{32,48},{48,32},{64,80},{80,64},{96,112},{112,96},{1... | collective-permute-start | bytes 811016 | tf_op jit(solution)/shard_map/ppermute | solution.py:610
  28.5 7.4 %collective-permute-start.12 = (f32[2,33,8,128]{3,2,1,0:T(8,128)S(1)}, f32[2,33,8,128]{3,2,1,0:T(8,128)S(1)}, u32[]{:S(2)}, u32[]{:S(2)}) collective-permute-start(f32[2,33,8,128]{3,2,1,0:T(8,128)S(1)} %collective-permute-done.4.refs_5_), channel_id=1, source_target_pairs={{0,16},{16,0},{32,48},{48,32},{64,80},{80,64},{96,112},{112,96},{1... | collective-permute-start | bytes 811016 | tf_op jit(solution)/shard_map/ppermute | solution.py:610
  32.3 3.6 %collective-permute-start.15 = (f32[2,33,8,128]{3,2,1,0:T(8,128)S(1)}, f32[2,33,8,128]{3,2,1,0:T(8,128)S(1)}, u32[]{:S(2)}, u32[]{:S(2)}) collective-permute-start(f32[2,33,8,128]{3,2,1,0:T(8,128)S(1)} %collective-permute-done.7.refs_8_), channel_id=1, source_target_pairs={{0,16},{16,0},{32,48},{48,32},{64,80},{80,64},{96,112},{112,96},{1... | collective-permute-start | bytes 811016 | tf_op jit(solution)/shard_map/ppermute | solution.py:610
  35.9 1.5 %collective-permute-start.14 = (f32[2,33,8,128]{3,2,1,0:T(8,128)S(1)}, f32[2,33,8,128]{3,2,1,0:T(8,128)S(1)}, u32[]{:S(2)}, u32[]{:S(2)}) collective-permute-start(f32[2,33,8,128]{3,2,1,0:T(8,128)S(1)} %collective-permute-done.6.refs_7_), channel_id=1, source_target_pairs={{0,16},{16,0},{32,48},{48,32},{64,80},{80,64},{96,112},{112,96},{1... | collective-permute-start | bytes 811016 | tf_op jit(solution)/shard_map/ppermute | solution.py:610
  37.4 1.0 copy-start
  38.4 0.7 copy-start.1
  54.9 8.3 %collective-permute-start.17 = (f32[8,2,8,128]{3,2,1,0:T(8,128)S(1)}, f32[8,2,8,128]{3,2,1,0:T(8,128)S(1)}, u32[]{:S(2)}, u32[]{:S(2)}) collective-permute-start(f32[8,2,8,128]{3,2,1,0:T(8,128)S(1)} %get-tuple-element.30.refs_8_.refs_10_), channel_id=1, source_target_pairs={{1,2},{3,4},{5,6},{7,8},{9,10},{11,12},{13,14},{2,1},{4,3},{6,5},{... | collective-permute-start | bytes 196616 | tf_op jit(solution)/shard_map/ppermute | solution.py:587
  57.6 5.7 %collective-permute-start.16 = (f32[8,2,8,128]{3,2,1,0:T(8,128)S(1)}, f32[8,2,8,128]{3,2,1,0:T(8,128)S(1)}, u32[]{:S(2)}, u32[]{:S(2)}) collective-permute-start(f32[8,2,8,128]{3,2,1,0:T(8,128)S(1)} %get-tuple-element.30.refs_8_.refs_10_), channel_id=1, source_target_pairs={{0,1},{2,3},{4,5},{6,7},{8,9},{10,11},{12,13},{14,15},{1,0},{3,2},... | collective-permute-start | bytes 196616 | tf_op jit(solution)/shard_map/ppermute | solution.py:588
  87.6 7.9 %collective-permute-start.19 = (f32[4,2,8,128]{3,2,1,0:T(8,128)S(1)}, f32[4,2,8,128]{3,2,1,0:T(8,128)S(1)}, u32[]{:S(2)}, u32[]{:S(2)}) collective-permute-start(f32[4,2,8,128]{3,2,1,0:T(8,128)S(1)} %get-tuple-element.34.refs_7_), channel_id=1, source_target_pairs={{1,2},{3,4},{5,6},{7,8},{9,10},{11,12},{13,14},{2,1},{4,3},{6,5},{... | collective-permute-start | bytes 98312 | tf_op jit(solution)/shard_map/ppermute | solution.py:587
  91.8 4.0 %collective-permute-start.18 = (f32[4,2,8,128]{3,2,1,0:T(8,128)S(1)}, f32[4,2,8,128]{3,2,1,0:T(8,128)S(1)}, u32[]{:S(2)}, u32[]{:S(2)}) collective-permute-start(f32[4,2,8,128]{3,2,1,0:T(8,128)S(1)} %get-tuple-element.34.refs_7_), channel_id=1, source_target_pairs={{0,1},{2,3},{4,5},{6,7},{8,9},{10,11},{12,13},{14,15},{1,0},{3,2},... | collective-permute-start | bytes 98312 | tf_op jit(solution)/shard_map/ppermute | solution.py:588
